TPU v7x, 256 devices: a whole 4x4x8 slice. The times are simulated.
256 devices in a mesh: view: 2 (over x_hi), row: 4 (over x_lo, core), col: 32 (over y, z).
Axes of the slice: x: 4 (x_hi: 2, x_lo: 2; x = x_hi * 2 + x_lo), y: 4, z: 8, core: 2. Of those that a mesh axis runs over, the one named last changes fastest.
Arguments:
- image: float32 [2, 32, 32768], P('view', 'row', 'col'), may hold values from -6 to 6
- coarse: int32 [2, 32, 32768], P('view', 'row', 'col'), may hold values from 0 to 512, as said below
- bounds: int32 [2, 4, 32, 2], P('view', 'row', 'col'), may hold values from 0 to 512, as said below
Outputs:
- refinement: float32 [2, 32, 32768], P('view', 'row', 'col')
- dual: float32 [2, 2, 32, 32768], P('view', None, 'row', 'col')
Inputs may be any that keep to these rules, and one draw needn't show every extreme that they name: `bounds`: for each view and tile the lower bound is under the upper bound, the lower bound is at most 255 and the upper at least 256; some tile has upper bound 512 and some has lower bound 0. Every pixel's coarse disparity lies within its tile's bounds; both ends of the range are reached.
All inputs are finite; a program needn't handle non-finite values.
Results may differ from a plain program's by a relative error of at most 0.000088.
Values sent between devices are 32-bit elements; how exact they have to be, the bound alone decides.
No kernel may reach another device: no remote copies, remote signals or barrier semaphores. Data moves between devices by JAX's collectives and lax.ppermute only.
A program may use at most 64 MiB of HBM per device.

v0:
```python
import jax
import jax.numpy as jnp
from jax import lax
from jax.sharding import PartitionSpec as P

DMAX = 512
ITERS = 4


data_weight = 1.0
couple_weight = 0.5
tau_step = 0.25
sigma_step = 0.5
huber_eps = 0.05
edge_gain = 2.0
slope_floor = 0.05


def from_partner(block, axis, bit):
    count = lax.axis_size(axis)
    route = []
    for low in range(count):
        high = low | 1 << bit
        if high != low and high < count:
            route += [(low, high), (high, low)]
    return lax.ppermute(block, axis, route)


def extended(block, sides, width):
    for axis, dim in sides:
        count = lax.axis_size(axis)
        forward = [(i, i + 1) for i in range(count - 1)]
        backward = [(target, source) for source, target in forward]
        low = lax.ppermute(
            lax.slice_in_dim(block, block.shape[dim] - width, None, axis=dim), axis, forward
        )
        high = lax.ppermute(lax.slice_in_dim(block, 0, width, axis=dim), axis, backward)
        block = jnp.concatenate([low, block, high], axis=dim)
    return block


def far_panel(field):
    partner = from_partner(field, "view", 0)
    return extended(partner, (("col", 1),), DMAX + 1)


def flat_read(strip, flat_index):
    values = jnp.take(strip.reshape(-1), flat_index.reshape(-1), axis=0, mode="clip")
    return values.reshape(flat_index.shape)


def masked_slopes(center, right_cell, below_cell, row_global, col_global, total_rows, total_cols):
    usable = (row_global >= 0) & (col_global >= 0)
    grad_across = jnp.where(usable & (col_global < total_cols - 1), right_cell - center, 0.0)
    grad_down = jnp.where(usable & (row_global < total_rows - 1), below_cell - center, 0.0)
    return (grad_across, grad_down)


def framed_slopes(field, row_start, col_start, total_rows, total_cols):
    framed = extended(field, (("row", 0), ("col", 1)), 1)
    center = framed[:-1, :-1]
    row_global = row_start - 1 + lax.broadcasted_iota(jnp.int32, center.shape, 0)
    col_global = col_start - 1 + lax.broadcasted_iota(jnp.int32, center.shape, 1)
    return masked_slopes(
        center, framed[:-1, 1:], framed[1:, :-1], row_global, col_global, total_rows, total_cols
    )


def edge_weights(grad_across, grad_down):
    return 1.0 / (1.0 + edge_gain * (grad_across * grad_across + grad_down * grad_down))


def dual_update(dual_across, dual_down, grad_across, grad_down, edge_weight):
    trial_across = (dual_across + sigma_step * grad_across) / (1.0 + sigma_step * huber_eps)
    trial_down = (dual_down + sigma_step * grad_down) / (1.0 + sigma_step * huber_eps)
    shrink = jnp.sqrt(
        jnp.maximum(
            1.0,
            (trial_across * trial_across + trial_down * trial_down) / (edge_weight * edge_weight),
        )
    )
    return (trial_across / shrink, trial_down / shrink)


def on_device(image, coarse, bounds):
    picture = image[0]
    offset = coarse[0]
    tile_rows, tile_cols = picture.shape
    total_rows = tile_rows * lax.axis_size("row")
    total_cols = tile_cols * lax.axis_size("col")
    row_start = lax.axis_index("row") * tile_rows
    col_start = lax.axis_index("col") * tile_cols
    direction = 1 - 2 * lax.axis_index("view")
    direction_real = direction.astype(jnp.float32)
    pad_width = DMAX + 1
    col_local = lax.broadcasted_iota(jnp.int32, picture.shape, 1)
    row_local = lax.broadcasted_iota(jnp.int32, picture.shape, 0)
    target = col_start + col_local - direction * offset
    pick_col = col_local - direction * offset + pad_width
    inside = ((target >= 0) & (target < total_cols)).astype(jnp.float32)
    offset_real = offset.astype(jnp.float32)
    lower_bound = bounds[0, 0, 0, 0].astype(jnp.float32)
    upper_bound = bounds[0, 0, 0, 1].astype(jnp.float32)
    image_strip = far_panel(picture)
    strip_width = image_strip.shape[1]
    flat_center = row_local * strip_width + pick_col
    warped = flat_read(image_strip, flat_center)
    ahead_value = flat_read(image_strip, flat_center + 1)
    before = flat_read(image_strip, flat_center - 1)
    slope_data = -direction_real * (ahead_value - before) * 0.5
    residue = warped - picture
    couple = couple_weight * inside
    blend_denom = 1.0 + tau_step * couple
    clip_limit = data_weight * tau_step / blend_denom
    primal = offset_real
    relaxed = primal
    edge_weight = edge_weights(
        *framed_slopes(picture, row_start, col_start, total_rows, total_cols)
    )
    rim_shape = (tile_rows + 1, tile_cols + 1)
    dual_across = jnp.zeros(rim_shape, jnp.float32)
    dual_down = jnp.zeros(rim_shape, jnp.float32)
    for sweep in range(ITERS):
        grad_across, grad_down = framed_slopes(
            relaxed, row_start, col_start, total_rows, total_cols
        )
        dual_across, dual_down = dual_update(
            dual_across, dual_down, grad_across, grad_down, edge_weight
        )
        diverge = (
            dual_across[1:, 1:] - dual_across[1:, :-1] + dual_down[1:, 1:] - dual_down[:-1, 1:]
        )
        partner = flat_read(far_panel(primal), flat_center)
        blended = (primal + tau_step * diverge + tau_step * couple * partner) / blend_denom
        mismatch = residue + slope_data * (blended - offset_real)
        update_step = jnp.clip(
            mismatch / jnp.maximum(slope_data * slope_data, slope_floor), -clip_limit, clip_limit
        )
        refined = jnp.clip(blended - slope_data * update_step, lower_bound, upper_bound)
        relaxed = 2.0 * refined - primal
        primal = refined
    dual_out = jnp.stack([dual_across[1:, 1:], dual_down[1:, 1:]], axis=0)
    return ((primal - offset_real)[None], dual_out[None])


def solution(mesh):
    return jax.shard_map(
        on_device,
        mesh=mesh,
        in_specs=(P("view", "row", "col"), P("view", "row", "col"), P("view", "row", "col", None)),
        out_specs=(P("view", "row", "col"), P("view", None, "row", "col")),
        check_vma=False,
    )
```

profile of v0, /device:TPU:25, one launch (start us, length us, event | category | flops | bytes accessed | tf_op | source)
XLA Modules:
  0.0 455.7 jit_solution(6887580942060033089)
XLA Ops:
  0.6 0.8 fusion.83
  1.5 3.7 collective-permute-start
  5.2 1.9 collective-permute-start.1
  7.1 3.6 collective-permute-start.4
  10.8 1.9 collective-permute-start.5
  12.7 2.5 collective-permute-start.11
  18.9 3.5 collective-permute-start.3
  22.4 6.0 %collective-permute-start.2 = (f32[10,1]{1,0:T(8,128)S(1)}, f32[10,1]{1,0:T(8,128)S(1)}, u32[]{:S(2)}, u32[]{:S(2)}) collective-permute-start(f32[10,1]{1,0:T(8,128)S(1)} %get-tuple-element.31), channel_id=1, source_target_pairs={{1,0},{2,1},{3,2},{4,3},{5,4},{6,5},{7,6},{8,7},{9,8},{10,9},{11,1... | collective-permute-start | bytes 128 | tf_op jit(solution)/shard_map/ppermute | solution.py:37
  28.6 1.9 collective-permute-start.7
  30.5 5.5 %collective-permute-start.6 = (f32[10,1]{1,0:T(8,128)S(1)}, f32[10,1]{1,0:T(8,128)S(1)}, u32[]{:S(2)}, u32[]{:S(2)}) collective-permute-start(f32[10,1]{1,0:T(8,128)S(1)} %get-tuple-element.29), channel_id=1, source_target_pairs={{1,0},{2,1},{3,2},{4,3},{5,4},{6,5},{7,6},{8,7},{9,8},{10,9},{11,1... | collective-permute-start | bytes 128 | tf_op jit(solution)/shard_map/ppermute | solution.py:37
  37.2 1.9 collective-permute-start.12
  39.1 5.7 %collective-permute-start.13 = (f32[8,513]{1,0:T(8,128)S(1)}, f32[8,513]{1,0:T(8,128)S(1)}, u32[]{:S(2)}, u32[]{:S(2)}) collective-permute-start(f32[8,513]{1,0:T(8,128)S(1)} %get-tuple-element.54), channel_id=1, source_target_pairs={{1,0},{2,1},{3,2},{4,3},{5,4},{6,5},{7,6},{8,7},{9,8},{10,9},{11,1... | collective-permute-start | bytes 49256 | tf_op jit(solution)/shard_map/ppermute | solution.py:37
  44.9 3.4 collective-permute-start.10
  48.3 1.9 collective-permute-start.9
  50.4 45.5 %gather_fusion.1 = f32[8192]{0:T(1024)S(1)} fusion(f32[16400]{0:T(1024)S(1)} %reshape.141, s32[8192]{0:T(1024)S(1)} %broadcast_clamp_fusion.1), kind=kCustom, calls=%fused_computation.1 | custom fusion | bytes 98304 | tf_op jit(solution)/shard_map/jit(_take)/gather | solution.py:48
  96.0 45.5 %gather_fusion.2 = f32[8192]{0:T(1024)S(1)} fusion(f32[16400]{0:T(1024)S(1)} %reshape.141, s32[8192]{0:T(1024)S(1)} %broadcast_clamp_fusion), kind=kCustom, calls=%fused_computation.2 | custom fusion | bytes 98304 | tf_op jit(solution)/shard_map/jit(_take)/gather | solution.py:48
  141.8 45.5 %gather_fusion.3 = f32[8192]{0:T(1024)S(1)} fusion(f32[16400]{0:T(1024)S(1)} %reshape.141, s32[8192]{0:T(1024)S(1)} %broadcast_clamp_fusion.2), kind=kCustom, calls=%fused_computation.3 | custom fusion | bytes 98304 | tf_op jit(solution)/shard_map/jit(_take)/gather | solution.py:48
  187.3 45.5 %gather_fusion = f32[8192]{0:T(1024)S(1)} fusion(f32[16400]{0:T(1024)S(1)} %reshape.139, s32[8192]{0:T(1024)S(1)} %broadcast_clamp_fusion.2), kind=kCustom, calls=%fused_computation | custom fusion | bytes 98304 | tf_op jit(solution)/shard_map/jit(_take)/gather | solution.py:48
  232.9 0.7 copy-done
  233.8 6.7 %collective-permute-start.14 = (f32[1,1024]{1,0:T(1,128)S(1)}, f32[1,1024]{1,0:T(1,128)S(1)}, u32[]{:S(2)}, u32[]{:S(2)}) collective-permute-start(f32[1,1024]{1,0:T(1,128)S(1)} %get-tuple-element.41), channel_id=1, source_target_pairs={{0,32},{32,64},{64,96},{1,33},{33,65},{65,97},{2,34},{34,66},{66,9... | collective-permute-start | bytes 12296 | tf_op jit(solution)/shard_map/ppermute | solution.py:34
  240.5 1.9 collective-permute-start.15
  242.4 2.5 collective-permute-start.18
  245.5 1.9 collective-permute-start.17
  247.4 5.8 %collective-permute-start.16 = (f32[10,1]{1,0:T(8,128)S(1)}, f32[10,1]{1,0:T(8,128)S(1)}, u32[]{:S(2)}, u32[]{:S(2)}) collective-permute-start(f32[10,1]{1,0:T(8,128)S(1)} %get-tuple-element.27), channel_id=1, source_target_pairs={{1,0},{2,1},{3,2},{4,3},{5,4},{6,5},{7,6},{8,7},{9,8},{10,9},{11,1... | collective-permute-start | bytes 128 | tf_op jit(solution)/shard_map/ppermute | solution.py:37
  254.2 1.9 collective-permute-start.19
  256.1 5.7 %collective-permute-start.20 = (f32[8,513]{1,0:T(8,128)S(1)}, f32[8,513]{1,0:T(8,128)S(1)}, u32[]{:S(2)}, u32[]{:S(2)}) collective-permute-start(f32[8,513]{1,0:T(8,128)S(1)} %get-tuple-element.43), channel_id=1, source_target_pairs={{1,0},{2,1},{3,2},{4,3},{5,4},{6,5},{7,6},{8,7},{9,8},{10,9},{11,1... | collective-permute-start | bytes 49256 | tf_op jit(solution)/shard_map/ppermute | solution.py:37
  262.0 0.7 collective-permute-done.20
  262.9 45.5 %gather_fusion.4 = f32[8192]{0:T(1024)S(1)} fusion(f32[16400]{0:T(1024)S(1)} %reshape.143, s32[8192]{0:T(1024)S(1)} %broadcast_clamp_fusion.2), kind=kCustom, calls=%fused_computation.4 | custom fusion | bytes 98304 | tf_op jit(solution)/shard_map/jit(_take)/gather | solution.py:48
  308.6 4.9 %collective-permute-start.21 = (f32[1,1024]{1,0:T(1,128)S(1)}, f32[1,1024]{1,0:T(1,128)S(1)}, u32[]{:S(2)}, u32[]{:S(2)}) collective-permute-start(f32[1,1024]{1,0:T(1,128)S(1)} %get-tuple-element.37), channel_id=1, source_target_pairs={{0,32},{32,64},{64,96},{1,33},{33,65},{65,97},{2,34},{34,66},{66,9... | collective-permute-start | bytes 12296 | tf_op jit(solution)/shard_map/ppermute | solution.py:34
  313.5 1.9 collective-permute-start.22
  315.4 1.8 collective-permute-start.25
  317.3 1.2 collective-permute-done.22
  318.5 1.9 collective-permute-start.24
  320.4 6.0 %collective-permute-start.23 = (f32[10,1]{1,0:T(8,128)S(1)}, f32[10,1]{1,0:T(8,128)S(1)}, u32[]{:S(2)}, u32[]{:S(2)}) collective-permute-start(f32[10,1]{1,0:T(8,128)S(1)} %get-tuple-element.25), channel_id=1, source_target_pairs={{1,0},{2,1},{3,2},{4,3},{5,4},{6,5},{7,6},{8,7},{9,8},{10,9},{11,1... | collective-permute-start | bytes 128 | tf_op jit(solution)/shard_map/ppermute | solution.py:37
  327.5 1.9 collective-permute-start.26
  329.4 5.7 %collective-permute-start.27 = (f32[8,513]{1,0:T(8,128)S(1)}, f32[8,513]{1,0:T(8,128)S(1)}, u32[]{:S(2)}, u32[]{:S(2)}) collective-permute-start(f32[8,513]{1,0:T(8,128)S(1)} %get-tuple-element.39), channel_id=1, source_target_pairs={{1,0},{2,1},{3,2},{4,3},{5,4},{6,5},{7,6},{8,7},{9,8},{10,9},{11,1... | collective-permute-start | bytes 49256 | tf_op jit(solution)/shard_map/ppermute | solution.py:37
  335.3 0.7 collective-permute-done.27
  336.2 45.5 %gather_fusion.5 = f32[8192]{0:T(1024)S(1)} fusion(f32[16400]{0:T(1024)S(1)} %reshape.145, s32[8192]{0:T(1024)S(1)} %broadcast_clamp_fusion.2), kind=kCustom, calls=%fused_computation.5 | custom fusion | bytes 98304 | tf_op jit(solution)/shard_map/jit(_take)/gather | solution.py:48
  381.9 4.1 collective-permute-start.28
  386.1 1.9 collective-permute-start.29
  388.0 2.5 collective-permute-start.32
  391.1 1.9 collective-permute-start.31
  393.0 6.0 %collective-permute-start.30 = (f32[10,1]{1,0:T(8,128)S(1)}, f32[10,1]{1,0:T(8,128)S(1)}, u32[]{:S(2)}, u32[]{:S(2)}) collective-permute-start(f32[10,1]{1,0:T(8,128)S(1)} %get-tuple-element.23), channel_id=1, source_target_pairs={{1,0},{2,1},{3,2},{4,3},{5,4},{6,5},{7,6},{8,7},{9,8},{10,9},{11,1... | collective-permute-start | bytes 128 | tf_op jit(solution)/shard_map/ppermute | solution.py:37
  400.1 1.9 collective-permute-start.33
  402.0 5.7 %collective-permute-start.34 = (f32[8,513]{1,0:T(8,128)S(1)}, f32[8,513]{1,0:T(8,128)S(1)}, u32[]{:S(2)}, u32[]{:S(2)}) collective-permute-start(f32[8,513]{1,0:T(8,128)S(1)} %get-tuple-element.33), channel_id=1, source_target_pairs={{1,0},{2,1},{3,2},{4,3},{5,4},{6,5},{7,6},{8,7},{9,8},{10,9},{11,1... | collective-permute-start | bytes 49256 | tf_op jit(solution)/shard_map/ppermute | solution.py:37
  407.9 0.7 collective-permute-done.34
  408.8 45.5 %gather_fusion.6 = f32[8192]{0:T(1024)S(1)} fusion(f32[16400]{0:T(1024)S(1)} %reshape.147, s32[8192]{0:T(1024)S(1)} %broadcast_clamp_fusion.2), kind=kCustom, calls=%fused_computation.6 | custom fusion | bytes 98304 | tf_op jit(solution)/shard_map/jit(_take)/gather | solution.py:48
  454.4 0.7 slice_bitcast_fusion.1
  (101 shorter events, 10.1 us)
Async XLA Ops:
  0.6 6.5 %copy-start.1 = (f32[1,8,1024]{2,1,0:T(8,128)S(1)}, f32[1,8,1024]{2,1,0:T(8,128)}, u32[]{:S(2)}) copy-start(f32[1,8,1024]{2,1,0:T(8,128)} %param.3) | copy-start | bytes 98308
  1.5 16.7 %collective-permute-start = (f32[1,1024]{1,0:T(1,128)S(1)}, f32[1,1024]{1,0:T(1,128)S(1)}, u32[]{:S(2)}, u32[]{:S(2)}) collective-permute-start(f32[1,1024]{1,0:T(1,128)S(1)} %get-tuple-element.47), channel_id=1, source_target_pairs={{0,32},{32,64},{64,96},{1,33},{33,65},{65,97},{2,34},{34,66},{66,9... | collective-permute-start | bytes 12296 | tf_op jit(solution)/shard_map/ppermute | solution.py:34
  5.2 13.6 %collective-permute-start.1 = (f32[1,1024]{1,0:T(1,128)S(1)}, f32[1,1024]{1,0:T(1,128)S(1)}, u32[]{:S(2)}, u32[]{:S(2)}) collective-permute-start(f32[1,1024]{1,0:T(1,128)S(1)} %get-tuple-element.48), channel_id=1, source_target_pairs={{32,0},{64,32},{96,64},{33,1},{65,33},{97,65},{34,2},{66,34},{98,6... | collective-permute-start | bytes 12296 | tf_op jit(solution)/shard_map/ppermute | solution.py:37
  7.1 15.3 %collective-permute-start.4 = (f32[1,1024]{1,0:T(1,128)S(1)}, f32[1,1024]{1,0:T(1,128)S(1)}, u32[]{:S(2)}, u32[]{:S(2)}) collective-permute-start(f32[1,1024]{1,0:T(1,128)S(1)} %get-tuple-element.45), channel_id=1, source_target_pairs={{0,32},{32,64},{64,96},{1,33},{33,65},{65,97},{2,34},{34,66},{66,9... | collective-permute-start | bytes 12296 | tf_op jit(solution)/shard_map/ppermute | solution.py:34
  10.8 17.7 %collective-permute-start.5 = (f32[1,1024]{1,0:T(1,128)S(1)}, f32[1,1024]{1,0:T(1,128)S(1)}, u32[]{:S(2)}, u32[]{:S(2)}) collective-permute-start(f32[1,1024]{1,0:T(1,128)S(1)} %get-tuple-element.46), channel_id=1, source_target_pairs={{32,0},{64,32},{96,64},{33,1},{65,33},{97,65},{34,2},{66,34},{98,6... | collective-permute-start | bytes 12296 | tf_op jit(solution)/shard_map/ppermute | solution.py:37
  12.7 24.4 %collective-permute-start.11 = (f32[8,1024]{1,0:T(8,128)S(1)}, f32[8,1024]{1,0:T(8,128)S(1)}, u32[]{:S(2)}, u32[]{:S(2)}) collective-permute-start(f32[8,1024]{1,0:T(8,128)S(1)} %bitcast.53), channel_id=1, source_target_pairs={{0,128},{128,0},{1,129},{129,1},{2,130},{130,2},{3,131},{131,3},{4... | collective-permute-start | bytes 98312 | tf_op jit(solution)/shard_map/ppermute | solution.py:26
  15.6 0.7 copy-start.2
  18.2 26.6 %collective-permute-start.8 = (f32[8,1024]{1,0:T(8,128)S(1)}, f32[8,1024]{1,0:T(8,128)S(1)}, u32[]{:S(2)}, u32[]{:S(2)}) collective-permute-start(f32[8,1024]{1,0:T(8,128)S(1)} %get-tuple-element.50), channel_id=1, source_target_pairs={{0,128},{128,0},{1,129},{129,1},{2,130},{130,2},{3,131},{131,3},{4... | collective-permute-start | bytes 98312 | tf_op jit(solution)/shard_map/ppermute | solution.py:26
  18.9 11.6 %collective-permute-start.3 = (f32[10,1]{1,0:T(8,128)S(1)}, f32[10,1]{1,0:T(8,128)S(1)}, u32[]{:S(2)}, u32[]{:S(2)}) collective-permute-start(f32[10,1]{1,0:T(8,128)S(1)} %get-tuple-element.32), channel_id=1, source_target_pairs={{0,1},{1,2},{2,3},{3,4},{4,5},{5,6},{6,7},{7,8},{8,9},{9,10},{10,1... | collective-permute-start | bytes 128 | tf_op jit(solution)/shard_map/ppermute | solution.py:34
  22.4 13.8 %collective-permute-start.2 = (f32[10,1]{1,0:T(8,128)S(1)}, f32[10,1]{1,0:T(8,128)S(1)}, u32[]{:S(2)}, u32[]{:S(2)}) collective-permute-start(f32[10,1]{1,0:T(8,128)S(1)} %get-tuple-element.31), channel_id=1, source_target_pairs={{1,0},{2,1},{3,2},{4,3},{5,4},{6,5},{7,6},{8,7},{9,8},{10,9},{11,1... | collective-permute-start | bytes 128 | tf_op jit(solution)/shard_map/ppermute | solution.py:37
  28.6 7.5 %collective-permute-start.7 = (f32[10,1]{1,0:T(8,128)S(1)}, f32[10,1]{1,0:T(8,128)S(1)}, u32[]{:S(2)}, u32[]{:S(2)}) collective-permute-start(f32[10,1]{1,0:T(8,128)S(1)} %get-tuple-element.30), channel_id=1, source_target_pairs={{0,1},{1,2},{2,3},{3,4},{4,5},{5,6},{6,7},{7,8},{8,9},{9,10},{10,1... | collective-permute-start | bytes 128 | tf_op jit(solution)/shard_map/ppermute | solution.py:34
  30.5 6.3 %collective-permute-start.6 = (f32[10,1]{1,0:T(8,128)S(1)}, f32[10,1]{1,0:T(8,128)S(1)}, u32[]{:S(2)}, u32[]{:S(2)}) collective-permute-start(f32[10,1]{1,0:T(8,128)S(1)} %get-tuple-element.29), channel_id=1, source_target_pairs={{1,0},{2,1},{3,2},{4,3},{5,4},{6,5},{7,6},{8,7},{9,8},{10,9},{11,1... | collective-permute-start | bytes 128 | tf_op jit(solution)/shard_map/ppermute | solution.py:37
  37.2 13.1 %collective-permute-start.12 = (f32[8,513]{1,0:T(8,128)S(1)}, f32[8,513]{1,0:T(8,128)S(1)}, u32[]{:S(2)}, u32[]{:S(2)}) collective-permute-start(f32[8,513]{1,0:T(8,128)S(1)} %get-tuple-element.55), channel_id=1, source_target_pairs={{0,1},{1,2},{2,3},{3,4},{4,5},{5,6},{6,7},{7,8},{8,9},{9,10},{10,1... | collective-permute-start | bytes 49256 | tf_op jit(solution)/shard_map/ppermute | solution.py:34
  39.1 11.1 %collective-permute-start.13 = (f32[8,513]{1,0:T(8,128)S(1)}, f32[8,513]{1,0:T(8,128)S(1)}, u32[]{:S(2)}, u32[]{:S(2)}) collective-permute-start(f32[8,513]{1,0:T(8,128)S(1)} %get-tuple-element.54), channel_id=1, source_target_pairs={{1,0},{2,1},{3,2},{4,3},{5,4},{6,5},{7,6},{8,7},{9,8},{10,9},{11,1... | collective-permute-start | bytes 49256 | tf_op jit(solution)/shard_map/ppermute | solution.py:37
  44.9 96.6 %collective-permute-start.10 = (f32[8,513]{1,0:T(8,128)S(1)}, f32[8,513]{1,0:T(8,128)S(1)}, u32[]{:S(2)}, u32[]{:S(2)}) collective-permute-start(f32[8,513]{1,0:T(8,128)S(1)} %get-tuple-element.52), channel_id=1, source_target_pairs={{1,0},{2,1},{3,2},{4,3},{5,4},{6,5},{7,6},{8,7},{9,8},{10,9},{11,1... | collective-permute-start | bytes 49256 | tf_op jit(solution)/shard_map/ppermute | solution.py:37
  48.3 93.3 %collective-permute-start.9 = (f32[8,513]{1,0:T(8,128)S(1)}, f32[8,513]{1,0:T(8,128)S(1)}, u32[]{:S(2)}, u32[]{:S(2)}) collective-permute-start(f32[8,513]{1,0:T(8,128)S(1)} %get-tuple-element.53), channel_id=1, source_target_pairs={{0,1},{1,2},{2,3},{3,4},{4,5},{5,6},{6,7},{7,8},{8,9},{9,10},{10,1... | collective-permute-start | bytes 49256 | tf_op jit(solution)/shard_map/ppermute | solution.py:34
  232.9 0.8 copy-start
  233.8 11.2 %collective-permute-start.14 = (f32[1,1024]{1,0:T(1,128)S(1)}, f32[1,1024]{1,0:T(1,128)S(1)}, u32[]{:S(2)}, u32[]{:S(2)}) collective-permute-start(f32[1,1024]{1,0:T(1,128)S(1)} %get-tuple-element.41), channel_id=1, source_target_pairs={{0,32},{32,64},{64,96},{1,33},{33,65},{65,97},{2,34},{34,66},{66,9... | collective-permute-start | bytes 12296 | tf_op jit(solution)/shard_map/ppermute | solution.py:34
  240.5 4.9 %collective-permute-start.15 = (f32[1,1024]{1,0:T(1,128)S(1)}, f32[1,1024]{1,0:T(1,128)S(1)}, u32[]{:S(2)}, u32[]{:S(2)}) collective-permute-start(f32[1,1024]{1,0:T(1,128)S(1)} %get-tuple-element.42), channel_id=1, source_target_pairs={{32,0},{64,32},{96,64},{33,1},{65,33},{97,65},{34,2},{66,34},{98,6... | collective-permute-start | bytes 12296 | tf_op jit(solution)/shard_map/ppermute | solution.py:37
  242.4 11.7 %collective-permute-start.18 = (f32[8,1024]{1,0:T(8,128)S(1)}, f32[8,1024]{1,0:T(8,128)S(1)}, u32[]{:S(2)}, u32[]{:S(2)}) collective-permute-start(f32[8,1024]{1,0:T(8,128)S(1)} %get-tuple-element.13), channel_id=1, source_target_pairs={{0,128},{128,0},{1,129},{129,1},{2,130},{130,2},{3,131},{131,3},{4... | collective-permute-start | bytes 98312 | tf_op jit(solution)/shard_map/ppermute | solution.py:26
  245.5 7.7 %collective-permute-start.17 = (f32[10,1]{1,0:T(8,128)S(1)}, f32[10,1]{1,0:T(8,128)S(1)}, u32[]{:S(2)}, u32[]{:S(2)}) collective-permute-start(f32[10,1]{1,0:T(8,128)S(1)} %get-tuple-element.28), channel_id=1, source_target_pairs={{0,1},{1,2},{2,3},{3,4},{4,5},{5,6},{6,7},{7,8},{8,9},{9,10},{10,1... | collective-permute-start | bytes 128 | tf_op jit(solution)/shard_map/ppermute | solution.py:34
  247.4 6.5 %collective-permute-start.16 = (f32[10,1]{1,0:T(8,128)S(1)}, f32[10,1]{1,0:T(8,128)S(1)}, u32[]{:S(2)}, u32[]{:S(2)}) collective-permute-start(f32[10,1]{1,0:T(8,128)S(1)} %get-tuple-element.27), channel_id=1, source_target_pairs={{1,0},{2,1},{3,2},{4,3},{5,4},{6,5},{7,6},{8,7},{9,8},{10,9},{11,1... | collective-permute-start | bytes 128 | tf_op jit(solution)/shard_map/ppermute | solution.py:37
  254.2 7.8 %collective-permute-start.19 = (f32[8,513]{1,0:T(8,128)S(1)}, f32[8,513]{1,0:T(8,128)S(1)}, u32[]{:S(2)}, u32[]{:S(2)}) collective-permute-start(f32[8,513]{1,0:T(8,128)S(1)} %get-tuple-element.44), channel_id=1, source_target_pairs={{0,1},{1,2},{2,3},{3,4},{4,5},{5,6},{6,7},{7,8},{8,9},{9,10},{10,1... | collective-permute-start | bytes 49256 | tf_op jit(solution)/shard_map/ppermute | solution.py:34
  256.1 6.6 %collective-permute-start.20 = (f32[8,513]{1,0:T(8,128)S(1)}, f32[8,513]{1,0:T(8,128)S(1)}, u32[]{:S(2)}, u32[]{:S(2)}) collective-permute-start(f32[8,513]{1,0:T(8,128)S(1)} %get-tuple-element.43), channel_id=1, source_target_pairs={{1,0},{2,1},{3,2},{4,3},{5,4},{6,5},{7,6},{8,7},{9,8},{10,9},{11,1... | collective-permute-start | bytes 49256 | tf_op jit(solution)/shard_map/ppermute | solution.py:37
  308.6 8.6 %collective-permute-start.21 = (f32[1,1024]{1,0:T(1,128)S(1)}, f32[1,1024]{1,0:T(1,128)S(1)}, u32[]{:S(2)}, u32[]{:S(2)}) collective-permute-start(f32[1,1024]{1,0:T(1,128)S(1)} %get-tuple-element.37), channel_id=1, source_target_pairs={{0,32},{32,64},{64,96},{1,33},{33,65},{65,97},{2,34},{34,66},{66,9... | collective-permute-start | bytes 12296 | tf_op jit(solution)/shard_map/ppermute | solution.py:34
  313.5 4.9 %collective-permute-start.22 = (f32[1,1024]{1,0:T(1,128)S(1)}, f32[1,1024]{1,0:T(1,128)S(1)}, u32[]{:S(2)}, u32[]{:S(2)}) collective-permute-start(f32[1,1024]{1,0:T(1,128)S(1)} %get-tuple-element.38), channel_id=1, source_target_pairs={{32,0},{64,32},{96,64},{33,1},{65,33},{97,65},{34,2},{66,34},{98,6... | collective-permute-start | bytes 12296 | tf_op jit(solution)/shard_map/ppermute | solution.py:37
  315.4 12.0 %collective-permute-start.25 = (f32[8,1024]{1,0:T(8,128)S(1)}, f32[8,1024]{1,0:T(8,128)S(1)}, u32[]{:S(2)}, u32[]{:S(2)}) collective-permute-start(f32[8,1024]{1,0:T(8,128)S(1)} %get-tuple-element.9), channel_id=1, source_target_pairs={{0,128},{128,0},{1,129},{129,1},{2,130},{130,2},{3,131},{131,3},{4... | collective-permute-start | bytes 98312 | tf_op jit(solution)/shard_map/ppermute | solution.py:26
  318.5 8.0 %collective-permute-start.24 = (f32[10,1]{1,0:T(8,128)S(1)}, f32[10,1]{1,0:T(8,128)S(1)}, u32[]{:S(2)}, u32[]{:S(2)}) collective-permute-start(f32[10,1]{1,0:T(8,128)S(1)} %get-tuple-element.26), channel_id=1, source_target_pairs={{0,1},{1,2},{2,3},{3,4},{4,5},{5,6},{6,7},{7,8},{8,9},{9,10},{10,1... | collective-permute-start | bytes 128 | tf_op jit(solution)/shard_map/ppermute | solution.py:34
  320.4 6.8 %collective-permute-start.23 = (f32[10,1]{1,0:T(8,128)S(1)}, f32[10,1]{1,0:T(8,128)S(1)}, u32[]{:S(2)}, u32[]{:S(2)}) collective-permute-start(f32[10,1]{1,0:T(8,128)S(1)} %get-tuple-element.25), channel_id=1, source_target_pairs={{1,0},{2,1},{3,2},{4,3},{5,4},{6,5},{7,6},{8,7},{9,8},{10,9},{11,1... | collective-permute-start | bytes 128 | tf_op jit(solution)/shard_map/ppermute | solution.py:37
  327.5 7.8 %collective-permute-start.26 = (f32[8,513]{1,0:T(8,128)S(1)}, f32[8,513]{1,0:T(8,128)S(1)}, u32[]{:S(2)}, u32[]{:S(2)}) collective-permute-start(f32[8,513]{1,0:T(8,128)S(1)} %get-tuple-element.40), channel_id=1, source_target_pairs={{0,1},{1,2},{2,3},{3,4},{4,5},{5,6},{6,7},{7,8},{8,9},{9,10},{10,1... | collective-permute-start | bytes 49256 | tf_op jit(solution)/shard_map/ppermute | solution.py:34
  329.4 6.6 %collective-permute-start.27 = (f32[8,513]{1,0:T(8,128)S(1)}, f32[8,513]{1,0:T(8,128)S(1)}, u32[]{:S(2)}, u32[]{:S(2)}) collective-permute-start(f32[8,513]{1,0:T(8,128)S(1)} %get-tuple-element.39), channel_id=1, source_target_pairs={{1,0},{2,1},{3,2},{4,3},{5,4},{6,5},{7,6},{8,7},{9,8},{10,9},{11,1... | collective-permute-start | bytes 49256 | tf_op jit(solution)/shard_map/ppermute | solution.py:37
  381.9 8.6 %collective-permute-start.28 = (f32[1,1024]{1,0:T(1,128)S(1)}, f32[1,1024]{1,0:T(1,128)S(1)}, u32[]{:S(2)}, u32[]{:S(2)}) collective-permute-start(f32[1,1024]{1,0:T(1,128)S(1)} %get-tuple-element.35), channel_id=1, source_target_pairs={{0,32},{32,64},{64,96},{1,33},{33,65},{65,97},{2,34},{34,66},{66,9... | collective-permute-start | bytes 12296 | tf_op jit(solution)/shard_map/ppermute | solution.py:34
  386.1 4.9 %collective-permute-start.29 = (f32[1,1024]{1,0:T(1,128)S(1)}, f32[1,1024]{1,0:T(1,128)S(1)}, u32[]{:S(2)}, u32[]{:S(2)}) collective-permute-start(f32[1,1024]{1,0:T(1,128)S(1)} %get-tuple-element.36), channel_id=1, source_target_pairs={{32,0},{64,32},{96,64},{33,1},{65,33},{97,65},{34,2},{66,34},{98,6... | collective-permute-start | bytes 12296 | tf_op jit(solution)/shard_map/ppermute | solution.py:37
  388.0 12.0 %collective-permute-start.32 = (f32[8,1024]{1,0:T(8,128)S(1)}, f32[8,1024]{1,0:T(8,128)S(1)}, u32[]{:S(2)}, u32[]{:S(2)}) collective-permute-start(f32[8,1024]{1,0:T(8,128)S(1)} %get-tuple-element.5), channel_id=1, source_target_pairs={{0,128},{128,0},{1,129},{129,1},{2,130},{130,2},{3,131},{131,3},{4... | collective-permute-start | bytes 98312 | tf_op jit(solution)/shard_map/ppermute | solution.py:26
  391.1 8.0 %collective-permute-start.31 = (f32[10,1]{1,0:T(8,128)S(1)}, f32[10,1]{1,0:T(8,128)S(1)}, u32[]{:S(2)}, u32[]{:S(2)}) collective-permute-start(f32[10,1]{1,0:T(8,128)S(1)} %get-tuple-element.24), channel_id=1, source_target_pairs={{0,1},{1,2},{2,3},{3,4},{4,5},{5,6},{6,7},{7,8},{8,9},{9,10},{10,1... | collective-permute-start | bytes 128 | tf_op jit(solution)/shard_map/ppermute | solution.py:34
  393.0 6.8 %collective-permute-start.30 = (f32[10,1]{1,0:T(8,128)S(1)}, f32[10,1]{1,0:T(8,128)S(1)}, u32[]{:S(2)}, u32[]{:S(2)}) collective-permute-start(f32[10,1]{1,0:T(8,128)S(1)} %get-tuple-element.23), channel_id=1, source_target_pairs={{1,0},{2,1},{3,2},{4,3},{5,4},{6,5},{7,6},{8,7},{9,8},{10,9},{11,1... | collective-permute-start | bytes 128 | tf_op jit(solution)/shard_map/ppermute | solution.py:37
  400.1 7.8 %collective-permute-start.33 = (f32[8,513]{1,0:T(8,128)S(1)}, f32[8,513]{1,0:T(8,128)S(1)}, u32[]{:S(2)}, u32[]{:S(2)}) collective-permute-start(f32[8,513]{1,0:T(8,128)S(1)} %get-tuple-element.34), channel_id=1, source_target_pairs={{0,1},{1,2},{2,3},{3,4},{4,5},{5,6},{6,7},{7,8},{8,9},{9,10},{10,1... | collective-permute-start | bytes 49256 | tf_op jit(solution)/shard_map/ppermute | solution.py:34
  402.0 6.6 %collective-permute-start.34 = (f32[8,513]{1,0:T(8,128)S(1)}, f32[8,513]{1,0:T(8,128)S(1)}, u32[]{:S(2)}, u32[]{:S(2)}) collective-permute-start(f32[8,513]{1,0:T(8,128)S(1)} %get-tuple-element.33), channel_id=1, source_target_pairs={{1,0},{2,1},{3,2},{4,3},{5,4},{6,5},{7,6},{8,7},{9,8},{10,9},{11,1... | collective-permute-start | bytes 49256 | tf_op jit(solution)/shard_map/ppermute | solution.py:37
where the time goes:
time: 458 us; the launch traced here: 456 us
  local copies, waits for them, and re-layouts  322 us (70%)
  starting transfers between devices  119 us (26%)
  waiting for transfers between devices  6.85 us (1%)
  other arithmetic  4.8 us (1%)
    gather x7, local copies, waits for them, and re-layouts, flat_read(): jnp.take(strip.reshape(-1), flat_index.reshape(-1), axis=0, mode='clip')  319 us
    ppermute x15, starting transfers between devices, extended(): lax.ppermute(lax.slice_in_dim(block, 0, width, axis=dim), axis, backward)  65.2 us
    ppermute x15, starting transfers between devices, extended(): lax.ppermute(lax.slice_in_dim(block, block.shape[dim] - width, None, axis...  43.8 us
    ppermute x5, starting transfers between devices, from_partner(): return lax.ppermute(block, axis, route)  10 us
  transfers between devices with their start and end apart: 35, of which 10 were waited for; matrix products, arithmetic and copies ran while one was open for 21% of the time, Pallas kernels for 0%

commit v1 on v0

v1 whole, which is shorter than its diff:
```python
import jax
import jax.numpy as jnp
from jax import lax
from jax.experimental import pallas as pl
from jax.experimental.pallas import tpu as pltpu
from jax.sharding import PartitionSpec as P

AXES = ("view", "row", "col")
LANES = 128
OUT_ROWS = 8
BLOCKS = 8
TILE_PACK = 17
STRIP = 32
SHIFT = 10
WIDE = 40
TALL = 16
VMEM_BYTES = 40 * 1024 * 1024

tau = 0.25
sigma = 0.5
huber_eps = 0.05
edge_gain = 2.0
slope_floor = 0.05
couple_weight = 0.5
data_weight = 1.0


def swapped(block, partner, sizes):
    views, rows, cols = sizes
    route = []
    for v in range(views):
        for r in range(rows):
            for c in range(cols):
                to_v, to_r, to_c = partner(v, r, c)
                if 0 <= to_r < rows and 0 <= to_c < cols:
                    route.append(((v * rows + r) * cols + c, (to_v * rows + to_r) * cols + to_c))
    return lax.ppermute(block, AXES, route)


def to_slabs(tile):
    parts = jnp.stack([tile[:, LANES * j : LANES * (j + 1)] for j in range(BLOCKS)])
    return jnp.transpose(parts, (1, 0, 2))


def pack_kernel(image_ref, coarse_ref, bounds_ref, out_ref):
    out_ref[0:8] = to_slabs(image_ref[0])
    out_ref[8:16] = to_slabs(coarse_ref[0].astype(jnp.float32))
    sub = lax.broadcasted_iota(jnp.int32, (BLOCKS, LANES), 0)
    out_ref[16] = jnp.where(sub == 0, bounds_ref[0, 0], bounds_ref[0, 1]).astype(jnp.float32)


def join_kernel(own_ref, other_ref, both_ref, first_ref, second_ref):
    lower = ((lax.axis_index("col") >> 1) & 1) == 0
    both_ref[0:TILE_PACK] = own_ref[...]
    both_ref[TILE_PACK : 2 * TILE_PACK] = other_ref[...]
    for w, ref in enumerate((own_ref, other_ref)):
        for i in range(16):
            head, tail = ref[i, 0:1, :], ref[i, 7:8, :]
            at = w * 16 + i
            first_ref[at : at + 1, :] = jnp.where(lower, tail, head)
            second_ref[at : at + 1, :] = jnp.where(lower, head, tail)


def assemble_kernel(both_ref, a_ref, b_ref, thin1_ref, thin2_ref, m1_ref, m2_ref):
    col, row = lax.axis_index("col"), lax.axis_index("row")
    odd = (col & 1) == 1
    upper = ((col >> 1) & 1) == 1
    even_row = (row & 1) == 0
    thin_left = jnp.where(upper, thin1_ref[...], thin2_ref[...])
    thin_right = jnp.where(upper, thin2_ref[...], thin1_ref[...])

    def put(plane, y, at, top, bottom):
        n = top.shape[0]
        m1_ref[plane, y, at : at + n, :] = jnp.where(even_row, bottom, top)
        m2_ref[plane, y, at : at + n, :] = jnp.where(even_row, top, bottom)

    for plane in range(4):
        w, kind = plane // 2, plane % 2
        base = w * TILE_PACK + kind * 8
        for y in range(4):
            t, b = base + y, base + y + 4
            at, ab = plane * 8 + y, plane * 8 + y + 4
            put(plane, y, 0, thin_left[at : at + 1], thin_left[ab : ab + 1])
            put(plane, y, 1, jnp.where(odd, a_ref[t], b_ref[t]), jnp.where(odd, a_ref[b], b_ref[b]))
            put(plane, y, 9, both_ref[t], both_ref[b])
            put(plane, y, 17, jnp.where(odd, b_ref[t], a_ref[t]), jnp.where(odd, b_ref[b], a_ref[b]))
            put(plane, y, 25, thin_right[at : at + 1], thin_right[ab : ab + 1])
            if kind == 0 and y == 0:
                s = w * TILE_PACK + 16
                left = jnp.where(odd, a_ref[s, 0:2], b_ref[s, 0:2])
                right = jnp.where(odd, b_ref[s, 0:2], a_ref[s, 0:2])
                put(plane, y, 26, left, left)
                put(plane, y, 28, both_ref[s, 0:2], both_ref[s, 0:2])
                put(plane, y, 30, right, right)
            else:
                zero = jnp.zeros((6, LANES), jnp.float32)
                put(plane, y, 26, zero, zero)


def plans(view):
    if view == 0:
        other = (((-9, -1, 4), (-8, 0, 4)), ((-5, 1), (-5, 1)), ((-5, 0), (-4, 0)), None)
        slopes = ((-8, 0, 8), (-9, -1, 5))
    else:
        other = (((-5, 3, 8), (-4, 4, 8)), ((-1, 5), (-1, 5)), ((-1, 4), (0, 4)), None)
        slopes = ((-8, 0, 8), (-5, 3, 9))
    own = (((-5, 3, 5), (-5, 3, 5)), ((-5, 3, 4), (-4, 4)), ((-1, 1), (-1, 1)), ((-1, 0), (0,)))
    return own, other, slopes


def refine_kernel(sizes, m1_ref, m2_ref, g1_ref, g2_ref, refine_ref, dual_ref, *scratch):
    (F, G, D, RES, SL, INV, RD, IE, LO, HI, UA, UB, RA, RB, XA, XB, YA, YB, MX, CV, XG, OUT) = scratch
    _, n_row, n_col = sizes
    view, row, col = lax.axis_index("view"), lax.axis_index("row"), lax.axis_index("col")
    even_row = (row & 1) == 0
    lane = lax.broadcasted_iota(jnp.int32, (8, LANES), 1)
    sub = lax.broadcasted_iota(jnp.int32, (8, LANES), 0)
    total = n_col * BLOCKS * LANES

    for plane in range(4):
        for y in range(4):
            for at in (0, 8, 16, 24):
                n = 2 if at == 24 else 8
                m1, m2 = m1_ref[plane, y, at : at + n], m2_ref[plane, y, at : at + n]
                g1, g2 = g1_ref[plane, y, at : at + n], g2_ref[plane, y, at : at + n]
                to = slice(at + 1, at + 1 + n)
                F[plane, y, to] = jnp.where(even_row, g2, g1)
                F[plane, y + 4, to] = jnp.where(even_row, m2, m1)
                F[plane, y + 8, to] = jnp.where(even_row, m1, m2)
                F[plane, y + 12, to] = jnp.where(even_row, g1, g2)
        for y in range(TALL):
            F[plane, y, 0:1] = jnp.zeros((1, LANES), jnp.float32)
            F[plane, y, 27:40] = jnp.zeros((13, LANES), jnp.float32)
    for w in range(2):
        above = jnp.where(even_row, g2_ref[2 * w, 0, 26:32], g1_ref[2 * w, 0, 26:32])
        below = jnp.where(even_row, g1_ref[2 * w, 0, 26:32], g2_ref[2 * w, 0, 26:32])
        for rg, rows in enumerate((above, m1_ref[2 * w, 0, 26:32], below)):
            for j in range(3):
                at = SHIFT - 8 + 8 * j
                LO[w, rg, at : at + 8] = jnp.broadcast_to(rows[2 * j : 2 * j + 1], (8, LANES))
                HI[w, rg, at : at + 8] = jnp.broadcast_to(rows[2 * j + 1 : 2 * j + 2], (8, LANES))
            LO[w, rg, 26:40] = jnp.zeros((14, LANES), jnp.float32)
            HI[w, rg, 26:40] = jnp.zeros((14, LANES), jnp.float32)
            LO[w, rg, 0:2] = jnp.zeros((2, LANES), jnp.float32)
            HI[w, rg, 0:2] = jnp.zeros((2, LANES), jnp.float32)
    for i in range(0, WIDE, 8):
        x = (col * BLOCKS + (i - SHIFT) + sub) * LANES
        XG[i : i + 8] = x
        valid = (x >= 0) & (x < total)
        CV[i : i + 8] = jnp.where(valid, 1.0, 0.0)
        MX[i : i + 8] = jnp.where(valid & (x + lane < total - 1), 1.0, 0.0)

    def ahead(ref, lead, i):
        here, after = ref[(*lead, pl.ds(i, 8))], ref[(*lead, pl.ds(i + 1, 8))]
        return here, pltpu.roll(jnp.where(lane == 0, after, here), LANES - 1, 1)

    def behind(ref, lead, i):
        here, before = ref[(*lead, pl.ds(i, 8))], ref[(*lead, pl.ds(i - 1, 8))]
        return here, pltpu.roll(jnp.where(lane == LANES - 1, before, here), 1, 1)

    def masks(ry):
        y = row * OUT_ROWS + ry - 4
        ok = jnp.where((y >= 0) & (y < n_row * OUT_ROWS), 1.0, 0.0)
        down = jnp.where((y >= 0) & (y < n_row * OUT_ROWS - 1), 1.0, 0.0)
        return ok, down

    def dual_step(k, w, ry, starts, ubar, p_in, p_out):
        ok, down = masks(ry)
        for g in starts:
            i = g + SHIFT
            mx = MX[i : i + 8] * ok
            my = CV[i : i + 8] * down
            if k == 0:
                here, right = ahead(F, (2 * w, ry), i)
                gx, gy = (right - here) * mx, (F[2 * w, ry + 1, pl.ds(i, 8)] - here) * my
                inverse = 1.0 + edge_gain * (gx * gx + gy * gy)
                ie = inverse * inverse
                IE[w, ry, pl.ds(i, 8)] = ie
            else:
                ie = IE[w, ry, pl.ds(i, 8)]
            lead = (2 * w + 1, ry) if k == 0 else (w, ry)
            lead_down = (2 * w + 1, ry + 1) if k == 0 else (w, ry + 1)
            here, right = ahead(ubar, lead, i)
            gx = (right - here) * mx
            gy = (ubar[(*lead_down, pl.ds(i, 8))] - here) * my
            if k == 0:
                qx, qy = sigma * gx, sigma * gy
            else:
                qx = p_in[0][w, ry, pl.ds(i, 8)] + sigma * gx
                qy = p_in[1][w, ry, pl.ds(i, 8)] + sigma * gy
            qx, qy = qx * (1.0 / (1.0 + sigma * huber_eps)), qy * (1.0 / (1.0 + sigma * huber_eps))
            shrink = lax.rsqrt(jnp.maximum(1.0, (qx * qx + qy * qy) * ie))
            p_out[0][w, ry, pl.ds(i, 8)] = qx * shrink
            p_out[1][w, ry, pl.ds(i, 8)] = qy * shrink

    def primal_step(k, w, sign, ry, starts, u_in, p_out, u_out, ubar_out):
        ok, _ = masks(ry)
        rg = (ry >= 4).astype(jnp.int32) + (ry >= 12).astype(jnp.int32)
        for g in starts:
            i = g + SHIFT
            here = pl.ds(i, 8)
            d0 = F[2 * w + 1, ry, here]
            if k == 0:
                t = lane - sign * d0.astype(jnp.int32)
                D[w, ry, here] = t
            else:
                t = D[w, ry, here]
            place, hop = t & (LANES - 1), t >> 7
            picks = [hop == -sign * m for m in range(1, 5)]

            def read(ref, lead):
                value = jnp.take_along_axis(ref[(*lead, here)], place, axis=1)
                for m in range(1, 5):
                    more = jnp.take_along_axis(ref[(*lead, pl.ds(i - sign * m, 8))], place, axis=1)
                    value = jnp.where(picks[m - 1], more, value)
                return value

            if k == 0:
                residue = read(F, (2 * (1 - w), ry)) - F[2 * w, ry, here]
                slope = read(G, (1 - w, ry)) * float(-sign)
                inv = 1.0 / jnp.maximum(slope * slope, slope_floor)
                target = XG[i : i + 8] + t
                inside = (target >= 0) & (target < total)
                rden = jnp.where(inside, 1.0 / (1.0 + tau * couple_weight), 1.0)
                if k + 1 < 4:
                    RES[w, ry, here] = residue
                    SL[w, ry, here] = slope
                    INV[w, ry, here] = inv
                    RD[w, ry, here] = rden
            else:
                residue, slope = RES[w, ry, here], SL[w, ry, here]
                inv, rden = INV[w, ry, here], RD[w, ry, here]
            partner = read(u_in, (2 * (1 - w) + 1, ry) if k == 0 else (1 - w, ry))
            u = d0 if k == 0 else u_in[w, ry, here]
            px, px_left = behind(p_out[0], (w, ry), i)
            div = px - px_left + p_out[1][w, ry, here] - p_out[1][w, ry - 1, here]
            blended = (u + tau * div + (tau * couple_weight) * partner) * rden
            mismatch = residue + slope * (blended - d0)
            limit = (data_weight * tau) * rden
            step = jnp.minimum(jnp.maximum(mismatch * inv, -limit), limit)
            new = jnp.minimum(jnp.maximum(blended - slope * step, LO[w, rg, here]), HI[w, rg, here])
            if k < 3:
                new = new * (CV[i : i + 8] * ok)
                u_out[w, ry, here] = new
                ubar_out[w, ry, here] = 2.0 * new - u
            else:
                OUT[ry - 4] = new - d0

    def run(v):
        own, other, slopes = plans(v)
        signs = (1 - 2 * v, 2 * v - 1)

        def slope_row(ry, carry):
            for w in range(2):
                for g in slopes[w]:
                    i = g + SHIFT
                    _, right = ahead(F, (2 * w, ry), i)
                    _, left = behind(F, (2 * w, ry), i)
                    G[w, ry, pl.ds(i, 8)] = (right - left) * 0.5
            return carry

        lax.fori_loop(1, 15, slope_row, 0)
        u_bufs = (F, UA, UB, UA, None)
        ubar_bufs = (F, RA, RB, RA, None)
        p_bufs = (None, (XA, YA), (XB, YB), (XA, YA), (XB, YB))
        for k in range(4):
            first, last = k + 1, 15 - k

            def dual_row(ry, k=k):
                for w, plan in enumerate((own, other)):
                    if plan[k] is not None:
                        dual_step(k, w, ry, plan[k][0], ubar_bufs[k], p_bufs[k], p_bufs[k + 1])

            def body(ry, carry, k=k, dual_row=dual_row):
                dual_row(ry)
                for w, plan in enumerate((own, other)):
                    if plan[k] is not None:
                        primal_step(k, w, signs[w], ry, plan[k][1], u_bufs[k], p_bufs[k + 1], u_bufs[k + 1], ubar_bufs[k + 1])
                return carry

            dual_row(first - 1)
            lax.fori_loop(first, last, body, 0)

    @pl.when(view == 0)
    def _():
        run(0)

    @pl.when(view == 1)
    def _():
        run(1)

    def from_slabs(slabs, put):
        parts = jnp.transpose(slabs, (1, 0, 2))
        for j in range(BLOCKS):
            put(slice(LANES * j, LANES * (j + 1)), parts[j])

    def put_refine(at, value):
        refine_ref[0, :, at] = value

    def put_x(at, value):
        dual_ref[0, 0, :, at] = value

    def put_y(at, value):
        dual_ref[0, 1, :, at] = value

    from_slabs(OUT[...], put_refine)
    from_slabs(XB[0, 4:12, SHIFT : SHIFT + 8], put_x)
    from_slabs(YB[0, 4:12, SHIFT : SHIFT + 8], put_y)


def on_device(sizes, image, coarse, bounds):
    f32 = jnp.float32
    vmem = pl.BlockSpec(memory_space=pltpu.VMEM)
    smem = pl.BlockSpec(memory_space=pltpu.SMEM)
    params = pltpu.CompilerParams(vmem_limit_bytes=VMEM_BYTES)
    own = pl.pallas_call(
        pack_kernel,
        out_shape=jax.ShapeDtypeStruct((TILE_PACK, BLOCKS, LANES), f32),
        in_specs=[vmem, vmem, smem],
        out_specs=vmem,
        compiler_params=params,
    )(image, coarse, bounds.reshape(1, 2))
    other = swapped(own, lambda v, r, c: (1 - v, r, c), sizes)
    thin_shape = jax.ShapeDtypeStruct((32, LANES), f32)
    both, thin1, thin2 = pl.pallas_call(
        join_kernel,
        out_shape=(jax.ShapeDtypeStruct((2 * TILE_PACK, BLOCKS, LANES), f32), thin_shape, thin_shape),
        in_specs=[vmem, vmem],
        out_specs=(vmem, vmem, vmem),
        compiler_params=params,
    )(own, other)
    side_b = swapped(both, lambda v, r, c: (v, r, ((c + 1) ^ 1) - 1), sizes)
    side_a = swapped(both, lambda v, r, c: (v, r, c ^ 1), sizes)
    thin2 = swapped(thin2, lambda v, r, c: (v, r, ((c + 2) ^ 2) - 2), sizes)
    thin1 = swapped(thin1, lambda v, r, c: (v, r, c ^ 2), sizes)
    strip = jax.ShapeDtypeStruct((4, 4, STRIP, LANES), f32)
    m1, m2 = pl.pallas_call(
        assemble_kernel,
        out_shape=(strip, strip),
        in_specs=[vmem] * 5,
        out_specs=(vmem, vmem),
        compiler_params=params,
    )(both, side_a, side_b, thin1, thin2)
    g2 = swapped(m2, lambda v, r, c: (v, ((r + 1) ^ 1) - 1, c), sizes)
    g1 = swapped(m1, lambda v, r, c: (v, r ^ 1, c), sizes)

    def field(n, dtype=f32):
        return pltpu.VMEM((n, TALL, WIDE, LANES), dtype)

    scratch = [field(4), field(2), field(2, jnp.int32)]
    scratch += [field(2) for _ in range(5)]
    scratch += [pltpu.VMEM((2, 3, WIDE, LANES), f32) for _ in range(2)]
    scratch += [field(2) for _ in range(8)]
    scratch += [pltpu.VMEM((WIDE, LANES), f32), pltpu.VMEM((WIDE, LANES), f32), pltpu.VMEM((WIDE, LANES), jnp.int32)]
    scratch += [pltpu.VMEM((OUT_ROWS, BLOCKS, LANES), f32)]
    refine, dual = pl.pallas_call(
        lambda *refs: refine_kernel(sizes, *refs),
        out_shape=(
            jax.ShapeDtypeStruct((1, OUT_ROWS, BLOCKS * LANES), f32),
            jax.ShapeDtypeStruct((1, 2, OUT_ROWS, BLOCKS * LANES), f32),
        ),
        in_specs=[vmem] * 4,
        out_specs=(vmem, vmem),
        scratch_shapes=scratch,
        compiler_params=params,
    )(m1, m2, g1, g2)
    return refine, dual


def solution(mesh):
    sizes = tuple(mesh.shape[axis] for axis in AXES)
    return jax.shard_map(
        lambda *args: on_device(sizes, *args),
        mesh=mesh,
        in_specs=(P("view", "row", "col"), P("view", "row", "col"), P("view", "row", "col", None)),
        out_specs=(P("view", "row", "col"), P("view", None, "row", "col")),
        check_vma=False,
    )
```

time: 458 us -> 48.4 us (0.11)
  local copies, waits for them, and re-layouts: 322 us -> 2.16 us
  starting transfers between devices: 119 us -> 22.5 us
  Pallas kernels: 0 us -> 12 us
  other arithmetic: 4.8 us -> 0 us
    gather x7 -> x0, local copies, waits for them, and re-layouts: 319 us -> none  [flat_read(): jnp.take(strip.reshape(-1), flat_index.reshape(-1), axis=0, mode='clip')]
    ppermute x35 -> x7, starting transfers between devices: 119 us -> 22.5 us  [swapped(): return lax.ppermute(block, AXES, route)]
    pallas_call x0 -> x4, Pallas kernels: none -> 12 us  [the longest x1 11.3 us: on_device(): pl.pallas_call(lambda *refs: refine_kernel(sizes, *refs), out_shape=(jax....]
    ppermute x35 -> x7, waiting for transfers between devices: 6.85 us -> 10.8 us  [swapped(): return lax.ppermute(block, AXES, route)]
  transfers between devices with their start and end apart: 35 -> 7, of which waited for: 10 -> 3; matrix products, arithmetic and copies ran while one was open for 21% -> 0% of each run, Pallas kernels for 0% -> 0%
where the time goes in v1:
time: 48.4 us; the launch traced here: 48.1 us
  starting transfers between devices  22.5 us (46%)
  Pallas kernels  12 us (25%)
  waiting for transfers between devices  10.8 us (22%)
  local copies, waits for them, and re-layouts  2.16 us (4%)
  between operations  0.71 us (1%)
    ppermute x7, starting transfers between devices, swapped(): return lax.ppermute(block, AXES, route)  22.5 us
    pallas_call x1, Pallas kernels, on_device(): pl.pallas_call(lambda *refs: refine_kernel(sizes, *refs), out_shape=(jax....  11.3 us
    ppermute x7, waiting for transfers between devices, swapped(): return lax.ppermute(block, AXES, route)  10.8 us
    unnamed x6, local copies, waits for them, and re-layouts  2.16 us
  transfers between devices with their start and end apart: 7, of which 3 were waited for; matrix products, arithmetic and copies ran while one was open for 0% of the time, Pallas kernels for 0%

profile of v1, /device:TPU:25, one launch (start us, length us, event | category | flops | bytes accessed | tf_op | source)
XLA Modules:
  0.0 48.1 jit_solution(4759921194861933436)
XLA Ops:
  0.6 0.0 copy-start.2
  0.6 0.6 %copy-done.2 = s32[1,1,1,2]{3,2,1,0:T(1,128)S(1)} copy-done((s32[1,1,1,2]{3,2,1,0:T(1,128)S(1)}, s32[1,1,1,2]{3,2,1,0:T(1,128)}, u32[]{:S(2)}) %copy-start.2) | copy-done | bytes 32
  1.3 0.0 copy-start
  1.3 0.8 %copy-done = f32[1,8,1024]{2,1,0:T(8,128)S(1)} copy-done((f32[1,8,1024]{2,1,0:T(8,128)S(1)}, f32[1,8,1024]{2,1,0:T(8,128)}, u32[]{:S(2)}) %copy-start) | copy-done | bytes 32792
  2.0 0.0 copy-start.1
  2.0 0.8 %copy-done.1 = s32[1,8,1024]{2,1,0:T(8,128)S(1)} copy-done((s32[1,8,1024]{2,1,0:T(8,128)S(1)}, s32[1,8,1024]{2,1,0:T(8,128)}, u32[]{:S(2)}) %copy-start.1) | copy-done | bytes 32792
  2.8 0.6 %shard_map.50.own_ref = f32[17,8,128]{2,1,0:T(8,128)S(1)} custom-call(f32[1,8,1024]{2,1,0:T(8,128)S(1)} %copy-done, s32[1,8,1024]{2,1,0:T(8,128)S(1)} %copy-done.1, s32[1,2]{1,0:T(1,128)S(1)} %bitcast.1), custom_call_target="tpu_custom_call" | custom-call | tf_op jit(solution)/shard_map/pallas_call | solution.py:316
  3.4 2.8 %collective-permute-start = (f32[17,8,128]{2,1,0:T(8,128)S(1)}, f32[17,8,128]{2,1,0:T(8,128)S(1)}, u32[]{:S(2)}, u32[]{:S(2)}) collective-permute-start(f32[17,8,128]{2,1,0:T(8,128)S(1)} %shard_map.50.own_ref), channel_id=1, source_target_pairs={{0,128},{1,129},{2,130},{3,131},{4,132},{5,133},{6,134},{7,135},{8... | collective-permute-start | bytes 208904 | tf_op jit(solution)/shard_map/ppermute | solution.py:37
  6.2 1.9 %collective-permute-done.other_ref = f32[17,8,128]{2,1,0:T(8,128)S(1)} collective-permute-done((f32[17,8,128]{2,1,0:T(8,128)S(1)}, f32[17,8,128]{2,1,0:T(8,128)S(1)}, u32[]{:S(2)}, u32[]{:S(2)}) %collective-permute-start) | collective-permute-done | bytes 69664 | tf_op jit(solution)/shard_map/ppermute | solution.py:37
  8.2 7.7 %collective-permute-start.2 = (f32[34,8,128]{2,1,0:T(8,128)S(1)}, f32[34,8,128]{2,1,0:T(8,128)S(1)}, u32[]{:S(2)}, u32[]{:S(2)}) collective-permute-start(f32[34,8,128]{2,1,0:T(8,128)S(1)} %get-tuple-element.7.both_ref), channel_id=1, source_target_pairs={{1,2},{2,1},{3,4},{4,3},{5,6},{6,5},{7,8},{8,7},{9,10},{10,9},{11,... | collective-permute-start | bytes 417800 | tf_op jit(solution)/shard_map/ppermute | solution.py:37
  15.8 0.1 collective-permute-start.1
  15.9 1.7 %collective-permute-start.3 = (f32[32,128]{1,0:T(8,128)S(1)}, f32[32,128]{1,0:T(8,128)S(1)}, u32[]{:S(2)}, u32[]{:S(2)}) collective-permute-start(f32[32,128]{1,0:T(8,128)S(1)} %get-tuple-element.8), channel_id=1, source_target_pairs={{0,2},{1,3},{2,0},{3,1},{4,6},{5,7},{6,4},{7,5},{8,10},{9,11},{10,... | collective-permute-start | bytes 49160 | tf_op jit(solution)/shard_map/ppermute | solution.py:37
  17.6 3.3 %collective-permute-start.4 = (f32[32,128]{1,0:T(8,128)S(1)}, f32[32,128]{1,0:T(8,128)S(1)}, u32[]{:S(2)}, u32[]{:S(2)}) collective-permute-start(f32[32,128]{1,0:T(8,128)S(1)} %get-tuple-element.9), channel_id=1, source_target_pairs={{2,4},{3,5},{4,2},{5,3},{6,8},{7,9},{8,6},{9,7},{10,12},{11,13},{1... | collective-permute-start | bytes 49160 | tf_op jit(solution)/shard_map/ppermute | solution.py:37
  20.9 0.0 collective-permute-done.3.thin1_ref
  20.9 4.2 %collective-permute-done.4.thin2_ref = f32[32,128]{1,0:T(8,128)S(1)} collective-permute-done((f32[32,128]{1,0:T(8,128)S(1)}, f32[32,128]{1,0:T(8,128)S(1)}, u32[]{:S(2)}, u32[]{:S(2)}) %collective-permute-start.4) | collective-permute-done | bytes 16416 | tf_op jit(solution)/shard_map/ppermute | solution.py:37
  25.1 0.0 collective-permute-done.2.b_ref
  25.1 0.0 collective-permute-done.1.a_ref
  25.1 0.1 shard_map.52
  25.2 3.9 %collective-permute-start.5 = (f32[4,4,32,128]{3,2,1,0:T(8,128)S(1)}, f32[4,4,32,128]{3,2,1,0:T(8,128)S(1)}, u32[]{:S(2)}, u32[]{:S(2)}) collective-permute-start(f32[4,4,32,128]{3,2,1,0:T(8,128)S(1)} %get-tuple-element.10.refs_0_), channel_id=1, source_target_pairs={{0,32},{1,33},{2,34},{3,35},{4,36},{5,37},{6,38},{7,39},{8,40},{9,... | collective-permute-start | bytes 786440 | tf_op jit(solution)/shard_map/ppermute | solution.py:37
  29.1 3.0 %collective-permute-start.6 = (f32[4,4,32,128]{3,2,1,0:T(8,128)S(1)}, f32[4,4,32,128]{3,2,1,0:T(8,128)S(1)}, u32[]{:S(2)}, u32[]{:S(2)}) collective-permute-start(f32[4,4,32,128]{3,2,1,0:T(8,128)S(1)} %get-tuple-element.11.refs_1_), channel_id=1, source_target_pairs={{32,64},{33,65},{34,66},{35,67},{36,68},{37,69},{38,70},{39,71},{4... | collective-permute-start | bytes 786440 | tf_op jit(solution)/shard_map/ppermute | solution.py:37
  32.1 0.0 collective-permute-done.5.refs_2_
  32.1 4.6 %collective-permute-done.6.refs_3_ = f32[4,4,32,128]{3,2,1,0:T(8,128)S(1)} collective-permute-done((f32[4,4,32,128]{3,2,1,0:T(8,128)S(1)}, f32[4,4,32,128]{3,2,1,0:T(8,128)S(1)}, u32[]{:S(2)}, u32[]{:S(2)}) %collective-permute-start.6) | collective-permute-done | bytes 262176 | tf_op jit(solution)/shard_map/ppermute | solution.py:37
  36.8 11.3 %shard_map.53 = (f32[1,8,1024]{2,1,0:T(8,128)}, f32[1,2,8,1024]{3,2,1,0:T(8,128)}) custom-call(f32[4,4,32,128]{3,2,1,0:T(8,128)S(1)} %get-tuple-element.10.refs_0_, f32[4,4,32,128]{3,2,1,0:T(8,128)S(1)} %get-tuple-element.11.refs_1_, f32[4,4,32,128]{3,2,1,0:T(8,128)S(1)} %collective-permute-done.5.refs_2_, f32[4,4,32,128]{3,2,1,0:T(8,128)S(1)} %collective-permute-done.6.refs_3_), custom_call_target="tpu_custom_call" | custom-call | tf_op jit(solution)/shard_map/pallas_call | solution.py:356
  (1 shorter events, 0.0 us)
Async XLA Ops:
  0.6 0.7 %copy-start.2 = (s32[1,1,1,2]{3,2,1,0:T(1,128)S(1)}, s32[1,1,1,2]{3,2,1,0:T(1,128)}, u32[]{:S(2)}) copy-start(s32[1,1,1,2]{3,2,1,0:T(1,128)} %param.5) | copy-start | bytes 28
  1.3 0.8 %copy-start = (f32[1,8,1024]{2,1,0:T(8,128)S(1)}, f32[1,8,1024]{2,1,0:T(8,128)}, u32[]{:S(2)}) copy-start(f32[1,8,1024]{2,1,0:T(8,128)} %image_ref.1) | copy-start | bytes 98308
  2.0 0.8 %copy-start.1 = (s32[1,8,1024]{2,1,0:T(8,128)S(1)}, s32[1,8,1024]{2,1,0:T(8,128)}, u32[]{:S(2)}) copy-start(s32[1,8,1024]{2,1,0:T(8,128)} %coarse_ref.1) | copy-start | bytes 98308
  3.4 4.8 %collective-permute-start = (f32[17,8,128]{2,1,0:T(8,128)S(1)}, f32[17,8,128]{2,1,0:T(8,128)S(1)}, u32[]{:S(2)}, u32[]{:S(2)}) collective-permute-start(f32[17,8,128]{2,1,0:T(8,128)S(1)} %shard_map.50.own_ref), channel_id=1, source_target_pairs={{0,128},{1,129},{2,130},{3,131},{4,132},{5,133},{6,134},{7,135},{8... | collective-permute-start | bytes 208904 | tf_op jit(solution)/shard_map/ppermute | solution.py:37
  8.2 17.0 %collective-permute-start.2 = (f32[34,8,128]{2,1,0:T(8,128)S(1)}, f32[34,8,128]{2,1,0:T(8,128)S(1)}, u32[]{:S(2)}, u32[]{:S(2)}) collective-permute-start(f32[34,8,128]{2,1,0:T(8,128)S(1)} %get-tuple-element.7.both_ref), channel_id=1, source_target_pairs={{1,2},{2,1},{3,4},{4,3},{5,6},{6,5},{7,8},{8,7},{9,10},{10,9},{11,... | collective-permute-start | bytes 417800 | tf_op jit(solution)/shard_map/ppermute | solution.py:37
  15.8 9.3 %collective-permute-start.1 = (f32[34,8,128]{2,1,0:T(8,128)S(1)}, f32[34,8,128]{2,1,0:T(8,128)S(1)}, u32[]{:S(2)}, u32[]{:S(2)}) collective-permute-start(f32[34,8,128]{2,1,0:T(8,128)S(1)} %get-tuple-element.7.both_ref), channel_id=1, source_target_pairs={{0,1},{1,0},{2,3},{3,2},{4,5},{5,4},{6,7},{7,6},{8,9},{9,8},{10,11... | collective-permute-start | bytes 417800 | tf_op jit(solution)/shard_map/ppermute | solution.py:37
  15.9 5.0 %collective-permute-start.3 = (f32[32,128]{1,0:T(8,128)S(1)}, f32[32,128]{1,0:T(8,128)S(1)}, u32[]{:S(2)}, u32[]{:S(2)}) collective-permute-start(f32[32,128]{1,0:T(8,128)S(1)} %get-tuple-element.8), channel_id=1, source_target_pairs={{0,2},{1,3},{2,0},{3,1},{4,6},{5,7},{6,4},{7,5},{8,10},{9,11},{10,... | collective-permute-start | bytes 49160 | tf_op jit(solution)/shard_map/ppermute | solution.py:37
  17.6 7.5 %collective-permute-start.4 = (f32[32,128]{1,0:T(8,128)S(1)}, f32[32,128]{1,0:T(8,128)S(1)}, u32[]{:S(2)}, u32[]{:S(2)}) collective-permute-start(f32[32,128]{1,0:T(8,128)S(1)} %get-tuple-element.9), channel_id=1, source_target_pairs={{2,4},{3,5},{4,2},{5,3},{6,8},{7,9},{8,6},{9,7},{10,12},{11,13},{1... | collective-permute-start | bytes 49160 | tf_op jit(solution)/shard_map/ppermute | solution.py:37
  25.2 6.9 %collective-permute-start.5 = (f32[4,4,32,128]{3,2,1,0:T(8,128)S(1)}, f32[4,4,32,128]{3,2,1,0:T(8,128)S(1)}, u32[]{:S(2)}, u32[]{:S(2)}) collective-permute-start(f32[4,4,32,128]{3,2,1,0:T(8,128)S(1)} %get-tuple-element.10.refs_0_), channel_id=1, source_target_pairs={{0,32},{1,33},{2,34},{3,35},{4,36},{5,37},{6,38},{7,39},{8,40},{9,... | collective-permute-start | bytes 786440 | tf_op jit(solution)/shard_map/ppermute | solution.py:37
  29.1 7.7 %collective-permute-start.6 = (f32[4,4,32,128]{3,2,1,0:T(8,128)S(1)}, f32[4,4,32,128]{3,2,1,0:T(8,128)S(1)}, u32[]{:S(2)}, u32[]{:S(2)}) collective-permute-start(f32[4,4,32,128]{3,2,1,0:T(8,128)S(1)} %get-tuple-element.11.refs_1_), channel_id=1, source_target_pairs={{32,64},{33,65},{34,66},{35,67},{36,68},{37,69},{38,70},{39,71},{4... | collective-permute-start | bytes 786440 | tf_op jit(solution)/shard_map/ppermute | solution.py:37

commit v2 on v1

v2 whole, which is shorter than its diff:
```python
import jax
import jax.numpy as jnp
from jax import lax
from jax.experimental import pallas as pl
from jax.experimental.pallas import tpu as pltpu
from jax.sharding import PartitionSpec as P

AXES = ("view", "row", "col")
LANES = 128
OUT_ROWS = 8
BLOCKS = 8
TILE_PACK = 17
STRIP = 36
SHIFT = 16
WIDE = 40
TALL = 16
VMEM_BYTES = 40 * 1024 * 1024

tau = 0.25
sigma = 0.5
huber_eps = 0.05
edge_gain = 2.0
slope_floor = 0.05
couple_weight = 0.5
data_weight = 1.0


def swapped(block, partner, sizes):
    views, rows, cols = sizes
    route = []
    for v in range(views):
        for r in range(rows):
            for c in range(cols):
                to_v, to_r, to_c = partner(v, r, c)
                if 0 <= to_r < rows and 0 <= to_c < cols:
                    route.append(((v * rows + r) * cols + c, (to_v * rows + to_r) * cols + to_c))
    return lax.ppermute(block, AXES, route)


def to_slabs(tile):
    parts = jnp.stack([tile[:, LANES * j : LANES * (j + 1)] for j in range(BLOCKS)])
    return jnp.transpose(parts, (1, 0, 2))


def pack_kernel(image_hbm, coarse_hbm, bounds_hbm, out_ref, edge_ref, image_ref, coarse_ref, bounds_ref, sems):
    copies = [
        pltpu.make_async_copy(source, target, sems.at[n])
        for n, (source, target) in enumerate(
            ((image_hbm, image_ref), (coarse_hbm, coarse_ref), (bounds_hbm, bounds_ref))
        )
    ]
    for copy in copies:
        copy.start()
    odd = (lax.axis_index("col") & 1) == 1
    last = (BLOCKS - 1) * LANES
    copies[0].wait()
    image = image_ref[0]
    out_ref[0:8] = to_slabs(image)
    edge_ref[0] = jnp.where(odd, image[:, :LANES], image[:, last:])
    copies[1].wait()
    coarse = coarse_ref[0].astype(jnp.float32)
    out_ref[8:16] = to_slabs(coarse)
    edge_ref[1] = jnp.where(odd, coarse[:, :LANES], coarse[:, last:])
    copies[2].wait()
    sub = lax.broadcasted_iota(jnp.int32, (BLOCKS, LANES), 0)
    out_ref[16] = jnp.where(sub == 0, bounds_ref[0, 0, 0, 0], bounds_ref[0, 0, 0, 1]).astype(jnp.float32)


def join_kernel(own_ref, other_ref, edge_own_ref, edge_other_ref, both_ref, more_ref):
    for ref in (both_ref, more_ref):
        ref[0:TILE_PACK] = own_ref[...]
        ref[TILE_PACK : 2 * TILE_PACK] = other_ref[...]
    more_ref[2 * TILE_PACK] = edge_own_ref[0]
    more_ref[2 * TILE_PACK + 1 :] = edge_other_ref[...]


def near_kernel(b_ref, out_ref):
    odd = (lax.axis_index("col") & 1) == 1
    for n, base in enumerate((0, TILE_PACK, TILE_PACK + 8)):
        for y in range(8):
            out_ref[n, y : y + 1, :] = jnp.where(odd, b_ref[base + y, 0:1], b_ref[base + y, 7:8])


def halo_slabs(view):
    mid = (-5, 1) if view == 0 else (-1, 5)
    slabs = [(p, d, g) for p in (0, 1) for d in (1, 2) for g in (-8, 0, 8)]
    slabs += [(p, d, g) for p in (0, 1) for d in (3, 4) for g in (-1, 1)]
    slabs += [(p, 1, g) for p in (2, 3) for g in (-8, 0, 8)]
    slabs += [(p, d, g) for p in (2, 3) for d in (2, 3) for g in mid]
    return slabs


def assemble_kernel(both_ref, a_ref, b_ref, far_ref, m1_ref, m2_ref, F, LO, HI):
    odd = (lax.axis_index("col") & 1) == 1
    even_row = (lax.axis_index("row") & 1) == 0
    first = lax.axis_index("view") == 0
    zero = jnp.zeros((8, LANES), jnp.float32)
    for plane in range(4):
        base = (plane // 2) * TILE_PACK + (plane % 2) * 8
        for y in range(8):
            at = base + y
            F[plane, y + 4, 0:8] = zero
            F[plane, y + 4, 8:16] = jnp.where(odd, a_ref[at], b_ref[at])
            F[plane, y + 4, 16:24] = both_ref[at]
            F[plane, y + 4, 24:32] = jnp.where(odd, b_ref[at], a_ref[at])
            F[plane, y + 4, 32:40] = zero
    far, near = far_ref[...], b_ref[2 * TILE_PACK :]
    left, right = jnp.where(odd, far, near), jnp.where(odd, near, far)
    cross = jnp.where(first, left, right)
    low, high = SHIFT - 9, SHIFT + 16
    for y in range(8):
        row = slice(y, y + 1)
        F[0, y + 4, low : low + 1] = left[0, row]
        F[0, y + 4, high : high + 1] = right[0, row]
        for plane in (2, 3):
            F[plane, y + 4, low : low + 1] = cross[plane - 1, row]
            F[plane, y + 4, high : high + 1] = cross[plane - 1, row]

    def put(at, top, bottom):
        m1_ref[at] = jnp.where(even_row, bottom, top)
        m2_ref[at] = jnp.where(even_row, top, bottom)

    for at, ((plane, d, g), (_, _, g1)) in enumerate(zip(halo_slabs(0), halo_slabs(1), strict=True)):
        pair = []
        for ry in (3 + d, 12 - d):
            value = F[plane, ry, SHIFT + g : SHIFT + g + 8]
            if g1 != g:
                value = jnp.where(first, value, F[plane, ry, SHIFT + g1 : SHIFT + g1 + 8])
            pair.append(value)
        put(at, *pair)
    for w in range(2):
        s = w * TILE_PACK + 16
        tiles = (jnp.where(odd, a_ref[s], b_ref[s]), both_ref[s], jnp.where(odd, b_ref[s], a_ref[s]))
        thin = [jnp.concatenate([cross[1, y : y + 1], cross[2, y : y + 1]], axis=0) for y in (0, 7)]
        ends = [jnp.concatenate([t[0:2] for t in tiles] + [t], axis=0) for t in thin]
        put(STRIP - 2 + w, *ends)
        spread_bounds(LO, HI, w, 1, ends[0])


def spread_bounds(LO, HI, w, rg, rows):
    zero = jnp.zeros((8, LANES), jnp.float32)
    for j in range(3):
        at = SHIFT - 8 + 8 * j
        LO[w, rg, at : at + 8] = jnp.broadcast_to(rows[2 * j : 2 * j + 1], (8, LANES))
        HI[w, rg, at : at + 8] = jnp.broadcast_to(rows[2 * j + 1 : 2 * j + 2], (8, LANES))
    for ref in (LO, HI):
        ref[w, rg, 0:8] = zero
        ref[w, rg, 32:40] = zero


def plans(view):
    if view == 0:
        other_wide = (((-9, -1, 4), (-8, 0, 4)), ((-5, 1), (-5, 1)), ((-5, 0), (-4, 0)))
        other_narrow = ((-5, 1), (-5, 1))
        slope_wide, slope_narrow = (-9, -1, 5), (-5, 1)
    else:
        other_wide = (((-5, 3, 8), (-4, 4, 8)), ((-1, 5), (-1, 5)), ((-1, 4), (0, 4)))
        other_narrow = ((-1, 5), (-1, 5))
        slope_wide, slope_narrow = (-5, 3, 9), (-1, 5)
    own_wide = (((-5, 3, 5), (-5, 3, 5)), ((-5, 3, 4), (-4, 4)), ((-1, 1), (-1, 1)), ((-1, 0), (0,)))
    own_narrow = ((-1, 1), (-1, 1))
    return own_wide, own_narrow, other_wide, other_narrow, slope_wide, slope_narrow


def make_steps(sizes, state, MX, CV, XG, OUT):
    (F, LO, HI, G, D, RES, SL, INV, RD, IE, UA, RA, UB, RB, XA, YA, XB, YB) = state
    _, n_row, n_col = sizes
    view, row, col = lax.axis_index("view"), lax.axis_index("row"), lax.axis_index("col")
    lane = lax.broadcasted_iota(jnp.int32, (8, LANES), 1)
    sub = lax.broadcasted_iota(jnp.int32, (8, LANES), 0)
    total = n_col * BLOCKS * LANES
    u_bufs = (F, UA, UB, UA, None)
    ubar_bufs = (F, RA, RB, RA, None)
    p_bufs = (None, (XA, YA), (XB, YB), (XA, YA), (XB, YB))
    for i in range(0, WIDE, 8):
        x = (col * BLOCKS + (i - SHIFT) + sub) * LANES
        XG[i : i + 8] = x
        valid = (x >= 0) & (x < total)
        CV[i : i + 8] = jnp.where(valid, 1.0, 0.0)
        MX[i : i + 8] = jnp.where(valid & (x + lane < total - 1), 1.0, 0.0)

    def ahead(ref, lead, i):
        here, after = ref[(*lead, pl.ds(i, 8))], ref[(*lead, pl.ds(i + 1, 8))]
        return here, pltpu.roll(jnp.where(lane == 0, after, here), LANES - 1, 1)

    def behind(ref, lead, i):
        here, before = ref[(*lead, pl.ds(i, 8))], ref[(*lead, pl.ds(i - 1, 8))]
        return here, pltpu.roll(jnp.where(lane == LANES - 1, before, here), 1, 1)

    def masks(ry):
        y = row * OUT_ROWS + ry - 4
        ok = jnp.where((y >= 0) & (y < n_row * OUT_ROWS), 1.0, 0.0)
        down = jnp.where((y >= 0) & (y < n_row * OUT_ROWS - 1), 1.0, 0.0)
        return ok, down

    def dual_step(k, w, ry, starts, ubar, p_in, p_out, stores):
        ok, down = masks(ry)
        for g in starts:
            i = g + SHIFT
            mx = MX[i : i + 8] * ok
            my = CV[i : i + 8] * down
            here_at = (w, ry, pl.ds(i, 8))
            if k == 0:
                here, right = ahead(F, (2 * w, ry), i)
                gx, gy = (right - here) * mx, (F[2 * w, ry + 1, pl.ds(i, 8)] - here) * my
                inverse = 1.0 + edge_gain * (gx * gx + gy * gy)
                ie = inverse * inverse
                stores.append((IE, here_at, ie))
            else:
                ie = IE[here_at]
            lead = (2 * w + 1, ry) if k == 0 else (w, ry)
            lead_down = (2 * w + 1, ry + 1) if k == 0 else (w, ry + 1)
            here, right = ahead(ubar, lead, i)
            gx = (right - here) * mx
            gy = (ubar[(*lead_down, pl.ds(i, 8))] - here) * my
            if k == 0:
                qx, qy = sigma * gx, sigma * gy
            else:
                qx = p_in[0][here_at] + sigma * gx
                qy = p_in[1][here_at] + sigma * gy
            qx, qy = qx * (1.0 / (1.0 + sigma * huber_eps)), qy * (1.0 / (1.0 + sigma * huber_eps))
            shrink = lax.rsqrt(jnp.maximum(1.0, (qx * qx + qy * qy) * ie))
            stores.append((p_out[0], here_at, qx * shrink))
            stores.append((p_out[1], here_at, qy * shrink))

    def primal_step(k, w, sign, ry, starts, u_in, p_out, u_out, ubar_out, stores):
        ok, _ = masks(ry)
        rg = sum(int(ry >= n) if isinstance(ry, int) else (ry >= n).astype(jnp.int32) for n in (4, 12))
        for g in starts:
            i = g + SHIFT
            here = pl.ds(i, 8)
            here_at = (w, ry, here)
            d0 = F[2 * w + 1, ry, here]
            if k == 0:
                t = lane - sign * d0.astype(jnp.int32)
                stores.append((D, here_at, t))
            else:
                t = D[here_at]
            place, hop = t & (LANES - 1), t >> 7
            picks = [hop == -sign * m for m in range(1, 5)]

            def read(ref, lead):
                value = jnp.take_along_axis(ref[(*lead, here)], place, axis=1)
                for m in range(1, 5):
                    more = jnp.take_along_axis(ref[(*lead, pl.ds(i - sign * m, 8))], place, axis=1)
                    value = jnp.where(picks[m - 1], more, value)
                return value

            if k == 0:
                residue = read(F, (2 * (1 - w), ry)) - F[2 * w, ry, here]
                slope = read(G, (1 - w, ry)) * float(-sign)
                inv = 1.0 / jnp.maximum(slope * slope, slope_floor)
                target = XG[i : i + 8] + t
                inside = (target >= 0) & (target < total)
                rden = jnp.where(inside, 1.0 / (1.0 + tau * couple_weight), 1.0)
                stores += [(RES, here_at, residue), (SL, here_at, slope), (INV, here_at, inv), (RD, here_at, rden)]
            else:
                residue, slope = RES[here_at], SL[here_at]
                inv, rden = INV[here_at], RD[here_at]
            partner = read(u_in, (2 * (1 - w) + 1, ry) if k == 0 else (1 - w, ry))
            u = d0 if k == 0 else u_in[here_at]
            px, px_left = behind(p_out[0], (w, ry), i)
            div = px - px_left + p_out[1][here_at] - p_out[1][w, ry - 1, here]
            blended = (u + tau * div + (tau * couple_weight) * partner) * rden
            mismatch = residue + slope * (blended - d0)
            limit = (data_weight * tau) * rden
            step = jnp.minimum(jnp.maximum(mismatch * inv, -limit), limit)
            new = jnp.minimum(jnp.maximum(blended - slope * step, LO[w, rg, here]), HI[w, rg, here])
            if k < 3:
                new = new * (CV[i : i + 8] * ok)
                stores.append((u_out, here_at, new))
                stores.append((ubar_out, here_at, 2.0 * new - u))
            else:
                stores.append((OUT, (ry - 4,), new - d0))

    def slope_step(w, ry, starts, stores):
        for g in starts:
            i = g + SHIFT
            _, right = ahead(F, (2 * w, ry), i)
            _, left = behind(F, (2 * w, ry), i)
            stores.append((G, (w, ry, pl.ds(i, 8)), (right - left) * 0.5))

    def dual(k, w, y, starts, stores):
        dual_step(k, w, y + 4, starts, ubar_bufs[k], p_bufs[k], p_bufs[k + 1], stores)

    def primal(k, w, y, sign, starts, stores):
        primal_step(k, w, sign, y + 4, starts, u_bufs[k], p_bufs[k + 1], u_bufs[k + 1], ubar_bufs[k + 1], stores)

    def slopes(w, y, starts, stores):
        slope_step(w, y + 4, starts, stores)

    return dual, primal, slopes


def flush(stores):
    for ref, at, value in stores:
        ref[at] = value


def by_view(run):
    view = lax.axis_index("view")

    @pl.when(view == 0)
    def _():
        run(0)

    @pl.when(view == 1)
    def _():
        run(1)


def inner_kernel(sizes, F, LO, HI, *refs):
    state, (MX, CV, XG) = (F, LO, HI, *refs[:15]), refs[15:]
    dual, primal, slopes = make_steps(sizes, state, MX, CV, XG, None)

    def run(v):
        own, _, other, _, slope_other, _ = plans(v)
        signs = (1 - 2 * v, 2 * v - 1)
        for k in range(3):
            first, last = k + 1, 7 - k

            def dual_row(y, stores, k=k):
                for w, plan in enumerate((own, other)):
                    dual(k, w, y, plan[k][0], stores)
                if k == 0:
                    slopes(0, y, (-8, 0, 8), stores)
                    slopes(1, y, slope_other, stores)

            def body(y, carry, k=k, dual_row=dual_row, last=last):
                stores = []
                for w, plan in enumerate((own, other)):
                    primal(k, w, y, signs[w], plan[k][1], stores)
                dual_row(jnp.minimum(y + 1, last - 1), stores)
                flush(stores)
                return carry

            for y in (first - 1, first):
                stores = []
                dual_row(y, stores)
                flush(stores)
            lax.fori_loop(first, last, body, 0)
        stores = []
        slopes(0, 7, (-8, 0, 8), stores)
        slopes(1, 7, slope_other, stores)
        flush(stores)

    by_view(run)


def outer_kernel(sizes, m1_ref, m2_ref, g1_ref, g2_ref, *refs):
    refine_ref, dual_ref = refs[18:20]
    state = refs[20:38]
    MX, CV, XG, OUT = refs[38:]
    F, LO, HI = state[:3]
    XB, YB = state[16:]
    dual, primal, slopes = make_steps(sizes, state, MX, CV, XG, OUT)
    even_row = (lax.axis_index("row") & 1) == 0

    def above_below(at):
        one, two = g1_ref[at], g2_ref[at]
        return jnp.where(even_row, two, one), jnp.where(even_row, one, two)

    def run(v):
        own, own_narrow, other, other_narrow, slope_wide, slope_narrow = plans(v)
        signs = (1 - 2 * v, 2 * v - 1)
        for at, (plane, d, g) in enumerate(halo_slabs(v)):
            above, below = above_below(at)
            F[plane, 4 - d, SHIFT + g : SHIFT + g + 8] = above
            F[plane, 11 + d, SHIFT + g : SHIFT + g + 8] = below
        thin = SHIFT - 9 if v == 0 else SHIFT + 16
        for w in range(2):
            above, below = above_below(STRIP - 2 + w)
            spread_bounds(LO, HI, w, 0, above)
            spread_bounds(LO, HI, w, 2, below)
            if w == 0:
                for plane in (2, 3):
                    F[plane, 3, thin : thin + 1] = above[4 + plane : 5 + plane]
                    F[plane, 12, thin : thin + 1] = below[4 + plane : 5 + plane]
        stores = []
        for y in (-2, -1, 8, 9):
            slopes(0, y, (-5, 3, 5), stores)
        for y in (-1, 8):
            slopes(1, y, slope_wide, stores)
        for y in (-3, -2, 9, 10):
            slopes(1, y, slope_narrow, stores)
        flush(stores)

        def pairs(step):
            def body(i, carry):
                stores = []
                step(i, stores)
                flush(stores)
                return carry

            lax.fori_loop(0, 2, body, 0)

        def block(step):
            stores = []
            step(stores)
            flush(stores)

        for k in range(3):
            narrow_own = own_narrow if k < 2 else own[2]
            narrow_other = other_narrow if k == 0 else other[k]
            top_o, low_o = k - 4, 9 - k
            top_n, low_n = k - 3, 8 - k

            def dual_loop(i, stores):
                for y in (top_o + i, low_o + i):
                    dual(k, 0, y, narrow_own[0], stores)
                for y in (top_n + i, low_n + i):
                    dual(k, 1, y, narrow_other[0], stores)

            def dual_block(stores):
                for y in (k - 2, k - 1, 7 - k, 8 - k):
                    dual(k, 0, y, own[k][0], stores)
                for y in (k - 1, 7 - k):
                    dual(k, 1, y, other[k][0], stores)

            def primal_loop(i, stores):
                for y in (k - 3 + i, 9 - k + i):
                    primal(k, 0, y, signs[0], narrow_own[1], stores)
                for y in (k - 2 + i, 8 - k + i):
                    primal(k, 1, y, signs[1], narrow_other[1], stores)

            def primal_block(stores):
                for y in (k - 1, k, 7 - k, 8 - k):
                    primal(k, 0, y, signs[0], own[k][1], stores)
                for y in (k, 7 - k):
                    primal(k, 1, y, signs[1], other[k][1], stores)

            pairs(dual_loop)
            block(dual_block)
            pairs(primal_loop)
            block(primal_block)

        def last_dual(i, carry):
            stores = []
            for y in (3 * i - 1, 3 * i, 3 * i + 1):
                dual(3, 0, y, own[3][0], stores)
            flush(stores)
            return carry

        def last_primal(i, carry):
            stores = []
            for y in (4 * i, 4 * i + 1, 4 * i + 2, 4 * i + 3):
                primal(3, 0, y, signs[0], own[3][1], stores)
            flush(stores)
            return carry

        lax.fori_loop(0, 3, last_dual, 0)
        lax.fori_loop(0, 2, last_primal, 0)

    by_view(run)

    def from_slabs(slabs, put):
        parts = jnp.transpose(slabs, (1, 0, 2))
        for j in range(BLOCKS):
            put(slice(LANES * j, LANES * (j + 1)), parts[j])

    def put_refine(at, value):
        refine_ref[0, :, at] = value

    def put_x(at, value):
        dual_ref[0, 0, :, at] = value

    def put_y(at, value):
        dual_ref[0, 1, :, at] = value

    from_slabs(OUT[...], put_refine)
    from_slabs(XB[0, 4:12, SHIFT : SHIFT + 8], put_x)
    from_slabs(YB[0, 4:12, SHIFT : SHIFT + 8], put_y)


def on_device(sizes, image, coarse, bounds):
    f32 = jnp.float32
    vmem = pl.BlockSpec(memory_space=pltpu.VMEM)
    hbm = pl.BlockSpec(memory_space=pltpu.HBM)
    params = pltpu.CompilerParams(vmem_limit_bytes=VMEM_BYTES)
    own, edge = pl.pallas_call(
        pack_kernel,
        out_shape=(
            jax.ShapeDtypeStruct((TILE_PACK, BLOCKS, LANES), f32),
            jax.ShapeDtypeStruct((2, BLOCKS, LANES), f32),
        ),
        in_specs=[hbm] * 3,
        out_specs=(vmem,) * 2,
        scratch_shapes=[
            pltpu.VMEM(image.shape, f32),
            pltpu.VMEM(coarse.shape, jnp.int32),
            pltpu.SMEM(bounds.shape, jnp.int32),
            pltpu.SemaphoreType.DMA((3,)),
        ],
    )(image, coarse, bounds)
    other = swapped(own, lambda v, r, c: (1 - v, r, c), sizes)
    edge_own = swapped(edge, lambda v, r, c: (v, r, c ^ 1), sizes)
    edge_other = swapped(edge, lambda v, r, c: (1 - v, r, c ^ 1), sizes)
    both, more = pl.pallas_call(
        join_kernel,
        out_shape=(
            jax.ShapeDtypeStruct((2 * TILE_PACK, BLOCKS, LANES), f32),
            jax.ShapeDtypeStruct((2 * TILE_PACK + 3, BLOCKS, LANES), f32),
        ),
        in_specs=[vmem] * 4,
        out_specs=(vmem, vmem),
        compiler_params=params,
    )(own, other, edge_own, edge_other)
    side_b = swapped(more, lambda v, r, c: (v, r, ((c + 1) ^ 1) - 1), sizes)
    side_a = swapped(both, lambda v, r, c: (v, r, c ^ 1), sizes)
    near = pl.pallas_call(
        near_kernel,
        out_shape=jax.ShapeDtypeStruct((3, BLOCKS, LANES), f32),
        in_specs=[vmem],
        out_specs=vmem,
        compiler_params=params,
    )(side_b)
    far = swapped(near, lambda v, r, c: (v, r, c ^ 1), sizes)
    strip = jax.ShapeDtypeStruct((STRIP, 8, LANES), f32)

    def field(n, dtype=f32):
        return jax.ShapeDtypeStruct((n, TALL, WIDE, LANES), dtype)

    limits = jax.ShapeDtypeStruct((2, 3, WIDE, LANES), f32)
    m1, m2, *state = pl.pallas_call(
        assemble_kernel,
        out_shape=(strip, strip, field(4), limits, limits),
        in_specs=[vmem] * 4,
        out_specs=(vmem,) * 5,
        compiler_params=params,
    )(both, side_a, side_b, far)
    g2 = swapped(m2, lambda v, r, c: (v, ((r + 1) ^ 1) - 1, c), sizes)
    g1 = swapped(m1, lambda v, r, c: (v, r ^ 1, c), sizes)
    tables = [pltpu.VMEM((WIDE, LANES), f32), pltpu.VMEM((WIDE, LANES), f32), pltpu.VMEM((WIDE, LANES), jnp.int32)]
    fields = [field(2), field(2, jnp.int32)] + [field(2)] * 13
    more_state = pl.pallas_call(
        lambda *refs: inner_kernel(sizes, *refs),
        out_shape=tuple(fields),
        in_specs=[vmem] * 3,
        out_specs=(vmem,) * 15,
        scratch_shapes=tables,
        compiler_params=params,
        cost_estimate=pl.CostEstimate(flops=20_000_000, bytes_accessed=4_000_000, transcendentals=0),
    )(*state)
    state = [*state, *more_state]
    refine, dual, *_ = pl.pallas_call(
        lambda *refs: outer_kernel(sizes, *refs),
        out_shape=(
            jax.ShapeDtypeStruct((1, OUT_ROWS, BLOCKS * LANES), f32),
            jax.ShapeDtypeStruct((1, 2, OUT_ROWS, BLOCKS * LANES), f32),
            field(4),
            limits,
            limits,
            *fields,
        ),
        in_specs=[vmem] * 22,
        out_specs=(vmem,) * 20,
        input_output_aliases={4 + n: 2 + n for n in range(18)},
        scratch_shapes=[*tables, pltpu.VMEM((OUT_ROWS, BLOCKS, LANES), f32)],
        compiler_params=params,
    )(m1, m2, g1, g2, *state)
    return refine, dual


def solution(mesh):
    sizes = tuple(mesh.shape[axis] for axis in AXES)
    return jax.shard_map(
        lambda *args: on_device(sizes, *args),
        mesh=mesh,
        in_specs=(P("view", "row", "col"), P("view", "row", "col"), P("view", "row", "col", None)),
        out_specs=(P("view", "row", "col"), P("view", None, "row", "col")),
        check_vma=False,
    )
```

time: 48.4 us -> 39.3 us (0.81)
  starting transfers between devices: 22.5 us -> 18.7 us
  Pallas kernels: 12 us -> 8.73 us
  local copies, waits for them, and re-layouts: 2.16 us -> 0.88 us
  waiting for transfers between devices: 10.8 us -> 10.1 us
    ppermute x7 -> x8, starting transfers between devices: 22.5 us -> 18.7 us  [swapped(): return lax.ppermute(block, AXES, route)]
    pallas_call x3 -> x5, Pallas kernels: 11.9 us -> 8.71 us  [the longest x1 4.47 us: on_device(): pl.pallas_call(lambda *refs: outer_kernel(sizes, *refs), out_shape=(jax.S...]
    unnamed x6 -> x2, local copies, waits for them, and re-layouts: 2.16 us -> 0.88 us
    ppermute x7 -> x8, waiting for transfers between devices: 10.8 us -> 10.1 us  [swapped(): return lax.ppermute(block, AXES, route)]
  transfers between devices with their start and end apart: 7 -> 8, of which waited for: 3 -> 5; matrix products, arithmetic and copies ran while one was open for 0% -> 0% of each run, Pallas kernels for 0% -> 7%
where the time goes in v2:
time: 39.3 us; the launch traced here: 39.1 us
  starting transfers between devices  18.7 us (48%)
  waiting for transfers between devices  10.1 us (26%)
  Pallas kernels  8.73 us (22%)
  local copies, waits for them, and re-layouts  0.88 us (2%)
  between operations  0.71 us (2%)
    ppermute x8, starting transfers between devices, swapped(): return lax.ppermute(block, AXES, route)  18.7 us
    ppermute x8, waiting for transfers between devices, swapped(): return lax.ppermute(block, AXES, route)  10.1 us
    pallas_call x1, Pallas kernels, on_device(): pl.pallas_call(lambda *refs: outer_kernel(sizes, *refs), out_shape=(jax.S...  4.47 us
    pallas_call x1, Pallas kernels, on_device(): pl.pallas_call(lambda *refs: inner_kernel(sizes, *refs), out_shape=tuple(...  2.69 us
    pallas_call x1, Pallas kernels, on_device(): pl.pallas_call(pack_kernel, out_shape=(jax.ShapeDtypeStruct((TILE_PACK, B...  1.45 us
    unnamed x2, local copies, waits for them, and re-layouts  0.88 us
  transfers between devices with their start and end apart: 8, of which 5 were waited for; matrix products, arithmetic and copies ran while one was open for 0% of the time, Pallas kernels for 7%

profile of v2, /device:TPU:25, one launch (start us, length us, event | category | flops | bytes accessed | tf_op | source)
XLA Modules:
  0.0 39.1 jit_solution(151821480106825699)
XLA Ops:
  0.6 1.5 %shard_map.50 = (f32[17,8,128]{2,1,0:T(8,128)}, f32[2,8,128]{2,1,0:T(8,128)}) custom-call(f32[1,8,1024]{2,1,0:T(8,128)} %image_hbm.1, s32[1,8,1024]{2,1,0:T(8,128)} %coarse_hbm.1, s32[1,1,1,2]{3,2,1,0:T(1,128)} %bounds_hbm.1), custom_call_target="tpu_custom_call" | custom-call | tf_op jit(solution)/shard_map/pallas_call | solution.py:480
  2.1 2.8 %collective-permute-start = (f32[17,8,128]{2,1,0:T(8,128)}, f32[17,8,128]{2,1,0:T(8,128)S(1)}, u32[]{:S(2)}, u32[]{:S(2)}) collective-permute-start(f32[17,8,128]{2,1,0:T(8,128)} %get-tuple-element.28.own_ref), channel_id=1, source_target_pairs={{0,128},{1,129},{2,130},{3,131},{4,132},{5,133},{6,134},{7,135},{8... | collective-permute-start | bytes 208904 | tf_op jit(solution)/shard_map/ppermute | solution.py:37
  4.9 1.6 %collective-permute-start.2 = (f32[2,8,128]{2,1,0:T(8,128)}, f32[2,8,128]{2,1,0:T(8,128)S(1)}, u32[]{:S(2)}, u32[]{:S(2)}) collective-permute-start(f32[2,8,128]{2,1,0:T(8,128)} %get-tuple-element.29), channel_id=1, source_target_pairs={{0,129},{1,128},{2,131},{3,130},{4,133},{5,132},{6,135},{7,134},{8... | collective-permute-start | bytes 24584 | tf_op jit(solution)/shard_map/ppermute | solution.py:37
  6.5 0.1 collective-permute-start.1
  6.6 3.5 %collective-permute-done.2.edge_other_ref = f32[2,8,128]{2,1,0:T(8,128)S(1)} collective-permute-done((f32[2,8,128]{2,1,0:T(8,128)}, f32[2,8,128]{2,1,0:T(8,128)S(1)}, u32[]{:S(2)}, u32[]{:S(2)}) %collective-permute-start.2) | collective-permute-done | bytes 8224 | tf_op jit(solution)/shard_map/ppermute | solution.py:37
  10.0 0.0 collective-permute-done.1.edge_own_ref
  10.0 0.0 collective-permute-done.other_ref
  10.0 0.0 copy-start
  10.0 0.9 %copy-done = f32[17,8,128]{2,1,0:T(8,128)S(1)} copy-done((f32[17,8,128]{2,1,0:T(8,128)S(1)}, f32[17,8,128]{2,1,0:T(8,128)}, u32[]{:S(2)}) %copy-start) | copy-done | bytes 69656
  11.0 7.7 %collective-permute-start.4 = (f32[37,8,128]{2,1,0:T(8,128)S(1)}, f32[37,8,128]{2,1,0:T(8,128)S(1)}, u32[]{:S(2)}, u32[]{:S(2)}) collective-permute-start(f32[37,8,128]{2,1,0:T(8,128)S(1)} %get-tuple-element.31), channel_id=1, source_target_pairs={{1,2},{2,1},{3,4},{4,3},{5,6},{6,5},{7,8},{8,7},{9,10},{10,9},{11,... | collective-permute-start | bytes 454664 | tf_op jit(solution)/shard_map/ppermute | solution.py:37
  18.6 0.1 collective-permute-start.3
  18.7 2.5 %collective-permute-done.4.b_ref = f32[37,8,128]{2,1,0:T(8,128)S(1)} collective-permute-done((f32[37,8,128]{2,1,0:T(8,128)S(1)}, f32[37,8,128]{2,1,0:T(8,128)S(1)}, u32[]{:S(2)}, u32[]{:S(2)}) %collective-permute-start.4) | collective-permute-done | bytes 151584 | tf_op jit(solution)/shard_map/ppermute | solution.py:37
  21.2 0.1 collective-permute-start.5
  21.3 1.6 %collective-permute-done.3.a_ref = f32[34,8,128]{2,1,0:T(8,128)S(1)} collective-permute-done((f32[34,8,128]{2,1,0:T(8,128)S(1)}, f32[34,8,128]{2,1,0:T(8,128)S(1)}, u32[]{:S(2)}, u32[]{:S(2)}) %collective-permute-start.3) | collective-permute-done | bytes 139296 | tf_op jit(solution)/shard_map/ppermute | solution.py:37
  22.9 0.9 %collective-permute-done.5.far_ref = f32[3,8,128]{2,1,0:T(8,128)S(1)} collective-permute-done((f32[3,8,128]{2,1,0:T(8,128)S(1)}, f32[3,8,128]{2,1,0:T(8,128)S(1)}, u32[]{:S(2)}, u32[]{:S(2)}) %collective-permute-start.5) | collective-permute-done | bytes 12320 | tf_op jit(solution)/shard_map/ppermute | solution.py:37
  23.8 0.1 shard_map.53
  23.9 4.2 %collective-permute-start.6 = (f32[36,8,128]{2,1,0:T(8,128)S(1)}, f32[36,8,128]{2,1,0:T(8,128)S(1)}, u32[]{:S(2)}, u32[]{:S(2)}) collective-permute-start(f32[36,8,128]{2,1,0:T(8,128)S(1)} %get-tuple-element.32.refs_0_), channel_id=1, source_target_pairs={{0,32},{1,33},{2,34},{3,35},{4,36},{5,37},{6,38},{7,39},{8,40},{9,... | collective-permute-start | bytes 442376 | tf_op jit(solution)/shard_map/ppermute | solution.py:37
  28.1 2.1 %collective-permute-start.7 = (f32[36,8,128]{2,1,0:T(8,128)S(1)}, f32[36,8,128]{2,1,0:T(8,128)S(1)}, u32[]{:S(2)}, u32[]{:S(2)}) collective-permute-start(f32[36,8,128]{2,1,0:T(8,128)S(1)} %get-tuple-element.33.refs_1_), channel_id=1, source_target_pairs={{32,64},{33,65},{34,66},{35,67},{36,68},{37,69},{38,70},{39,71},{4... | collective-permute-start | bytes 442376 | tf_op jit(solution)/shard_map/ppermute | solution.py:37
  30.3 2.7 %shard_map.54 = (f32[2,16,40,128]{3,2,1,0:T(8,128)S(1)}, s32[2,16,40,128]{3,2,1,0:T(8,128)S(1)}, f32[2,16,40,128]{3,2,1,0:T(8,128)S(1)}, f32[2,16,40,128]{3,2,1,...) custom-call(f32[4,16,40,128]{3,2,1,0:T(8,128)S(1)} %get-tuple-elemen, ...), custom_call_target="tpu_custom_call" | custom-call | flops 20000000 | bytes 4000000 | tf_op jit(solution)/shard_map/pallas_call | solution.py:535
  33.0 0.0 collective-permute-done.6.refs_2_
  33.0 1.6 %collective-permute-done.7.refs_3_ = f32[36,8,128]{2,1,0:T(8,128)S(1)} collective-permute-done((f32[36,8,128]{2,1,0:T(8,128)S(1)}, f32[36,8,128]{2,1,0:T(8,128)S(1)}, u32[]{:S(2)}, u32[]{:S(2)}) %collective-permute-start.7) | collective-permute-done | bytes 147488 | tf_op jit(solution)/shard_map/ppermute | solution.py:37
  34.6 4.5 %shard_map.55 = (f32[1,8,1024]{2,1,0:T(8,128)}, f32[1,2,8,1024]{3,2,1,0:T(8,128)}, f32[4,16,40,128]{3,2,1,0:T(8,128)S(1)}, f32[2,3,40,128]{3,2,1,0:T(8,128)S(1)}...) custom-call(f32[36,8,128]{2,1,0:T(8,128)S(1)} %get-tuple-element.32., ...), custom_call_target="tpu_custom_call", output_to_operand_aliasing={{2}: (4, {}), {3}: (5, {}), {4}: (6, {}), {5}: (7, {}), {6}... | custom-call | tf_op jit(solution)/shard_map/pallas_call | solution.py:545
  (2 shorter events, 0.0 us)
Async XLA Ops:
  2.1 8.0 %collective-permute-start = (f32[17,8,128]{2,1,0:T(8,128)}, f32[17,8,128]{2,1,0:T(8,128)S(1)}, u32[]{:S(2)}, u32[]{:S(2)}) collective-permute-start(f32[17,8,128]{2,1,0:T(8,128)} %get-tuple-element.28.own_ref), channel_id=1, source_target_pairs={{0,128},{1,129},{2,130},{3,131},{4,132},{5,133},{6,134},{7,135},{8... | collective-permute-start | bytes 208904 | tf_op jit(solution)/shard_map/ppermute | solution.py:37
  4.9 5.1 %collective-permute-start.2 = (f32[2,8,128]{2,1,0:T(8,128)}, f32[2,8,128]{2,1,0:T(8,128)S(1)}, u32[]{:S(2)}, u32[]{:S(2)}) collective-permute-start(f32[2,8,128]{2,1,0:T(8,128)} %get-tuple-element.29), channel_id=1, source_target_pairs={{0,129},{1,128},{2,131},{3,130},{4,133},{5,132},{6,135},{7,134},{8... | collective-permute-start | bytes 24584 | tf_op jit(solution)/shard_map/ppermute | solution.py:37
  6.5 3.5 %collective-permute-start.1 = (f32[2,8,128]{2,1,0:T(8,128)}, f32[2,8,128]{2,1,0:T(8,128)S(1)}, u32[]{:S(2)}, u32[]{:S(2)}) collective-permute-start(f32[2,8,128]{2,1,0:T(8,128)} %get-tuple-element.29), channel_id=1, source_target_pairs={{0,1},{1,0},{2,3},{3,2},{4,5},{5,4},{6,7},{7,6},{8,9},{9,8},{10,11... | collective-permute-start | bytes 24584 | tf_op jit(solution)/shard_map/ppermute | solution.py:37
  10.0 0.9 %copy-start = (f32[17,8,128]{2,1,0:T(8,128)S(1)}, f32[17,8,128]{2,1,0:T(8,128)}, u32[]{:S(2)}) copy-start(f32[17,8,128]{2,1,0:T(8,128)} %get-tuple-element.28.own_ref) | copy-start | bytes 208900
  11.0 10.2 %collective-permute-start.4 = (f32[37,8,128]{2,1,0:T(8,128)S(1)}, f32[37,8,128]{2,1,0:T(8,128)S(1)}, u32[]{:S(2)}, u32[]{:S(2)}) collective-permute-start(f32[37,8,128]{2,1,0:T(8,128)S(1)} %get-tuple-element.31), channel_id=1, source_target_pairs={{1,2},{2,1},{3,4},{4,3},{5,6},{6,5},{7,8},{8,7},{9,10},{10,9},{11,... | collective-permute-start | bytes 454664 | tf_op jit(solution)/shard_map/ppermute | solution.py:37
  18.6 4.3 %collective-permute-start.3 = (f32[34,8,128]{2,1,0:T(8,128)S(1)}, f32[34,8,128]{2,1,0:T(8,128)S(1)}, u32[]{:S(2)}, u32[]{:S(2)}) collective-permute-start(f32[34,8,128]{2,1,0:T(8,128)S(1)} %get-tuple-element.30.both_ref), channel_id=1, source_target_pairs={{0,1},{1,0},{2,3},{3,2},{4,5},{5,4},{6,7},{7,6},{8,9},{9,8},{10,11... | collective-permute-start | bytes 417800 | tf_op jit(solution)/shard_map/ppermute | solution.py:37
  21.2 2.6 %collective-permute-start.5 = (f32[3,8,128]{2,1,0:T(8,128)S(1)}, f32[3,8,128]{2,1,0:T(8,128)S(1)}, u32[]{:S(2)}, u32[]{:S(2)}) collective-permute-start(f32[3,8,128]{2,1,0:T(8,128)S(1)} %shard_map.52), channel_id=1, source_target_pairs={{0,1},{1,0},{2,3},{3,2},{4,5},{5,4},{6,7},{7,6},{8,9},{9,8},{10,11... | collective-permute-start | bytes 36872 | tf_op jit(solution)/shard_map/ppermute | solution.py:37
  23.9 9.0 %collective-permute-start.6 = (f32[36,8,128]{2,1,0:T(8,128)S(1)}, f32[36,8,128]{2,1,0:T(8,128)S(1)}, u32[]{:S(2)}, u32[]{:S(2)}) collective-permute-start(f32[36,8,128]{2,1,0:T(8,128)S(1)} %get-tuple-element.32.refs_0_), channel_id=1, source_target_pairs={{0,32},{1,33},{2,34},{3,35},{4,36},{5,37},{6,38},{7,39},{8,40},{9,... | collective-permute-start | bytes 442376 | tf_op jit(solution)/shard_map/ppermute | solution.py:37
  28.1 6.5 %collective-permute-start.7 = (f32[36,8,128]{2,1,0:T(8,128)S(1)}, f32[36,8,128]{2,1,0:T(8,128)S(1)}, u32[]{:S(2)}, u32[]{:S(2)}) collective-permute-start(f32[36,8,128]{2,1,0:T(8,128)S(1)} %get-tuple-element.33.refs_1_), channel_id=1, source_target_pairs={{32,64},{33,65},{34,66},{35,67},{36,68},{37,69},{38,70},{39,71},{4... | collective-permute-start | bytes 442376 | tf_op jit(solution)/shard_map/ppermute | solution.py:37

commit v3 on v2

--- a/solution.py
+++ b/solution.py
@@ -66,6 +66,15 @@
     out_ref[16] = jnp.where(sub == 0, bounds_ref[0, 0, 0, 0], bounds_ref[0, 0, 0, 1]).astype(jnp.float32)
 
 
+def place_kernel(image_ref, coarse_ref, bounds_ref, out_ref):
+    out_ref[0:8] = to_slabs(image_ref[0])
+    out_ref[8:16] = to_slabs(coarse_ref[0].astype(jnp.float32))
+    limits = bounds_ref[...].astype(jnp.float32)
+    sub = lax.broadcasted_iota(jnp.int32, (BLOCKS, LANES), 0)
+    low, high = (jnp.broadcast_to(limits[:, n : n + 1], (BLOCKS, LANES)) for n in range(2))
+    out_ref[16] = jnp.where(sub == 0, low, high)
+
+
 def join_kernel(own_ref, other_ref, edge_own_ref, edge_other_ref, both_ref, more_ref):
     for ref in (both_ref, more_ref):
         ref[0:TILE_PACK] = own_ref[...]
@@ -95,6 +104,7 @@
     even_row = (lax.axis_index("row") & 1) == 0
     first = lax.axis_index("view") == 0
     zero = jnp.zeros((8, LANES), jnp.float32)
+    m2_ref[STRIP] = zero
     for plane in range(4):
         base = (plane // 2) * TILE_PACK + (plane % 2) * 8
         for y in range(8):
@@ -495,6 +505,14 @@
     other = swapped(own, lambda v, r, c: (1 - v, r, c), sizes)
     edge_own = swapped(edge, lambda v, r, c: (v, r, c ^ 1), sizes)
     edge_other = swapped(edge, lambda v, r, c: (1 - v, r, c ^ 1), sizes)
+    placed = pl.pallas_call(
+        place_kernel,
+        out_shape=jax.ShapeDtypeStruct((TILE_PACK, BLOCKS, LANES), f32),
+        in_specs=[vmem] * 3,
+        out_specs=vmem,
+        compiler_params=params,
+        cost_estimate=pl.CostEstimate(flops=4_000_000, bytes_accessed=200_000, transcendentals=0),
+    )(image, coarse, bounds.reshape(1, 2))
     both, more = pl.pallas_call(
         join_kernel,
         out_shape=(
@@ -504,7 +522,7 @@
         in_specs=[vmem] * 4,
         out_specs=(vmem, vmem),
         compiler_params=params,
-    )(own, other, edge_own, edge_other)
+    )(placed, other, edge_own, edge_other)
     side_b = swapped(more, lambda v, r, c: (v, r, ((c + 1) ^ 1) - 1), sizes)
     side_a = swapped(both, lambda v, r, c: (v, r, c ^ 1), sizes)
     near = pl.pallas_call(
@@ -516,6 +534,7 @@
     )(side_b)
     far = swapped(near, lambda v, r, c: (v, r, c ^ 1), sizes)
     strip = jax.ShapeDtypeStruct((STRIP, 8, LANES), f32)
+    longer = jax.ShapeDtypeStruct((STRIP + 1, 8, LANES), f32)
 
     def field(n, dtype=f32):
         return jax.ShapeDtypeStruct((n, TALL, WIDE, LANES), dtype)
@@ -523,7 +542,7 @@
     limits = jax.ShapeDtypeStruct((2, 3, WIDE, LANES), f32)
     m1, m2, *state = pl.pallas_call(
         assemble_kernel,
-        out_shape=(strip, strip, field(4), limits, limits),
+        out_shape=(strip, longer, field(4), limits, limits),
         in_specs=[vmem] * 4,
         out_specs=(vmem,) * 5,
         compiler_params=params,

time: 39.3 us -> 37 us (0.941)
  waiting for transfers between devices: 10.1 us -> 6.26 us
  local copies, waits for them, and re-layouts: 0.88 us -> 2.17 us
    ppermute x8, waiting for transfers between devices: 10.1 us -> 6.26 us  [swapped(): return lax.ppermute(block, AXES, route)]
    unnamed x2 -> x6, local copies, waits for them, and re-layouts: 0.88 us -> 2.17 us
  transfers between devices with their start and end apart: 8 -> 8, of which waited for: 5 -> 4; matrix products, arithmetic and copies ran while one was open for 0% -> 0% of each run, Pallas kernels for 7% -> 8%
where the time goes in v3:
time: 37 us; the launch traced here: 36.7 us
  starting transfers between devices  18.6 us (50%)
  Pallas kernels  8.86 us (24%)
  waiting for transfers between devices  6.26 us (17%)
  local copies, waits for them, and re-layouts  2.17 us (6%)
  between operations  0.71 us (2%)
    ppermute x8, starting transfers between devices, swapped(): return lax.ppermute(block, AXES, route)  18.6 us
    ppermute x8, waiting for transfers between devices, swapped(): return lax.ppermute(block, AXES, route)  6.26 us
    pallas_call x1, Pallas kernels, on_device(): pl.pallas_call(lambda *refs: outer_kernel(sizes, *refs), out_shape=(jax.S...  4.52 us
    pallas_call x1, Pallas kernels, on_device(): pl.pallas_call(lambda *refs: inner_kernel(sizes, *refs), out_shape=tuple(...  2.7 us
    unnamed x6, local copies, waits for them, and re-layouts  2.17 us
    pallas_call x1, Pallas kernels, on_device(): pl.pallas_call(pack_kernel, out_shape=(jax.ShapeDtypeStruct((TILE_PACK, B...  1.45 us
  transfers between devices with their start and end apart: 8, of which 4 were waited for; matrix products, arithmetic and copies ran while one was open for 0% of the time, Pallas kernels for 8%

profile of v3, /device:TPU:25, one launch (start us, length us, event | category | flops | bytes accessed | tf_op | source)
XLA Modules:
  0.0 36.7 jit_solution(3438920994632187705)
XLA Ops:
  0.6 1.5 %shard_map.51 = (f32[17,8,128]{2,1,0:T(8,128)}, f32[2,8,128]{2,1,0:T(8,128)}) custom-call(f32[1,8,1024]{2,1,0:T(8,128)} %image_hbm.1, s32[1,8,1024]{2,1,0:T(8,128)} %coarse_hbm.1, s32[1,1,1,2]{3,2,1,0:T(1,128)} %bounds_hbm.1), custom_call_target="tpu_custom_call" | custom-call | tf_op jit(solution)/shard_map/pallas_call | solution.py:490
  2.1 2.8 %collective-permute-start = (f32[17,8,128]{2,1,0:T(8,128)}, f32[17,8,128]{2,1,0:T(8,128)S(1)}, u32[]{:S(2)}, u32[]{:S(2)}) collective-permute-start(f32[17,8,128]{2,1,0:T(8,128)} %get-tuple-element.28), channel_id=1, source_target_pairs={{0,128},{1,129},{2,130},{3,131},{4,132},{5,133},{6,134},{7,135},{8... | collective-permute-start | bytes 208904 | tf_op jit(solution)/shard_map/ppermute | solution.py:37
  4.9 1.6 %collective-permute-start.2 = (f32[2,8,128]{2,1,0:T(8,128)}, f32[2,8,128]{2,1,0:T(8,128)S(1)}, u32[]{:S(2)}, u32[]{:S(2)}) collective-permute-start(f32[2,8,128]{2,1,0:T(8,128)} %get-tuple-element.29), channel_id=1, source_target_pairs={{0,129},{1,128},{2,131},{3,130},{4,133},{5,132},{6,135},{7,134},{8... | collective-permute-start | bytes 24584 | tf_op jit(solution)/shard_map/ppermute | solution.py:37
  6.5 0.1 collective-permute-start.1
  6.6 0.0 copy-start
  6.6 0.8 %copy-done = f32[1,8,1024]{2,1,0:T(8,128)S(1)} copy-done((f32[1,8,1024]{2,1,0:T(8,128)S(1)}, f32[1,8,1024]{2,1,0:T(8,128)}, u32[]{:S(2)}) %copy-start) | copy-done | bytes 32792
  7.3 0.0 copy-start.1
  7.3 0.8 %copy-done.1 = s32[1,8,1024]{2,1,0:T(8,128)S(1)} copy-done((s32[1,8,1024]{2,1,0:T(8,128)S(1)}, s32[1,8,1024]{2,1,0:T(8,128)}, u32[]{:S(2)}) %copy-start.1) | copy-done | bytes 32792
  8.1 0.0 copy-start.2
  8.1 0.7 %copy-done.2 = s32[1,1,1,2]{3,2,1,0:T(1,128)S(1)} copy-done((s32[1,1,1,2]{3,2,1,0:T(1,128)S(1)}, s32[1,1,1,2]{3,2,1,0:T(1,128)}, u32[]{:S(2)}) %copy-start.2) | copy-done | bytes 32
  8.7 0.1 shard_map.50.own_ref
  8.8 1.2 %collective-permute-done.2.edge_other_ref = f32[2,8,128]{2,1,0:T(8,128)S(1)} collective-permute-done((f32[2,8,128]{2,1,0:T(8,128)}, f32[2,8,128]{2,1,0:T(8,128)S(1)}, u32[]{:S(2)}, u32[]{:S(2)}) %collective-permute-start.2) | collective-permute-done | bytes 8224 | tf_op jit(solution)/shard_map/ppermute | solution.py:37
  10.0 0.0 collective-permute-done.1.edge_own_ref
  10.0 0.0 collective-permute-done.other_ref
  10.1 7.7 %collective-permute-start.4 = (f32[37,8,128]{2,1,0:T(8,128)S(1)}, f32[37,8,128]{2,1,0:T(8,128)S(1)}, u32[]{:S(2)}, u32[]{:S(2)}) collective-permute-start(f32[37,8,128]{2,1,0:T(8,128)S(1)} %get-tuple-element.31), channel_id=1, source_target_pairs={{1,2},{2,1},{3,4},{4,3},{5,6},{6,5},{7,8},{8,7},{9,10},{10,9},{11,... | collective-permute-start | bytes 454664 | tf_op jit(solution)/shard_map/ppermute | solution.py:37
  17.7 0.1 collective-permute-start.3
  17.8 2.5 %collective-permute-done.4.b_ref = f32[37,8,128]{2,1,0:T(8,128)S(1)} collective-permute-done((f32[37,8,128]{2,1,0:T(8,128)S(1)}, f32[37,8,128]{2,1,0:T(8,128)S(1)}, u32[]{:S(2)}, u32[]{:S(2)}) %collective-permute-start.4) | collective-permute-done | bytes 151584 | tf_op jit(solution)/shard_map/ppermute | solution.py:37
  20.3 0.1 collective-permute-start.5
  20.4 1.6 %collective-permute-done.3.a_ref = f32[34,8,128]{2,1,0:T(8,128)S(1)} collective-permute-done((f32[34,8,128]{2,1,0:T(8,128)S(1)}, f32[34,8,128]{2,1,0:T(8,128)S(1)}, u32[]{:S(2)}, u32[]{:S(2)}) %collective-permute-start.3) | collective-permute-done | bytes 139296 | tf_op jit(solution)/shard_map/ppermute | solution.py:37
  22.0 0.9 %collective-permute-done.5.far_ref = f32[3,8,128]{2,1,0:T(8,128)S(1)} collective-permute-done((f32[3,8,128]{2,1,0:T(8,128)S(1)}, f32[3,8,128]{2,1,0:T(8,128)S(1)}, u32[]{:S(2)}, u32[]{:S(2)}) %collective-permute-start.5) | collective-permute-done | bytes 12320 | tf_op jit(solution)/shard_map/ppermute | solution.py:37
  23.0 0.1 shard_map.54
  23.0 6.2 %collective-permute-start.7 = (f32[37,8,128]{2,1,0:T(8,128)S(1)}, f32[37,8,128]{2,1,0:T(8,128)S(1)}, u32[]{:S(2)}, u32[]{:S(2)}) collective-permute-start(f32[37,8,128]{2,1,0:T(8,128)S(1)} %get-tuple-element.33.refs_1_), channel_id=1, source_target_pairs={{32,64},{33,65},{34,66},{35,67},{36,68},{37,69},{38,70},{39,71},{4... | collective-permute-start | bytes 454664 | tf_op jit(solution)/shard_map/ppermute | solution.py:37
  29.3 0.1 collective-permute-start.6
  29.4 2.7 %shard_map.55 = (f32[2,16,40,128]{3,2,1,0:T(8,128)S(1)}, s32[2,16,40,128]{3,2,1,0:T(8,128)S(1)}, f32[2,16,40,128]{3,2,1,0:T(8,128)S(1)}, f32[2,16,40,128]{3,2,1,...) custom-call(f32[4,16,40,128]{3,2,1,0:T(8,128)S(1)} %get-tuple-elemen, ...), custom_call_target="tpu_custom_call" | custom-call | flops 20000000 | bytes 4000000 | tf_op jit(solution)/shard_map/pallas_call | solution.py:554
  32.1 0.0 collective-permute-done.6.refs_2_
  32.1 0.0 collective-permute-done.7.refs_3_
  32.1 4.5 %shard_map.56 = (f32[1,8,1024]{2,1,0:T(8,128)}, f32[1,2,8,1024]{3,2,1,0:T(8,128)}, f32[4,16,40,128]{3,2,1,0:T(8,128)S(1)}, f32[2,3,40,128]{3,2,1,0:T(8,128)S(1)}...) custom-call(f32[36,8,128]{2,1,0:T(8,128)S(1)} %get-tuple-element.32., ...), custom_call_target="tpu_custom_call", output_to_operand_aliasing={{2}: (4, {}), {3}: (5, {}), {4}: (6, {}), {5}: (7, {}), {6}... | custom-call | tf_op jit(solution)/shard_map/pallas_call | solution.py:564
  (2 shorter events, 0.0 us)
Async XLA Ops:
  2.1 8.0 %collective-permute-start = (f32[17,8,128]{2,1,0:T(8,128)}, f32[17,8,128]{2,1,0:T(8,128)S(1)}, u32[]{:S(2)}, u32[]{:S(2)}) collective-permute-start(f32[17,8,128]{2,1,0:T(8,128)} %get-tuple-element.28), channel_id=1, source_target_pairs={{0,128},{1,129},{2,130},{3,131},{4,132},{5,133},{6,134},{7,135},{8... | collective-permute-start | bytes 208904 | tf_op jit(solution)/shard_map/ppermute | solution.py:37
  4.9 5.1 %collective-permute-start.2 = (f32[2,8,128]{2,1,0:T(8,128)}, f32[2,8,128]{2,1,0:T(8,128)S(1)}, u32[]{:S(2)}, u32[]{:S(2)}) collective-permute-start(f32[2,8,128]{2,1,0:T(8,128)} %get-tuple-element.29), channel_id=1, source_target_pairs={{0,129},{1,128},{2,131},{3,130},{4,133},{5,132},{6,135},{7,134},{8... | collective-permute-start | bytes 24584 | tf_op jit(solution)/shard_map/ppermute | solution.py:37
  6.5 3.5 %collective-permute-start.1 = (f32[2,8,128]{2,1,0:T(8,128)}, f32[2,8,128]{2,1,0:T(8,128)S(1)}, u32[]{:S(2)}, u32[]{:S(2)}) collective-permute-start(f32[2,8,128]{2,1,0:T(8,128)} %get-tuple-element.29), channel_id=1, source_target_pairs={{0,1},{1,0},{2,3},{3,2},{4,5},{5,4},{6,7},{7,6},{8,9},{9,8},{10,11... | collective-permute-start | bytes 24584 | tf_op jit(solution)/shard_map/ppermute | solution.py:37
  6.6 0.8 %copy-start = (f32[1,8,1024]{2,1,0:T(8,128)S(1)}, f32[1,8,1024]{2,1,0:T(8,128)}, u32[]{:S(2)}) copy-start(f32[1,8,1024]{2,1,0:T(8,128)} %image_hbm.1) | copy-start | bytes 98308
  7.3 0.8 %copy-start.1 = (s32[1,8,1024]{2,1,0:T(8,128)S(1)}, s32[1,8,1024]{2,1,0:T(8,128)}, u32[]{:S(2)}) copy-start(s32[1,8,1024]{2,1,0:T(8,128)} %coarse_hbm.1) | copy-start | bytes 98308
  8.1 0.7 %copy-start.2 = (s32[1,1,1,2]{3,2,1,0:T(1,128)S(1)}, s32[1,1,1,2]{3,2,1,0:T(1,128)}, u32[]{:S(2)}) copy-start(s32[1,1,1,2]{3,2,1,0:T(1,128)} %bounds_hbm.1) | copy-start | bytes 28
  10.1 10.2 %collective-permute-start.4 = (f32[37,8,128]{2,1,0:T(8,128)S(1)}, f32[37,8,128]{2,1,0:T(8,128)S(1)}, u32[]{:S(2)}, u32[]{:S(2)}) collective-permute-start(f32[37,8,128]{2,1,0:T(8,128)S(1)} %get-tuple-element.31), channel_id=1, source_target_pairs={{1,2},{2,1},{3,4},{4,3},{5,6},{6,5},{7,8},{8,7},{9,10},{10,9},{11,... | collective-permute-start | bytes 454664 | tf_op jit(solution)/shard_map/ppermute | solution.py:37
  17.7 4.3 %collective-permute-start.3 = (f32[34,8,128]{2,1,0:T(8,128)S(1)}, f32[34,8,128]{2,1,0:T(8,128)S(1)}, u32[]{:S(2)}, u32[]{:S(2)}) collective-permute-start(f32[34,8,128]{2,1,0:T(8,128)S(1)} %get-tuple-element.30.both_ref), channel_id=1, source_target_pairs={{0,1},{1,0},{2,3},{3,2},{4,5},{5,4},{6,7},{7,6},{8,9},{9,8},{10,11... | collective-permute-start | bytes 417800 | tf_op jit(solution)/shard_map/ppermute | solution.py:37
  20.3 2.6 %collective-permute-start.5 = (f32[3,8,128]{2,1,0:T(8,128)S(1)}, f32[3,8,128]{2,1,0:T(8,128)S(1)}, u32[]{:S(2)}, u32[]{:S(2)}) collective-permute-start(f32[3,8,128]{2,1,0:T(8,128)S(1)} %shard_map.53), channel_id=1, source_target_pairs={{0,1},{1,0},{2,3},{3,2},{4,5},{5,4},{6,7},{7,6},{8,9},{9,8},{10,11... | collective-permute-start | bytes 36872 | tf_op jit(solution)/shard_map/ppermute | solution.py:37
  23.0 9.1 %collective-permute-start.7 = (f32[37,8,128]{2,1,0:T(8,128)S(1)}, f32[37,8,128]{2,1,0:T(8,128)S(1)}, u32[]{:S(2)}, u32[]{:S(2)}) collective-permute-start(f32[37,8,128]{2,1,0:T(8,128)S(1)} %get-tuple-element.33.refs_1_), channel_id=1, source_target_pairs={{32,64},{33,65},{34,66},{35,67},{36,68},{37,69},{38,70},{39,71},{4... | collective-permute-start | bytes 454664 | tf_op jit(solution)/shard_map/ppermute | solution.py:37
  29.3 2.8 %collective-permute-start.6 = (f32[36,8,128]{2,1,0:T(8,128)S(1)}, f32[36,8,128]{2,1,0:T(8,128)S(1)}, u32[]{:S(2)}, u32[]{:S(2)}) collective-permute-start(f32[36,8,128]{2,1,0:T(8,128)S(1)} %get-tuple-element.32.refs_0_), channel_id=1, source_target_pairs={{0,32},{1,33},{2,34},{3,35},{4,36},{5,37},{6,38},{7,39},{8,40},{9,... | collective-permute-start | bytes 442376 | tf_op jit(solution)/shard_map/ppermute | solution.py:37

commit v4 on v2

--- a/solution.py
+++ b/solution.py
@@ -42,7 +42,7 @@
     return jnp.transpose(parts, (1, 0, 2))
 
 
-def pack_kernel(image_hbm, coarse_hbm, bounds_hbm, out_ref, edge_ref, image_ref, coarse_ref, bounds_ref, sems):
+def pack_kernel(image_hbm, coarse_hbm, bounds_hbm, out_ref, longer_ref, image_ref, coarse_ref, bounds_ref, sems):
     copies = [
         pltpu.make_async_copy(source, target, sems.at[n])
         for n, (source, target) in enumerate(
@@ -51,34 +51,45 @@
     ]
     for copy in copies:
         copy.start()
-    odd = (lax.axis_index("col") & 1) == 1
-    last = (BLOCKS - 1) * LANES
     copies[0].wait()
     image = image_ref[0]
-    out_ref[0:8] = to_slabs(image)
-    edge_ref[0] = jnp.where(odd, image[:, :LANES], image[:, last:])
+    slabs = to_slabs(image)
+    out_ref[0:8] = slabs
+    longer_ref[0:8] = slabs
     copies[1].wait()
     coarse = coarse_ref[0].astype(jnp.float32)
-    out_ref[8:16] = to_slabs(coarse)
-    edge_ref[1] = jnp.where(odd, coarse[:, :LANES], coarse[:, last:])
+    slabs = to_slabs(coarse)
+    out_ref[8:16] = slabs
+    longer_ref[8:16] = slabs
     copies[2].wait()
     sub = lax.broadcasted_iota(jnp.int32, (BLOCKS, LANES), 0)
-    out_ref[16] = jnp.where(sub == 0, bounds_ref[0, 0, 0, 0], bounds_ref[0, 0, 0, 1]).astype(jnp.float32)
-
-
-def join_kernel(own_ref, other_ref, edge_own_ref, edge_other_ref, both_ref, more_ref):
-    for ref in (both_ref, more_ref):
-        ref[0:TILE_PACK] = own_ref[...]
-        ref[TILE_PACK : 2 * TILE_PACK] = other_ref[...]
-    more_ref[2 * TILE_PACK] = edge_own_ref[0]
-    more_ref[2 * TILE_PACK + 1 :] = edge_other_ref[...]
-
-
-def near_kernel(b_ref, out_ref):
+    limits = jnp.where(sub == 0, bounds_ref[0, 0, 0, 0], bounds_ref[0, 0, 0, 1]).astype(jnp.float32)
+    out_ref[16] = limits
+    longer_ref[16] = limits
+    longer_ref[17] = jnp.zeros((BLOCKS, LANES), jnp.float32)
+
+
+def place_kernel(own_ref, out_ref):
+    out_ref[...] = own_ref[...]
+
+
+def join_kernel(own_ref, other_ref, a_ref, more_ref):
+    odd = (lax.axis_index("col") & 1) == 1
+    more_ref[0:TILE_PACK] = own_ref[...]
+    more_ref[TILE_PACK : 2 * TILE_PACK] = other_ref[0:TILE_PACK]
+    for n in range(2):
+        for y in range(8):
+            at = 8 * n + y
+            more_ref[2 * TILE_PACK + n, y : y + 1, :] = jnp.where(odd, a_ref[at, 7:8], a_ref[at, 0:1])
+
+
+def near_kernel(b_ref, out_ref, thin_ref):
     odd = (lax.axis_index("col") & 1) == 1
     for n, base in enumerate((0, TILE_PACK, TILE_PACK + 8)):
         for y in range(8):
             out_ref[n, y : y + 1, :] = jnp.where(odd, b_ref[base + y, 0:1], b_ref[base + y, 7:8])
+    for n in range(2):
+        thin_ref[n] = b_ref[2 * TILE_PACK + n]
 
 
 def halo_slabs(view):
@@ -90,31 +101,35 @@
     return slabs
 
 
-def assemble_kernel(both_ref, a_ref, b_ref, far_ref, m1_ref, m2_ref, F, LO, HI):
+def assemble_kernel(both_ref, a_own_ref, a_other_ref, b_ref, far_ref, cross_ref, m1_ref, m2_ref, F, LO, HI):
     odd = (lax.axis_index("col") & 1) == 1
     even_row = (lax.axis_index("row") & 1) == 0
     first = lax.axis_index("view") == 0
     zero = jnp.zeros((8, LANES), jnp.float32)
+    m2_ref[STRIP] = zero
     for plane in range(4):
         base = (plane // 2) * TILE_PACK + (plane % 2) * 8
+        a_ref = (a_own_ref, a_other_ref)[plane // 2]
         for y in range(8):
-            at = base + y
+            at, a_tile = base + y, a_ref[(plane % 2) * 8 + y]
             F[plane, y + 4, 0:8] = zero
-            F[plane, y + 4, 8:16] = jnp.where(odd, a_ref[at], b_ref[at])
+            F[plane, y + 4, 8:16] = jnp.where(odd, a_tile, b_ref[at])
             F[plane, y + 4, 16:24] = both_ref[at]
-            F[plane, y + 4, 24:32] = jnp.where(odd, b_ref[at], a_ref[at])
+            F[plane, y + 4, 24:32] = jnp.where(odd, b_ref[at], a_tile)
             F[plane, y + 4, 32:40] = zero
-    far, near = far_ref[...], b_ref[2 * TILE_PACK :]
-    left, right = jnp.where(odd, far, near), jnp.where(odd, near, far)
-    cross = jnp.where(first, left, right)
+    far = far_ref[...]
+    near = (b_ref[2 * TILE_PACK], cross_ref[0], cross_ref[1])
+    left = [jnp.where(odd, far[n], near[n]) for n in range(3)]
+    right = [jnp.where(odd, near[n], far[n]) for n in range(3)]
+    cross = [jnp.where(first, one, two) for one, two in zip(left, right, strict=True)]
     low, high = SHIFT - 9, SHIFT + 16
     for y in range(8):
         row = slice(y, y + 1)
-        F[0, y + 4, low : low + 1] = left[0, row]
-        F[0, y + 4, high : high + 1] = right[0, row]
+        F[0, y + 4, low : low + 1] = left[0][row]
+        F[0, y + 4, high : high + 1] = right[0][row]
         for plane in (2, 3):
-            F[plane, y + 4, low : low + 1] = cross[plane - 1, row]
-            F[plane, y + 4, high : high + 1] = cross[plane - 1, row]
+            F[plane, y + 4, low : low + 1] = cross[plane - 1][row]
+            F[plane, y + 4, high : high + 1] = cross[plane - 1][row]
 
     def put(at, top, bottom):
         m1_ref[at] = jnp.where(even_row, bottom, top)
@@ -130,8 +145,9 @@
         put(at, *pair)
     for w in range(2):
         s = w * TILE_PACK + 16
-        tiles = (jnp.where(odd, a_ref[s], b_ref[s]), both_ref[s], jnp.where(odd, b_ref[s], a_ref[s]))
-        thin = [jnp.concatenate([cross[1, y : y + 1], cross[2, y : y + 1]], axis=0) for y in (0, 7)]
+        a_tile = (a_own_ref, a_other_ref)[w][16]
+        tiles = (jnp.where(odd, a_tile, b_ref[s]), both_ref[s], jnp.where(odd, b_ref[s], a_tile))
+        thin = [jnp.concatenate([cross[1][y : y + 1], cross[2][y : y + 1]], axis=0) for y in (0, 7)]
         ends = [jnp.concatenate([t[0:2] for t in tiles] + [t], axis=0) for t in thin]
         put(STRIP - 2 + w, *ends)
         spread_bounds(LO, HI, w, 1, ends[0])
@@ -326,19 +342,17 @@
                     slopes(0, y, (-8, 0, 8), stores)
                     slopes(1, y, slope_other, stores)
 
-            def body(y, carry, k=k, dual_row=dual_row, last=last):
-                stores = []
-                for w, plan in enumerate((own, other)):
-                    primal(k, w, y, signs[w], plan[k][1], stores)
-                dual_row(jnp.minimum(y + 1, last - 1), stores)
-                flush(stores)
-                return carry
-
             for y in (first - 1, first):
                 stores = []
                 dual_row(y, stores)
                 flush(stores)
-            lax.fori_loop(first, last, body, 0)
+            for y in range(first, last):
+                stores = []
+                for w, plan in enumerate((own, other)):
+                    primal(k, w, y, signs[w], plan[k][1], stores)
+                if y + 1 < last:
+                    dual_row(y + 1, stores)
+                flush(stores)
         stores = []
         slopes(0, 7, (-8, 0, 8), stores)
         slopes(1, 7, slope_other, stores)
@@ -386,13 +400,10 @@
         flush(stores)
 
         def pairs(step):
-            def body(i, carry):
+            for i in range(2):
                 stores = []
                 step(i, stores)
                 flush(stores)
-                return carry
-
-            lax.fori_loop(0, 2, body, 0)
 
         def block(step):
             stores = []
@@ -434,22 +445,19 @@
             pairs(primal_loop)
             block(primal_block)
 
-        def last_dual(i, carry):
-            stores = []
+        def last_dual(i, stores):
             for y in (3 * i - 1, 3 * i, 3 * i + 1):
                 dual(3, 0, y, own[3][0], stores)
-            flush(stores)
-            return carry
-
-        def last_primal(i, carry):
-            stores = []
+
+        def last_primal(i, stores):
             for y in (4 * i, 4 * i + 1, 4 * i + 2, 4 * i + 3):
                 primal(3, 0, y, signs[0], own[3][1], stores)
-            flush(stores)
-            return carry
-
-        lax.fori_loop(0, 3, last_dual, 0)
-        lax.fori_loop(0, 2, last_primal, 0)
+
+        for step, count in ((last_dual, 3), (last_primal, 2)):
+            for i in range(count):
+                stores = []
+                step(i, stores)
+                flush(stores)
 
     by_view(run)
 
@@ -477,14 +485,12 @@
     vmem = pl.BlockSpec(memory_space=pltpu.VMEM)
     hbm = pl.BlockSpec(memory_space=pltpu.HBM)
     params = pltpu.CompilerParams(vmem_limit_bytes=VMEM_BYTES)
-    own, edge = pl.pallas_call(
+    tile = jax.ShapeDtypeStruct((TILE_PACK, BLOCKS, LANES), f32)
+    own, longer = pl.pallas_call(
         pack_kernel,
-        out_shape=(
-            jax.ShapeDtypeStruct((TILE_PACK, BLOCKS, LANES), f32),
-            jax.ShapeDtypeStruct((2, BLOCKS, LANES), f32),
-        ),
+        out_shape=(tile, jax.ShapeDtypeStruct((TILE_PACK + 1, BLOCKS, LANES), f32)),
         in_specs=[hbm] * 3,
-        out_specs=(vmem,) * 2,
+        out_specs=(vmem, vmem),
         scratch_shapes=[
             pltpu.VMEM(image.shape, f32),
             pltpu.VMEM(coarse.shape, jnp.int32),
@@ -492,30 +498,46 @@
             pltpu.SemaphoreType.DMA((3,)),
         ],
     )(image, coarse, bounds)
-    other = swapped(own, lambda v, r, c: (1 - v, r, c), sizes)
-    edge_own = swapped(edge, lambda v, r, c: (v, r, c ^ 1), sizes)
-    edge_other = swapped(edge, lambda v, r, c: (1 - v, r, c ^ 1), sizes)
-    both, more = pl.pallas_call(
-        join_kernel,
-        out_shape=(
-            jax.ShapeDtypeStruct((2 * TILE_PACK, BLOCKS, LANES), f32),
-            jax.ShapeDtypeStruct((2 * TILE_PACK + 3, BLOCKS, LANES), f32),
-        ),
-        in_specs=[vmem] * 4,
-        out_specs=(vmem, vmem),
-        compiler_params=params,
-    )(own, other, edge_own, edge_other)
-    side_b = swapped(more, lambda v, r, c: (v, r, ((c + 1) ^ 1) - 1), sizes)
-    side_a = swapped(both, lambda v, r, c: (v, r, c ^ 1), sizes)
-    near = pl.pallas_call(
-        near_kernel,
-        out_shape=jax.ShapeDtypeStruct((3, BLOCKS, LANES), f32),
+
+    def in_pair(v, r, c):
+        return v, r, c ^ 1
+
+    def across(v, r, c):
+        return 1 - v, r, c
+
+    other = swapped(longer, across, sizes)
+    a_own = swapped(own, in_pair, sizes)
+    placed = pl.pallas_call(
+        place_kernel,
+        out_shape=tile,
         in_specs=[vmem],
         out_specs=vmem,
         compiler_params=params,
+        cost_estimate=pl.CostEstimate(flops=4_000_000, bytes_accessed=200_000, transcendentals=0),
+    )(own)
+    more = pl.pallas_call(
+        join_kernel,
+        out_shape=jax.ShapeDtypeStruct((2 * TILE_PACK + 2, BLOCKS, LANES), f32),
+        in_specs=[vmem] * 3,
+        out_specs=vmem,
+        compiler_params=params,
+    )(placed, other, a_own)
+    side_b = swapped(more, lambda v, r, c: (v, r, ((c + 1) ^ 1) - 1), sizes)
+    a_other = swapped(other, in_pair, sizes)
+    near, thin = pl.pallas_call(
+        near_kernel,
+        out_shape=(
+            jax.ShapeDtypeStruct((3, BLOCKS, LANES), f32),
+            jax.ShapeDtypeStruct((2, BLOCKS, LANES), f32),
+        ),
+        in_specs=[vmem],
+        out_specs=(vmem, vmem),
+        compiler_params=params,
     )(side_b)
-    far = swapped(near, lambda v, r, c: (v, r, c ^ 1), sizes)
+    cross = swapped(thin, across, sizes)
+    far = swapped(near, in_pair, sizes)
     strip = jax.ShapeDtypeStruct((STRIP, 8, LANES), f32)
+    strip_longer = jax.ShapeDtypeStruct((STRIP + 1, 8, LANES), f32)
 
     def field(n, dtype=f32):
         return jax.ShapeDtypeStruct((n, TALL, WIDE, LANES), dtype)
@@ -523,11 +545,11 @@
     limits = jax.ShapeDtypeStruct((2, 3, WIDE, LANES), f32)
     m1, m2, *state = pl.pallas_call(
         assemble_kernel,
-        out_shape=(strip, strip, field(4), limits, limits),
-        in_specs=[vmem] * 4,
+        out_shape=(strip, strip_longer, field(4), limits, limits),
+        in_specs=[vmem] * 6,
         out_specs=(vmem,) * 5,
         compiler_params=params,
-    )(both, side_a, side_b, far)
+    )(more, a_own, a_other, side_b, far, cross)
     g2 = swapped(m2, lambda v, r, c: (v, ((r + 1) ^ 1) - 1, c), sizes)
     g1 = swapped(m1, lambda v, r, c: (v, r ^ 1, c), sizes)
     tables = [pltpu.VMEM((WIDE, LANES), f32), pltpu.VMEM((WIDE, LANES), f32), pltpu.VMEM((WIDE, LANES), jnp.int32)]

time: 39.3 us -> 35 us (0.89)
  waiting for transfers between devices: 10.1 us -> 6.81 us
  Pallas kernels: 8.73 us -> 6.53 us
  starting transfers between devices: 18.7 us -> 19.8 us
    ppermute x8, waiting for transfers between devices: 10.1 us -> 6.81 us  [swapped(): return lax.ppermute(block, AXES, route)]
    pallas_call x1, Pallas kernels: 4.47 us -> 2.83 us  [on_device(): pl.pallas_call(lambda *refs: outer_kernel(sizes, *refs), out_shape=(jax.S...]
    ppermute x8, starting transfers between devices: 18.7 us -> 19.8 us  [swapped(): return lax.ppermute(block, AXES, route)]
    pallas_call x1, Pallas kernels: 2.69 us -> 2.09 us  [on_device(): pl.pallas_call(lambda *refs: inner_kernel(sizes, *refs), out_shape=tuple(...]
    pallas_call x4 -> x5, Pallas kernels: 1.56 us -> 1.61 us  [the longest x1 1.49 us: on_device(): pl.pallas_call(pack_kernel, out_shape=(tile, jax.ShapeDtypeStruct((TILE_P...]
  transfers between devices with their start and end apart: 8 -> 8, of which waited for: 5 -> 4; matrix products, arithmetic and copies ran while one was open for 0% -> 0% of each run, Pallas kernels for 7% -> 6%
where the time goes in v4:
time: 35 us; the launch traced here: 34.8 us
  starting transfers between devices  19.8 us (57%)
  waiting for transfers between devices  6.81 us (19%)
  Pallas kernels  6.53 us (19%)
  local copies, waits for them, and re-layouts  0.92 us (3%)
  between operations  0.71 us (2%)
    ppermute x8, starting transfers between devices, swapped(): return lax.ppermute(block, AXES, route)  19.8 us
    ppermute x8, waiting for transfers between devices, swapped(): return lax.ppermute(block, AXES, route)  6.81 us
    pallas_call x1, Pallas kernels, on_device(): pl.pallas_call(lambda *refs: outer_kernel(sizes, *refs), out_shape=(jax.S...  2.83 us
    pallas_call x1, Pallas kernels, on_device(): pl.pallas_call(lambda *refs: inner_kernel(sizes, *refs), out_shape=tuple(...  2.09 us
    pallas_call x1, Pallas kernels, on_device(): pl.pallas_call(pack_kernel, out_shape=(tile, jax.ShapeDtypeStruct((TILE_P...  1.49 us
    unnamed x2, local copies, waits for them, and re-layouts  0.92 us
  transfers between devices with their start and end apart: 8, of which 4 were waited for; matrix products, arithmetic and copies ran while one was open for 0% of the time, Pallas kernels for 6%

profile of v4, /device:TPU:25, one launch (start us, length us, event | category | flops | bytes accessed | tf_op | source)
XLA Modules:
  0.0 34.8 jit_solution(5197267569313894580)
XLA Ops:
  0.6 1.5 %shard_map.50 = (f32[17,8,128]{2,1,0:T(8,128)}, f32[18,8,128]{2,1,0:T(8,128)}) custom-call(f32[1,8,1024]{2,1,0:T(8,128)} %image_hbm.1, s32[1,8,1024]{2,1,0:T(8,128)} %coarse_hbm.1, s32[1,1,1,2]{3,2,1,0:T(1,128)} %bounds_hbm.1), custom_call_target="tpu_custom_call" | custom-call | tf_op jit(solution)/shard_map/pallas_call | solution.py:489
  2.1 2.8 %collective-permute-start = (f32[18,8,128]{2,1,0:T(8,128)}, f32[18,8,128]{2,1,0:T(8,128)S(1)}, u32[]{:S(2)}, u32[]{:S(2)}) collective-permute-start(f32[18,8,128]{2,1,0:T(8,128)} %get-tuple-element.29), channel_id=1, source_target_pairs={{0,128},{1,129},{2,130},{3,131},{4,132},{5,133},{6,134},{7,135},{8... | collective-permute-start | bytes 221192 | tf_op jit(solution)/shard_map/ppermute | solution.py:37
  5.0 1.6 %collective-permute-start.1 = (f32[17,8,128]{2,1,0:T(8,128)}, f32[17,8,128]{2,1,0:T(8,128)S(1)}, u32[]{:S(2)}, u32[]{:S(2)}) collective-permute-start(f32[17,8,128]{2,1,0:T(8,128)} %get-tuple-element.28.own_ref), channel_id=1, source_target_pairs={{0,1},{1,0},{2,3},{3,2},{4,5},{5,4},{6,7},{7,6},{8,9},{9,8},{10,11... | collective-permute-start | bytes 208904 | tf_op jit(solution)/shard_map/ppermute | solution.py:37
  6.6 0.0 copy-start
  6.6 0.9 %copy-done = f32[17,8,128]{2,1,0:T(8,128)S(1)} copy-done((f32[17,8,128]{2,1,0:T(8,128)S(1)}, f32[17,8,128]{2,1,0:T(8,128)}, u32[]{:S(2)}) %copy-start) | copy-done | bytes 69656
  7.5 1.0 %collective-permute-done.1.a_ref.a_own_ref = f32[17,8,128]{2,1,0:T(8,128)S(1)} collective-permute-done((f32[17,8,128]{2,1,0:T(8,128)}, f32[17,8,128]{2,1,0:T(8,128)S(1)}, u32[]{:S(2)}, u32[]{:S(2)}) %collective-permute-start.1) | collective-permute-done | bytes 69664 | tf_op jit(solution)/shard_map/ppermute | solution.py:37
  8.6 0.0 collective-permute-done.other_ref
  8.6 7.7 %collective-permute-start.3 = (f32[36,8,128]{2,1,0:T(8,128)S(1)}, f32[36,8,128]{2,1,0:T(8,128)S(1)}, u32[]{:S(2)}, u32[]{:S(2)}) collective-permute-start(f32[36,8,128]{2,1,0:T(8,128)S(1)} %shard_map.52.both_ref), channel_id=1, source_target_pairs={{1,2},{2,1},{3,4},{4,3},{5,6},{6,5},{7,8},{8,7},{9,10},{10,9},{11,... | collective-permute-start | bytes 442376 | tf_op jit(solution)/shard_map/ppermute | solution.py:37
  16.3 0.1 collective-permute-start.2
  16.4 2.4 %collective-permute-done.3.b_ref = f32[36,8,128]{2,1,0:T(8,128)S(1)} collective-permute-done((f32[36,8,128]{2,1,0:T(8,128)S(1)}, f32[36,8,128]{2,1,0:T(8,128)S(1)}, u32[]{:S(2)}, u32[]{:S(2)}) %collective-permute-start.3) | collective-permute-done | bytes 147488 | tf_op jit(solution)/shard_map/ppermute | solution.py:37
  18.8 0.1 collective-permute-start.4
  18.9 1.4 %collective-permute-start.5 = (f32[2,8,128]{2,1,0:T(8,128)S(1)}, f32[2,8,128]{2,1,0:T(8,128)S(1)}, u32[]{:S(2)}, u32[]{:S(2)}) collective-permute-start(f32[2,8,128]{2,1,0:T(8,128)S(1)} %get-tuple-element.31), channel_id=1, source_target_pairs={{0,128},{1,129},{2,130},{3,131},{4,132},{5,133},{6,134},{7,135},{8... | collective-permute-start | bytes 24584 | tf_op jit(solution)/shard_map/ppermute | solution.py:37
  20.3 0.0 collective-permute-done.2.a_other_ref
  20.3 2.7 %collective-permute-done.5.cross_ref = f32[2,8,128]{2,1,0:T(8,128)S(1)} collective-permute-done((f32[2,8,128]{2,1,0:T(8,128)S(1)}, f32[2,8,128]{2,1,0:T(8,128)S(1)}, u32[]{:S(2)}, u32[]{:S(2)}) %collective-permute-start.5) | collective-permute-done | bytes 8224 | tf_op jit(solution)/shard_map/ppermute | solution.py:37
  23.0 0.0 collective-permute-done.4.far_ref
  23.0 0.1 shard_map.54
  23.1 6.0 %collective-permute-start.7 = (f32[37,8,128]{2,1,0:T(8,128)S(1)}, f32[37,8,128]{2,1,0:T(8,128)S(1)}, u32[]{:S(2)}, u32[]{:S(2)}) collective-permute-start(f32[37,8,128]{2,1,0:T(8,128)S(1)} %get-tuple-element.33.refs_1_), channel_id=1, source_target_pairs={{32,64},{33,65},{34,66},{35,67},{36,68},{37,69},{38,70},{39,71},{4... | collective-permute-start | bytes 454664 | tf_op jit(solution)/shard_map/ppermute | solution.py:37
  29.1 0.1 collective-permute-start.6
  29.2 2.1 %shard_map.55 = (f32[2,16,40,128]{3,2,1,0:T(8,128)S(1)}, s32[2,16,40,128]{3,2,1,0:T(8,128)S(1)}, f32[2,16,40,128]{3,2,1,0:T(8,128)S(1)}, f32[2,16,40,128]{3,2,1,...) custom-call(f32[4,16,40,128]{3,2,1,0:T(8,128)S(1)} %get-tuple-elemen, ...), custom_call_target="tpu_custom_call" | custom-call | flops 20000000 | bytes 4000000 | tf_op jit(solution)/shard_map/pallas_call | solution.py:557
  31.3 0.0 collective-permute-done.6.refs_2_
  31.3 0.6 %collective-permute-done.7.refs_3_ = f32[37,8,128]{2,1,0:T(8,128)S(1)} collective-permute-done((f32[37,8,128]{2,1,0:T(8,128)S(1)}, f32[37,8,128]{2,1,0:T(8,128)S(1)}, u32[]{:S(2)}, u32[]{:S(2)}) %collective-permute-start.7) | collective-permute-done | bytes 151584 | tf_op jit(solution)/shard_map/ppermute | solution.py:37
  31.9 2.8 %shard_map.56 = (f32[1,8,1024]{2,1,0:T(8,128)}, f32[1,2,8,1024]{3,2,1,0:T(8,128)}, f32[4,16,40,128]{3,2,1,0:T(8,128)S(1)}, f32[2,3,40,128]{3,2,1,0:T(8,128)S(1)}...) custom-call(f32[36,8,128]{2,1,0:T(8,128)S(1)} %get-tuple-element.32., ...), custom_call_target="tpu_custom_call", output_to_operand_aliasing={{2}: (4, {}), {3}: (5, {}), {4}: (6, {}), {5}: (7, {}), {6}... | custom-call | tf_op jit(solution)/shard_map/pallas_call | solution.py:567
  (3 shorter events, 0.0 us)
Async XLA Ops:
  2.1 6.4 %collective-permute-start = (f32[18,8,128]{2,1,0:T(8,128)}, f32[18,8,128]{2,1,0:T(8,128)S(1)}, u32[]{:S(2)}, u32[]{:S(2)}) collective-permute-start(f32[18,8,128]{2,1,0:T(8,128)} %get-tuple-element.29), channel_id=1, source_target_pairs={{0,128},{1,129},{2,130},{3,131},{4,132},{5,133},{6,134},{7,135},{8... | collective-permute-start | bytes 221192 | tf_op jit(solution)/shard_map/ppermute | solution.py:37
  5.0 3.6 %collective-permute-start.1 = (f32[17,8,128]{2,1,0:T(8,128)}, f32[17,8,128]{2,1,0:T(8,128)S(1)}, u32[]{:S(2)}, u32[]{:S(2)}) collective-permute-start(f32[17,8,128]{2,1,0:T(8,128)} %get-tuple-element.28.own_ref), channel_id=1, source_target_pairs={{0,1},{1,0},{2,3},{3,2},{4,5},{5,4},{6,7},{7,6},{8,9},{9,8},{10,11... | collective-permute-start | bytes 208904 | tf_op jit(solution)/shard_map/ppermute | solution.py:37
  6.6 0.9 %copy-start = (f32[17,8,128]{2,1,0:T(8,128)S(1)}, f32[17,8,128]{2,1,0:T(8,128)}, u32[]{:S(2)}) copy-start(f32[17,8,128]{2,1,0:T(8,128)} %get-tuple-element.28.own_ref) | copy-start | bytes 208900
  8.6 10.2 %collective-permute-start.3 = (f32[36,8,128]{2,1,0:T(8,128)S(1)}, f32[36,8,128]{2,1,0:T(8,128)S(1)}, u32[]{:S(2)}, u32[]{:S(2)}) collective-permute-start(f32[36,8,128]{2,1,0:T(8,128)S(1)} %shard_map.52.both_ref), channel_id=1, source_target_pairs={{1,2},{2,1},{3,4},{4,3},{5,6},{6,5},{7,8},{8,7},{9,10},{10,9},{11,... | collective-permute-start | bytes 442376 | tf_op jit(solution)/shard_map/ppermute | solution.py:37
  16.3 4.0 %collective-permute-start.2 = (f32[18,8,128]{2,1,0:T(8,128)S(1)}, f32[18,8,128]{2,1,0:T(8,128)S(1)}, u32[]{:S(2)}, u32[]{:S(2)}) collective-permute-start(f32[18,8,128]{2,1,0:T(8,128)S(1)} %collective-permute-done.other_ref), channel_id=1, source_target_pairs={{0,1},{1,0},{2,3},{3,2},{4,5},{5,4},{6,7},{7,6},{8,9},{9,8},{10,11... | collective-permute-start | bytes 221192 | tf_op jit(solution)/shard_map/ppermute | solution.py:37
  18.8 4.2 %collective-permute-start.4 = (f32[3,8,128]{2,1,0:T(8,128)S(1)}, f32[3,8,128]{2,1,0:T(8,128)S(1)}, u32[]{:S(2)}, u32[]{:S(2)}) collective-permute-start(f32[3,8,128]{2,1,0:T(8,128)S(1)} %get-tuple-element.30), channel_id=1, source_target_pairs={{0,1},{1,0},{2,3},{3,2},{4,5},{5,4},{6,7},{7,6},{8,9},{9,8},{10,11... | collective-permute-start | bytes 36872 | tf_op jit(solution)/shard_map/ppermute | solution.py:37
  18.9 4.1 %collective-permute-start.5 = (f32[2,8,128]{2,1,0:T(8,128)S(1)}, f32[2,8,128]{2,1,0:T(8,128)S(1)}, u32[]{:S(2)}, u32[]{:S(2)}) collective-permute-start(f32[2,8,128]{2,1,0:T(8,128)S(1)} %get-tuple-element.31), channel_id=1, source_target_pairs={{0,128},{1,129},{2,130},{3,131},{4,132},{5,133},{6,134},{7,135},{8... | collective-permute-start | bytes 24584 | tf_op jit(solution)/shard_map/ppermute | solution.py:37
  23.1 8.9 %collective-permute-start.7 = (f32[37,8,128]{2,1,0:T(8,128)S(1)}, f32[37,8,128]{2,1,0:T(8,128)S(1)}, u32[]{:S(2)}, u32[]{:S(2)}) collective-permute-start(f32[37,8,128]{2,1,0:T(8,128)S(1)} %get-tuple-element.33.refs_1_), channel_id=1, source_target_pairs={{32,64},{33,65},{34,66},{35,67},{36,68},{37,69},{38,70},{39,71},{4... | collective-permute-start | bytes 454664 | tf_op jit(solution)/shard_map/ppermute | solution.py:37
  29.1 2.2 %collective-permute-start.6 = (f32[36,8,128]{2,1,0:T(8,128)S(1)}, f32[36,8,128]{2,1,0:T(8,128)S(1)}, u32[]{:S(2)}, u32[]{:S(2)}) collective-permute-start(f32[36,8,128]{2,1,0:T(8,128)S(1)} %get-tuple-element.32.refs_0_), channel_id=1, source_target_pairs={{0,32},{1,33},{2,34},{3,35},{4,36},{5,37},{6,38},{7,39},{8,40},{9,... | collective-permute-start | bytes 442376 | tf_op jit(solution)/shard_map/ppermute | solution.py:37

commit v5 on v4

--- a/solution.py
+++ b/solution.py
@@ -10,7 +10,7 @@
 OUT_ROWS = 8
 BLOCKS = 8
 TILE_PACK = 17
-STRIP = 36
+STRIP = 30
 SHIFT = 16
 WIDE = 40
 TALL = 16
@@ -94,10 +94,12 @@
 
 def halo_slabs(view):
     mid = (-5, 1) if view == 0 else (-1, 5)
-    slabs = [(p, d, g) for p in (0, 1) for d in (1, 2) for g in (-8, 0, 8)]
-    slabs += [(p, d, g) for p in (0, 1) for d in (3, 4) for g in (-1, 1)]
-    slabs += [(p, 1, g) for p in (2, 3) for g in (-8, 0, 8)]
-    slabs += [(p, d, g) for p in (2, 3) for d in (2, 3) for g in mid]
+    near = [(p, d) for p in (0, 1) for d in (1, 2)]
+    mean = [(p, d) for p in (0, 1) for d in (3, 4)]
+    slabs = [[(p, d, g, 8)] for p, d in near for g in (-5, 3)] + [[(p, d, 11, 2) for p, d in near]]
+    slabs += [[(p, d, -1, 8)] for p, d in mean] + [[(p, d, 7, 2) for p, d in mean]]
+    slabs += [[(p, 1, g, 8)] for p in (2, 3) for g in (-8, 0, 8)]
+    slabs += [[(p, d, g, 8)] for p in (2, 3) for d in (2, 3) for g in mid]
     return slabs
 
 
@@ -135,12 +137,16 @@
         m1_ref[at] = jnp.where(even_row, bottom, top)
         m2_ref[at] = jnp.where(even_row, top, bottom)
 
-    for at, ((plane, d, g), (_, _, g1)) in enumerate(zip(halo_slabs(0), halo_slabs(1), strict=True)):
+    def collect(pieces, row_of):
+        parts = [F[plane, row_of(d), SHIFT + g : SHIFT + g + n] for plane, d, g, n in pieces]
+        return parts[0] if len(parts) == 1 else jnp.concatenate(parts, axis=0)
+
+    for at, (one, two) in enumerate(zip(halo_slabs(0), halo_slabs(1), strict=True)):
         pair = []
-        for ry in (3 + d, 12 - d):
-            value = F[plane, ry, SHIFT + g : SHIFT + g + 8]
-            if g1 != g:
-                value = jnp.where(first, value, F[plane, ry, SHIFT + g1 : SHIFT + g1 + 8])
+        for row_of in (lambda d: 3 + d, lambda d: 12 - d):
+            value = collect(one, row_of)
+            if one != two:
+                value = jnp.where(first, value, collect(two, row_of))
             pair.append(value)
         put(at, *pair)
     for w in range(2):
@@ -377,10 +383,13 @@
     def run(v):
         own, own_narrow, other, other_narrow, slope_wide, slope_narrow = plans(v)
         signs = (1 - 2 * v, 2 * v - 1)
-        for at, (plane, d, g) in enumerate(halo_slabs(v)):
+        for at, pieces in enumerate(halo_slabs(v)):
             above, below = above_below(at)
-            F[plane, 4 - d, SHIFT + g : SHIFT + g + 8] = above
-            F[plane, 11 + d, SHIFT + g : SHIFT + g + 8] = below
+            start = 0
+            for plane, d, g, n in pieces:
+                F[plane, 4 - d, SHIFT + g : SHIFT + g + n] = above[start : start + n]
+                F[plane, 11 + d, SHIFT + g : SHIFT + g + n] = below[start : start + n]
+                start += n
         thin = SHIFT - 9 if v == 0 else SHIFT + 16
         for w in range(2):
             above, below = above_below(STRIP - 2 + w)

time: 35 us -> 34.8 us (level)
  no operation moved by 1% of the time
where the time goes in v5:
time: 34.8 us; the launch traced here: 34.5 us
  starting transfers between devices  19.8 us (57%)
  waiting for transfers between devices  6.54 us (19%)
  Pallas kernels  6.53 us (19%)
  local copies, waits for them, and re-layouts  0.92 us (3%)
  between operations  0.71 us (2%)
    ppermute x8, starting transfers between devices, swapped(): return lax.ppermute(block, AXES, route)  19.8 us
    ppermute x8, waiting for transfers between devices, swapped(): return lax.ppermute(block, AXES, route)  6.54 us
    pallas_call x1, Pallas kernels, on_device(): pl.pallas_call(lambda *refs: outer_kernel(sizes, *refs), out_shape=(jax.S...  2.83 us
    pallas_call x1, Pallas kernels, on_device(): pl.pallas_call(lambda *refs: inner_kernel(sizes, *refs), out_shape=tuple(...  2.09 us
    pallas_call x1, Pallas kernels, on_device(): pl.pallas_call(pack_kernel, out_shape=(tile, jax.ShapeDtypeStruct((TILE_P...  1.49 us
    unnamed x2, local copies, waits for them, and re-layouts  0.92 us
  transfers between devices with their start and end apart: 8, of which 4 were waited for; matrix products, arithmetic and copies ran while one was open for 0% of the time, Pallas kernels for 6%

profile of v5, /device:TPU:25, one launch (start us, length us, event | category | flops | bytes accessed | tf_op | source)
XLA Modules:
  0.0 34.5 jit_solution(15350997978305084230)
XLA Ops:
  0.6 1.5 %shard_map.50 = (f32[17,8,128]{2,1,0:T(8,128)}, f32[18,8,128]{2,1,0:T(8,128)}) custom-call(f32[1,8,1024]{2,1,0:T(8,128)} %image_hbm.1, s32[1,8,1024]{2,1,0:T(8,128)} %coarse_hbm.1, s32[1,1,1,2]{3,2,1,0:T(1,128)} %bounds_hbm.1), custom_call_target="tpu_custom_call" | custom-call | tf_op jit(solution)/shard_map/pallas_call | solution.py:498
  2.1 2.8 %collective-permute-start = (f32[18,8,128]{2,1,0:T(8,128)}, f32[18,8,128]{2,1,0:T(8,128)S(1)}, u32[]{:S(2)}, u32[]{:S(2)}) collective-permute-start(f32[18,8,128]{2,1,0:T(8,128)} %get-tuple-element.29), channel_id=1, source_target_pairs={{0,128},{1,129},{2,130},{3,131},{4,132},{5,133},{6,134},{7,135},{8... | collective-permute-start | bytes 221192 | tf_op jit(solution)/shard_map/ppermute | solution.py:37
  5.0 1.6 %collective-permute-start.1 = (f32[17,8,128]{2,1,0:T(8,128)}, f32[17,8,128]{2,1,0:T(8,128)S(1)}, u32[]{:S(2)}, u32[]{:S(2)}) collective-permute-start(f32[17,8,128]{2,1,0:T(8,128)} %get-tuple-element.28.own_ref), channel_id=1, source_target_pairs={{0,1},{1,0},{2,3},{3,2},{4,5},{5,4},{6,7},{7,6},{8,9},{9,8},{10,11... | collective-permute-start | bytes 208904 | tf_op jit(solution)/shard_map/ppermute | solution.py:37
  6.6 0.0 copy-start
  6.6 0.9 %copy-done = f32[17,8,128]{2,1,0:T(8,128)S(1)} copy-done((f32[17,8,128]{2,1,0:T(8,128)S(1)}, f32[17,8,128]{2,1,0:T(8,128)}, u32[]{:S(2)}) %copy-start) | copy-done | bytes 69656
  7.5 1.0 %collective-permute-done.1.a_ref.a_own_ref = f32[17,8,128]{2,1,0:T(8,128)S(1)} collective-permute-done((f32[17,8,128]{2,1,0:T(8,128)}, f32[17,8,128]{2,1,0:T(8,128)S(1)}, u32[]{:S(2)}, u32[]{:S(2)}) %collective-permute-start.1) | collective-permute-done | bytes 69664 | tf_op jit(solution)/shard_map/ppermute | solution.py:37
  8.6 0.0 collective-permute-done.other_ref
  8.6 7.7 %collective-permute-start.3 = (f32[36,8,128]{2,1,0:T(8,128)S(1)}, f32[36,8,128]{2,1,0:T(8,128)S(1)}, u32[]{:S(2)}, u32[]{:S(2)}) collective-permute-start(f32[36,8,128]{2,1,0:T(8,128)S(1)} %shard_map.52.both_ref), channel_id=1, source_target_pairs={{1,2},{2,1},{3,4},{4,3},{5,6},{6,5},{7,8},{8,7},{9,10},{10,9},{11,... | collective-permute-start | bytes 442376 | tf_op jit(solution)/shard_map/ppermute | solution.py:37
  16.3 0.1 collective-permute-start.2
  16.4 2.4 %collective-permute-done.3.b_ref = f32[36,8,128]{2,1,0:T(8,128)S(1)} collective-permute-done((f32[36,8,128]{2,1,0:T(8,128)S(1)}, f32[36,8,128]{2,1,0:T(8,128)S(1)}, u32[]{:S(2)}, u32[]{:S(2)}) %collective-permute-start.3) | collective-permute-done | bytes 147488 | tf_op jit(solution)/shard_map/ppermute | solution.py:37
  18.8 0.1 collective-permute-start.4
  18.9 1.4 %collective-permute-start.5 = (f32[2,8,128]{2,1,0:T(8,128)S(1)}, f32[2,8,128]{2,1,0:T(8,128)S(1)}, u32[]{:S(2)}, u32[]{:S(2)}) collective-permute-start(f32[2,8,128]{2,1,0:T(8,128)S(1)} %get-tuple-element.31), channel_id=1, source_target_pairs={{0,128},{1,129},{2,130},{3,131},{4,132},{5,133},{6,134},{7,135},{8... | collective-permute-start | bytes 24584 | tf_op jit(solution)/shard_map/ppermute | solution.py:37
  20.3 0.0 collective-permute-done.2.a_other_ref
  20.3 2.7 %collective-permute-done.5.cross_ref = f32[2,8,128]{2,1,0:T(8,128)S(1)} collective-permute-done((f32[2,8,128]{2,1,0:T(8,128)S(1)}, f32[2,8,128]{2,1,0:T(8,128)S(1)}, u32[]{:S(2)}, u32[]{:S(2)}) %collective-permute-start.5) | collective-permute-done | bytes 8224 | tf_op jit(solution)/shard_map/ppermute | solution.py:37
  23.0 0.0 collective-permute-done.4.far_ref
  23.0 0.1 shard_map.54
  23.1 6.0 %collective-permute-start.7 = (f32[31,8,128]{2,1,0:T(8,128)S(1)}, f32[31,8,128]{2,1,0:T(8,128)S(1)}, u32[]{:S(2)}, u32[]{:S(2)}) collective-permute-start(f32[31,8,128]{2,1,0:T(8,128)S(1)} %get-tuple-element.33.refs_1_), channel_id=1, source_target_pairs={{32,64},{33,65},{34,66},{35,67},{36,68},{37,69},{38,70},{39,71},{4... | collective-permute-start | bytes 380936 | tf_op jit(solution)/shard_map/ppermute | solution.py:37
  29.1 0.1 collective-permute-start.6
  29.2 2.1 %shard_map.55 = (f32[2,16,40,128]{3,2,1,0:T(8,128)S(1)}, s32[2,16,40,128]{3,2,1,0:T(8,128)S(1)}, f32[2,16,40,128]{3,2,1,0:T(8,128)S(1)}, f32[2,16,40,128]{3,2,1,...) custom-call(f32[4,16,40,128]{3,2,1,0:T(8,128)S(1)} %get-tuple-elemen, ...), custom_call_target="tpu_custom_call" | custom-call | flops 20000000 | bytes 4000000 | tf_op jit(solution)/shard_map/pallas_call | solution.py:566
  31.3 0.0 collective-permute-done.6.refs_2_
  31.3 0.4 %collective-permute-done.7.refs_3_ = f32[31,8,128]{2,1,0:T(8,128)S(1)} collective-permute-done((f32[31,8,128]{2,1,0:T(8,128)S(1)}, f32[31,8,128]{2,1,0:T(8,128)S(1)}, u32[]{:S(2)}, u32[]{:S(2)}) %collective-permute-start.7) | collective-permute-done | bytes 127008 | tf_op jit(solution)/shard_map/ppermute | solution.py:37
  31.7 2.8 %shard_map.56 = (f32[1,8,1024]{2,1,0:T(8,128)}, f32[1,2,8,1024]{3,2,1,0:T(8,128)}, f32[4,16,40,128]{3,2,1,0:T(8,128)S(1)}, f32[2,3,40,128]{3,2,1,0:T(8,128)S(1)}...) custom-call(f32[30,8,128]{2,1,0:T(8,128)S(1)} %get-tuple-element.32., ...), custom_call_target="tpu_custom_call", output_to_operand_aliasing={{2}: (4, {}), {3}: (5, {}), {4}: (6, {}), {5}: (7, {}), {6}... | custom-call | tf_op jit(solution)/shard_map/pallas_call | solution.py:576
  (3 shorter events, 0.0 us)
Async XLA Ops:
  2.1 6.4 %collective-permute-start = (f32[18,8,128]{2,1,0:T(8,128)}, f32[18,8,128]{2,1,0:T(8,128)S(1)}, u32[]{:S(2)}, u32[]{:S(2)}) collective-permute-start(f32[18,8,128]{2,1,0:T(8,128)} %get-tuple-element.29), channel_id=1, source_target_pairs={{0,128},{1,129},{2,130},{3,131},{4,132},{5,133},{6,134},{7,135},{8... | collective-permute-start | bytes 221192 | tf_op jit(solution)/shard_map/ppermute | solution.py:37
  5.0 3.6 %collective-permute-start.1 = (f32[17,8,128]{2,1,0:T(8,128)}, f32[17,8,128]{2,1,0:T(8,128)S(1)}, u32[]{:S(2)}, u32[]{:S(2)}) collective-permute-start(f32[17,8,128]{2,1,0:T(8,128)} %get-tuple-element.28.own_ref), channel_id=1, source_target_pairs={{0,1},{1,0},{2,3},{3,2},{4,5},{5,4},{6,7},{7,6},{8,9},{9,8},{10,11... | collective-permute-start | bytes 208904 | tf_op jit(solution)/shard_map/ppermute | solution.py:37
  6.6 0.9 %copy-start = (f32[17,8,128]{2,1,0:T(8,128)S(1)}, f32[17,8,128]{2,1,0:T(8,128)}, u32[]{:S(2)}) copy-start(f32[17,8,128]{2,1,0:T(8,128)} %get-tuple-element.28.own_ref) | copy-start | bytes 208900
  8.6 10.2 %collective-permute-start.3 = (f32[36,8,128]{2,1,0:T(8,128)S(1)}, f32[36,8,128]{2,1,0:T(8,128)S(1)}, u32[]{:S(2)}, u32[]{:S(2)}) collective-permute-start(f32[36,8,128]{2,1,0:T(8,128)S(1)} %shard_map.52.both_ref), channel_id=1, source_target_pairs={{1,2},{2,1},{3,4},{4,3},{5,6},{6,5},{7,8},{8,7},{9,10},{10,9},{11,... | collective-permute-start | bytes 442376 | tf_op jit(solution)/shard_map/ppermute | solution.py:37
  16.3 4.0 %collective-permute-start.2 = (f32[18,8,128]{2,1,0:T(8,128)S(1)}, f32[18,8,128]{2,1,0:T(8,128)S(1)}, u32[]{:S(2)}, u32[]{:S(2)}) collective-permute-start(f32[18,8,128]{2,1,0:T(8,128)S(1)} %collective-permute-done.other_ref), channel_id=1, source_target_pairs={{0,1},{1,0},{2,3},{3,2},{4,5},{5,4},{6,7},{7,6},{8,9},{9,8},{10,11... | collective-permute-start | bytes 221192 | tf_op jit(solution)/shard_map/ppermute | solution.py:37
  18.8 4.2 %collective-permute-start.4 = (f32[3,8,128]{2,1,0:T(8,128)S(1)}, f32[3,8,128]{2,1,0:T(8,128)S(1)}, u32[]{:S(2)}, u32[]{:S(2)}) collective-permute-start(f32[3,8,128]{2,1,0:T(8,128)S(1)} %get-tuple-element.30), channel_id=1, source_target_pairs={{0,1},{1,0},{2,3},{3,2},{4,5},{5,4},{6,7},{7,6},{8,9},{9,8},{10,11... | collective-permute-start | bytes 36872 | tf_op jit(solution)/shard_map/ppermute | solution.py:37
  18.9 4.1 %collective-permute-start.5 = (f32[2,8,128]{2,1,0:T(8,128)S(1)}, f32[2,8,128]{2,1,0:T(8,128)S(1)}, u32[]{:S(2)}, u32[]{:S(2)}) collective-permute-start(f32[2,8,128]{2,1,0:T(8,128)S(1)} %get-tuple-element.31), channel_id=1, source_target_pairs={{0,128},{1,129},{2,130},{3,131},{4,132},{5,133},{6,134},{7,135},{8... | collective-permute-start | bytes 24584 | tf_op jit(solution)/shard_map/ppermute | solution.py:37
  23.1 8.6 %collective-permute-start.7 = (f32[31,8,128]{2,1,0:T(8,128)S(1)}, f32[31,8,128]{2,1,0:T(8,128)S(1)}, u32[]{:S(2)}, u32[]{:S(2)}) collective-permute-start(f32[31,8,128]{2,1,0:T(8,128)S(1)} %get-tuple-element.33.refs_1_), channel_id=1, source_target_pairs={{32,64},{33,65},{34,66},{35,67},{36,68},{37,69},{38,70},{39,71},{4... | collective-permute-start | bytes 380936 | tf_op jit(solution)/shard_map/ppermute | solution.py:37
  29.1 2.2 %collective-permute-start.6 = (f32[30,8,128]{2,1,0:T(8,128)S(1)}, f32[30,8,128]{2,1,0:T(8,128)S(1)}, u32[]{:S(2)}, u32[]{:S(2)}) collective-permute-start(f32[30,8,128]{2,1,0:T(8,128)S(1)} %get-tuple-element.32.refs_0_), channel_id=1, source_target_pairs={{0,32},{1,33},{2,34},{3,35},{4,36},{5,37},{6,38},{7,39},{8,40},{9,... | collective-permute-start | bytes 368648 | tf_op jit(solution)/shard_map/ppermute | solution.py:37

commit v6 on v5

--- a/solution.py
+++ b/solution.py
@@ -245,7 +245,7 @@
             stores.append((p_out[0], here_at, qx * shrink))
             stores.append((p_out[1], here_at, qy * shrink))
 
-    def primal_step(k, w, sign, ry, starts, u_in, p_out, u_out, ubar_out, stores):
+    def primal_step(k, w, sign, ry, starts, u_in, p_out, u_out, ubar_out, stores, part):
         ok, _ = masks(ry)
         rg = sum(int(ry >= n) if isinstance(ry, int) else (ry >= n).astype(jnp.int32) for n in (4, 12))
         for g in starts:
@@ -253,7 +253,7 @@
             here = pl.ds(i, 8)
             here_at = (w, ry, here)
             d0 = F[2 * w + 1, ry, here]
-            if k == 0:
+            if k == 0 and part != "finish":
                 t = lane - sign * d0.astype(jnp.int32)
                 stores.append((D, here_at, t))
             else:
@@ -268,7 +268,7 @@
                     value = jnp.where(picks[m - 1], more, value)
                 return value
 
-            if k == 0:
+            if k == 0 and part != "finish":
                 residue = read(F, (2 * (1 - w), ry)) - F[2 * w, ry, here]
                 slope = read(G, (1 - w, ry)) * float(-sign)
                 inv = 1.0 / jnp.maximum(slope * slope, slope_floor)
@@ -279,6 +279,8 @@
             else:
                 residue, slope = RES[here_at], SL[here_at]
                 inv, rden = INV[here_at], RD[here_at]
+            if part == "prepare":
+                continue
             partner = read(u_in, (2 * (1 - w) + 1, ry) if k == 0 else (1 - w, ry))
             u = d0 if k == 0 else u_in[here_at]
             px, px_left = behind(p_out[0], (w, ry), i)
@@ -305,8 +307,8 @@
     def dual(k, w, y, starts, stores):
         dual_step(k, w, y + 4, starts, ubar_bufs[k], p_bufs[k], p_bufs[k + 1], stores)
 
-    def primal(k, w, y, sign, starts, stores):
-        primal_step(k, w, sign, y + 4, starts, u_bufs[k], p_bufs[k + 1], u_bufs[k + 1], ubar_bufs[k + 1], stores)
+    def primal(k, w, y, sign, starts, stores, part="whole"):
+        primal_step(k, w, sign, y + 4, starts, u_bufs[k], p_bufs[k + 1], u_bufs[k + 1], ubar_bufs[k + 1], stores, part)
 
     def slopes(w, y, starts, stores):
         slope_step(w, y + 4, starts, stores)
@@ -363,6 +365,12 @@
         slopes(0, 7, (-8, 0, 8), stores)
         slopes(1, 7, slope_other, stores)
         flush(stores)
+        stores = []
+        for y in (0, 7):
+            for w, plan in enumerate((own, other)):
+                primal(0, w, y, signs[w], plan[0][1], stores, "prepare")
+        dual(3, 0, 3, own[3][0], stores)
+        flush(stores)
 
     by_view(run)
 
@@ -370,7 +378,7 @@
 def outer_kernel(sizes, m1_ref, m2_ref, g1_ref, g2_ref, *refs):
     refine_ref, dual_ref = refs[18:20]
     state = refs[20:38]
-    MX, CV, XG, OUT = refs[38:]
+    MX, CV, XG, OUT, flat_refine, flat_dual, sems = refs[38:]
     F, LO, HI = state[:3]
     XB, YB = state[16:]
     dual, primal, slopes = make_steps(sizes, state, MX, CV, XG, OUT)
@@ -379,6 +387,9 @@
     def above_below(at):
         one, two = g1_ref[at], g2_ref[at]
         return jnp.where(even_row, two, one), jnp.where(even_row, one, two)
+
+    send_dual = pltpu.make_async_copy(flat_dual, dual_ref.at[0], sems.at[0])
+    send_refine = pltpu.make_async_copy(flat_refine, refine_ref.at[0], sems.at[1])
 
     def run(v):
         own, own_narrow, other, other_narrow, slope_wide, slope_narrow = plans(v)
@@ -444,10 +455,11 @@
                     primal(k, 1, y, signs[1], narrow_other[1], stores)
 
             def primal_block(stores):
+                ready = "finish" if k == 0 else "whole"
                 for y in (k - 1, k, 7 - k, 8 - k):
-                    primal(k, 0, y, signs[0], own[k][1], stores)
+                    primal(k, 0, y, signs[0], own[k][1], stores, ready if 0 <= y < 8 else "whole")
                 for y in (k, 7 - k):
-                    primal(k, 1, y, signs[1], other[k][1], stores)
+                    primal(k, 1, y, signs[1], other[k][1], stores, ready)
 
             pairs(dual_loop)
             block(dual_block)
@@ -455,38 +467,44 @@
             block(primal_block)
 
         def last_dual(i, stores):
-            for y in (3 * i - 1, 3 * i, 3 * i + 1):
+            for y in ((-1, 0, 1, 2), (4, 5, 6, 7))[i]:
                 dual(3, 0, y, own[3][0], stores)
 
         def last_primal(i, stores):
             for y in (4 * i, 4 * i + 1, 4 * i + 2, 4 * i + 3):
                 primal(3, 0, y, signs[0], own[3][1], stores)
 
-        for step, count in ((last_dual, 3), (last_primal, 2)):
-            for i in range(count):
-                stores = []
-                step(i, stores)
-                flush(stores)
+        def flatten(slabs, put):
+            parts = jnp.transpose(slabs, (1, 0, 2))
+            for j in range(BLOCKS):
+                put(slice(LANES * j, LANES * (j + 1)), parts[j])
+
+        def put_refine(at, value):
+            flat_refine[:, at] = value
+
+        def put_x(at, value):
+            flat_dual[0, :, at] = value
+
+        def put_y(at, value):
+            flat_dual[1, :, at] = value
+
+        for i in range(2):
+            stores = []
+            last_dual(i, stores)
+            flush(stores)
+        flatten(XB[0, 4:12, SHIFT : SHIFT + 8], put_x)
+        flatten(YB[0, 4:12, SHIFT : SHIFT + 8], put_y)
+        send_dual.start()
+        for i in range(2):
+            stores = []
+            last_primal(i, stores)
+            flush(stores)
+        flatten(OUT[...], put_refine)
+        send_refine.start()
+        send_dual.wait()
+        send_refine.wait()
 
     by_view(run)
-
-    def from_slabs(slabs, put):
-        parts = jnp.transpose(slabs, (1, 0, 2))
-        for j in range(BLOCKS):
-            put(slice(LANES * j, LANES * (j + 1)), parts[j])
-
-    def put_refine(at, value):
-        refine_ref[0, :, at] = value
-
-    def put_x(at, value):
-        dual_ref[0, 0, :, at] = value
-
-    def put_y(at, value):
-        dual_ref[0, 1, :, at] = value
-
-    from_slabs(OUT[...], put_refine)
-    from_slabs(XB[0, 4:12, SHIFT : SHIFT + 8], put_x)
-    from_slabs(YB[0, 4:12, SHIFT : SHIFT + 8], put_y)
 
 
 def on_device(sizes, image, coarse, bounds):
@@ -584,9 +602,15 @@
             *fields,
         ),
         in_specs=[vmem] * 22,
-        out_specs=(vmem,) * 20,
+        out_specs=(hbm, hbm) + (vmem,) * 18,
         input_output_aliases={4 + n: 2 + n for n in range(18)},
-        scratch_shapes=[*tables, pltpu.VMEM((OUT_ROWS, BLOCKS, LANES), f32)],
+        scratch_shapes=[
+            *tables,
+            pltpu.VMEM((OUT_ROWS, BLOCKS, LANES), f32),
+            pltpu.VMEM((OUT_ROWS, BLOCKS * LANES), f32),
+            pltpu.VMEM((2, OUT_ROWS, BLOCKS * LANES), f32),
+            pltpu.SemaphoreType.DMA((2,)),
+        ],
         compiler_params=params,
     )(m1, m2, g1, g2, *state)
     return refine, dual

time: 34.8 us -> 34.6 us (level)
  transfers between devices with their start and end apart: 8 -> 8, of which waited for: 4 -> 4; matrix products, arithmetic and copies ran while one was open for 0% -> 0% of each run, Pallas kernels for 6% -> 7%
where the time goes in v6:
time: 34.6 us; the launch traced here: 34.4 us
  starting transfers between devices  19.8 us (57%)
  Pallas kernels  6.67 us (19%)
  waiting for transfers between devices  6.29 us (18%)
  local copies, waits for them, and re-layouts  0.92 us (3%)
  between operations  0.71 us (2%)
    ppermute x8, starting transfers between devices, swapped(): return lax.ppermute(block, AXES, route)  19.8 us
    ppermute x8, waiting for transfers between devices, swapped(): return lax.ppermute(block, AXES, route)  6.29 us
    pallas_call x1, Pallas kernels, on_device(): pl.pallas_call(lambda *refs: outer_kernel(sizes, *refs), out_shape=(jax.S...  2.71 us
    pallas_call x1, Pallas kernels, on_device(): pl.pallas_call(lambda *refs: inner_kernel(sizes, *refs), out_shape=tuple(...  2.35 us
    pallas_call x1, Pallas kernels, on_device(): pl.pallas_call(pack_kernel, out_shape=(tile, jax.ShapeDtypeStruct((TILE_P...  1.49 us
    unnamed x2, local copies, waits for them, and re-layouts  0.92 us
  transfers between devices with their start and end apart: 8, of which 4 were waited for; matrix products, arithmetic and copies ran while one was open for 0% of the time, Pallas kernels for 7%

profile of v6, /device:TPU:25, one launch (start us, length us, event | category | flops | bytes accessed | tf_op | source)
XLA Modules:
  0.0 34.4 jit_solution(6587883835976357000)
XLA Ops:
  0.6 1.5 %shard_map.50 = (f32[17,8,128]{2,1,0:T(8,128)}, f32[18,8,128]{2,1,0:T(8,128)}) custom-call(f32[1,8,1024]{2,1,0:T(8,128)} %image_hbm.1, s32[1,8,1024]{2,1,0:T(8,128)} %coarse_hbm.1, s32[1,1,1,2]{3,2,1,0:T(1,128)} %bounds_hbm.1), custom_call_target="tpu_custom_call" | custom-call | tf_op jit(solution)/shard_map/pallas_call | solution.py:516
  2.1 2.8 %collective-permute-start = (f32[18,8,128]{2,1,0:T(8,128)}, f32[18,8,128]{2,1,0:T(8,128)S(1)}, u32[]{:S(2)}, u32[]{:S(2)}) collective-permute-start(f32[18,8,128]{2,1,0:T(8,128)} %get-tuple-element.29), channel_id=1, source_target_pairs={{0,128},{1,129},{2,130},{3,131},{4,132},{5,133},{6,134},{7,135},{8... | collective-permute-start | bytes 221192 | tf_op jit(solution)/shard_map/ppermute | solution.py:37
  5.0 1.6 %collective-permute-start.1 = (f32[17,8,128]{2,1,0:T(8,128)}, f32[17,8,128]{2,1,0:T(8,128)S(1)}, u32[]{:S(2)}, u32[]{:S(2)}) collective-permute-start(f32[17,8,128]{2,1,0:T(8,128)} %get-tuple-element.28.own_ref), channel_id=1, source_target_pairs={{0,1},{1,0},{2,3},{3,2},{4,5},{5,4},{6,7},{7,6},{8,9},{9,8},{10,11... | collective-permute-start | bytes 208904 | tf_op jit(solution)/shard_map/ppermute | solution.py:37
  6.6 0.0 copy-start
  6.6 0.9 %copy-done = f32[17,8,128]{2,1,0:T(8,128)S(1)} copy-done((f32[17,8,128]{2,1,0:T(8,128)S(1)}, f32[17,8,128]{2,1,0:T(8,128)}, u32[]{:S(2)}) %copy-start) | copy-done | bytes 69656
  7.5 1.0 %collective-permute-done.1.a_ref.a_own_ref = f32[17,8,128]{2,1,0:T(8,128)S(1)} collective-permute-done((f32[17,8,128]{2,1,0:T(8,128)}, f32[17,8,128]{2,1,0:T(8,128)S(1)}, u32[]{:S(2)}, u32[]{:S(2)}) %collective-permute-start.1) | collective-permute-done | bytes 69664 | tf_op jit(solution)/shard_map/ppermute | solution.py:37
  8.6 0.0 collective-permute-done.other_ref
  8.6 7.7 %collective-permute-start.3 = (f32[36,8,128]{2,1,0:T(8,128)S(1)}, f32[36,8,128]{2,1,0:T(8,128)S(1)}, u32[]{:S(2)}, u32[]{:S(2)}) collective-permute-start(f32[36,8,128]{2,1,0:T(8,128)S(1)} %shard_map.52.both_ref), channel_id=1, source_target_pairs={{1,2},{2,1},{3,4},{4,3},{5,6},{6,5},{7,8},{8,7},{9,10},{10,9},{11,... | collective-permute-start | bytes 442376 | tf_op jit(solution)/shard_map/ppermute | solution.py:37
  16.3 0.1 collective-permute-start.2
  16.4 2.4 %collective-permute-done.3.b_ref = f32[36,8,128]{2,1,0:T(8,128)S(1)} collective-permute-done((f32[36,8,128]{2,1,0:T(8,128)S(1)}, f32[36,8,128]{2,1,0:T(8,128)S(1)}, u32[]{:S(2)}, u32[]{:S(2)}) %collective-permute-start.3) | collective-permute-done | bytes 147488 | tf_op jit(solution)/shard_map/ppermute | solution.py:37
  18.8 0.1 collective-permute-start.4
  18.9 1.4 %collective-permute-start.5 = (f32[2,8,128]{2,1,0:T(8,128)S(1)}, f32[2,8,128]{2,1,0:T(8,128)S(1)}, u32[]{:S(2)}, u32[]{:S(2)}) collective-permute-start(f32[2,8,128]{2,1,0:T(8,128)S(1)} %get-tuple-element.31), channel_id=1, source_target_pairs={{0,128},{1,129},{2,130},{3,131},{4,132},{5,133},{6,134},{7,135},{8... | collective-permute-start | bytes 24584 | tf_op jit(solution)/shard_map/ppermute | solution.py:37
  20.3 0.0 collective-permute-done.2.a_other_ref
  20.3 2.7 %collective-permute-done.5.cross_ref = f32[2,8,128]{2,1,0:T(8,128)S(1)} collective-permute-done((f32[2,8,128]{2,1,0:T(8,128)S(1)}, f32[2,8,128]{2,1,0:T(8,128)S(1)}, u32[]{:S(2)}, u32[]{:S(2)}) %collective-permute-start.5) | collective-permute-done | bytes 8224 | tf_op jit(solution)/shard_map/ppermute | solution.py:37
  23.0 0.0 collective-permute-done.4.far_ref
  23.0 0.1 shard_map.54
  23.1 6.0 %collective-permute-start.7 = (f32[31,8,128]{2,1,0:T(8,128)S(1)}, f32[31,8,128]{2,1,0:T(8,128)S(1)}, u32[]{:S(2)}, u32[]{:S(2)}) collective-permute-start(f32[31,8,128]{2,1,0:T(8,128)S(1)} %get-tuple-element.33.refs_1_), channel_id=1, source_target_pairs={{32,64},{33,65},{34,66},{35,67},{36,68},{37,69},{38,70},{39,71},{4... | collective-permute-start | bytes 380936 | tf_op jit(solution)/shard_map/ppermute | solution.py:37
  29.1 0.1 collective-permute-start.6
  29.2 2.4 %shard_map.55 = (f32[2,16,40,128]{3,2,1,0:T(8,128)S(1)}, s32[2,16,40,128]{3,2,1,0:T(8,128)S(1)}, f32[2,16,40,128]{3,2,1,0:T(8,128)S(1)}, f32[2,16,40,128]{3,2,1,...) custom-call(f32[4,16,40,128]{3,2,1,0:T(8,128)S(1)} %get-tuple-elemen, ...), custom_call_target="tpu_custom_call" | custom-call | flops 20000000 | bytes 4000000 | tf_op jit(solution)/shard_map/pallas_call | solution.py:584
  31.5 0.0 collective-permute-done.6.refs_2_
  31.6 0.1 collective-permute-done.7.refs_3_
  31.7 2.7 %shard_map.56 = (f32[1,8,1024]{2,1,0:T(8,128)}, f32[1,2,8,1024]{3,2,1,0:T(8,128)}, f32[4,16,40,128]{3,2,1,0:T(8,128)S(1)}, f32[2,3,40,128]{3,2,1,0:T(8,128)S(1)}...) custom-call(f32[30,8,128]{2,1,0:T(8,128)S(1)} %get-tuple-element.32., ...), custom_call_target="tpu_custom_call", output_to_operand_aliasing={{2}: (4, {}), {3}: (5, {}), {4}: (6, {}), {5}: (7, {}), {6}... | custom-call | tf_op jit(solution)/shard_map/pallas_call | solution.py:594
  (3 shorter events, 0.0 us)
Async XLA Ops:
  2.1 6.4 %collective-permute-start = (f32[18,8,128]{2,1,0:T(8,128)}, f32[18,8,128]{2,1,0:T(8,128)S(1)}, u32[]{:S(2)}, u32[]{:S(2)}) collective-permute-start(f32[18,8,128]{2,1,0:T(8,128)} %get-tuple-element.29), channel_id=1, source_target_pairs={{0,128},{1,129},{2,130},{3,131},{4,132},{5,133},{6,134},{7,135},{8... | collective-permute-start | bytes 221192 | tf_op jit(solution)/shard_map/ppermute | solution.py:37
  5.0 3.6 %collective-permute-start.1 = (f32[17,8,128]{2,1,0:T(8,128)}, f32[17,8,128]{2,1,0:T(8,128)S(1)}, u32[]{:S(2)}, u32[]{:S(2)}) collective-permute-start(f32[17,8,128]{2,1,0:T(8,128)} %get-tuple-element.28.own_ref), channel_id=1, source_target_pairs={{0,1},{1,0},{2,3},{3,2},{4,5},{5,4},{6,7},{7,6},{8,9},{9,8},{10,11... | collective-permute-start | bytes 208904 | tf_op jit(solution)/shard_map/ppermute | solution.py:37
  6.6 0.9 %copy-start = (f32[17,8,128]{2,1,0:T(8,128)S(1)}, f32[17,8,128]{2,1,0:T(8,128)}, u32[]{:S(2)}) copy-start(f32[17,8,128]{2,1,0:T(8,128)} %get-tuple-element.28.own_ref) | copy-start | bytes 208900
  8.6 10.2 %collective-permute-start.3 = (f32[36,8,128]{2,1,0:T(8,128)S(1)}, f32[36,8,128]{2,1,0:T(8,128)S(1)}, u32[]{:S(2)}, u32[]{:S(2)}) collective-permute-start(f32[36,8,128]{2,1,0:T(8,128)S(1)} %shard_map.52.both_ref), channel_id=1, source_target_pairs={{1,2},{2,1},{3,4},{4,3},{5,6},{6,5},{7,8},{8,7},{9,10},{10,9},{11,... | collective-permute-start | bytes 442376 | tf_op jit(solution)/shard_map/ppermute | solution.py:37
  16.3 4.0 %collective-permute-start.2 = (f32[18,8,128]{2,1,0:T(8,128)S(1)}, f32[18,8,128]{2,1,0:T(8,128)S(1)}, u32[]{:S(2)}, u32[]{:S(2)}) collective-permute-start(f32[18,8,128]{2,1,0:T(8,128)S(1)} %collective-permute-done.other_ref), channel_id=1, source_target_pairs={{0,1},{1,0},{2,3},{3,2},{4,5},{5,4},{6,7},{7,6},{8,9},{9,8},{10,11... | collective-permute-start | bytes 221192 | tf_op jit(solution)/shard_map/ppermute | solution.py:37
  18.8 4.2 %collective-permute-start.4 = (f32[3,8,128]{2,1,0:T(8,128)S(1)}, f32[3,8,128]{2,1,0:T(8,128)S(1)}, u32[]{:S(2)}, u32[]{:S(2)}) collective-permute-start(f32[3,8,128]{2,1,0:T(8,128)S(1)} %get-tuple-element.30), channel_id=1, source_target_pairs={{0,1},{1,0},{2,3},{3,2},{4,5},{5,4},{6,7},{7,6},{8,9},{9,8},{10,11... | collective-permute-start | bytes 36872 | tf_op jit(solution)/shard_map/ppermute | solution.py:37
  18.9 4.1 %collective-permute-start.5 = (f32[2,8,128]{2,1,0:T(8,128)S(1)}, f32[2,8,128]{2,1,0:T(8,128)S(1)}, u32[]{:S(2)}, u32[]{:S(2)}) collective-permute-start(f32[2,8,128]{2,1,0:T(8,128)S(1)} %get-tuple-element.31), channel_id=1, source_target_pairs={{0,128},{1,129},{2,130},{3,131},{4,132},{5,133},{6,134},{7,135},{8... | collective-permute-start | bytes 24584 | tf_op jit(solution)/shard_map/ppermute | solution.py:37
  23.1 8.6 %collective-permute-start.7 = (f32[31,8,128]{2,1,0:T(8,128)S(1)}, f32[31,8,128]{2,1,0:T(8,128)S(1)}, u32[]{:S(2)}, u32[]{:S(2)}) collective-permute-start(f32[31,8,128]{2,1,0:T(8,128)S(1)} %get-tuple-element.33.refs_1_), channel_id=1, source_target_pairs={{32,64},{33,65},{34,66},{35,67},{36,68},{37,69},{38,70},{39,71},{4... | collective-permute-start | bytes 380936 | tf_op jit(solution)/shard_map/ppermute | solution.py:37
  29.1 2.5 %collective-permute-start.6 = (f32[30,8,128]{2,1,0:T(8,128)S(1)}, f32[30,8,128]{2,1,0:T(8,128)S(1)}, u32[]{:S(2)}, u32[]{:S(2)}) collective-permute-start(f32[30,8,128]{2,1,0:T(8,128)S(1)} %get-tuple-element.32.refs_0_), channel_id=1, source_target_pairs={{0,32},{1,33},{2,34},{3,35},{4,36},{5,37},{6,38},{7,39},{8,40},{9,... | collective-permute-start | bytes 368648 | tf_op jit(solution)/shard_map/ppermute | solution.py:37
